TPU v7x, 128 devices: a whole 4x4x4 slice. The times are simulated.
128 devices in a mesh: dp: 8 (over z, core), table: 16 (over x, y).
Axes of the slice: x: 4, y: 4, z: 4, core: 2. Of those that a mesh axis runs over, the one named last changes fastest.
Arguments:
- history_lengths: int32 [8, 32], P(None, 'table'), may hold values from 1 to 256, as said below
- balance_list: int32 [8, 32], P(None, 'table'), may hold values from 0 to 15, as said below
- owner_device: int32 [256, 256, 1], P(('dp', 'table')), may hold values from 0 to 127; in each aligned block of 512 rows (0 to 511, 512 to 1023, ..., all dimensions but the last counted through in order) at most 8 rows name the same one
- owner_row: int32 [256, 256], P(('dp', 'table')), may hold values from 0 to 4095
- width_class: int32 [524288], replicated, may hold values from 0 to 2
- slab_index: int32 [524288], P(('dp', 'table')), may hold values from 0 to 2047
- narrow_table: bfloat16 [131072, 128], P(('dp', 'table')), may hold values from -6 to 6
- middle_table: bfloat16 [262144, 128], P(('dp', 'table')), may hold values from -6 to 6
- wide_table: bfloat16 [262144, 256], P(('dp', 'table')), may hold values from -6 to 6
- narrow_lift: bfloat16 [64, 512], replicated, may hold values from -0.75 to 0.75
- middle_lift: bfloat16 [128, 512], replicated, may hold values from -0.5 to 0.5
- wide_lift: bfloat16 [256, 512], replicated, may hold values from -0.375 to 0.375
- joined_weight: bfloat16 [512, 2048], replicated, may hold values from -0.25 to 0.25
- output_weight: bfloat16 [512, 512], replicated, may hold values from -0.25 to 0.25
- cotangent: bfloat16 [256, 256, 512], P(('dp', 'table')), may hold values from -6 to 6
Outputs:
- layer_output: bfloat16 [256, 256, 512], P(('dp', 'table'))
- narrow_grad: float32 [131072, 128], P(('dp', 'table'))
- middle_grad: float32 [262144, 128], P(('dp', 'table'))
- wide_grad: float32 [262144, 256], P(('dp', 'table'))
- narrow_delta: float32 [64, 512], replicated
- middle_delta: float32 [128, 512], replicated
- wide_delta: float32 [256, 512], replicated
Inputs may be any that keep to these rules, and one draw needn't show every extreme that they name: `history_lengths`: at least one history has length 256. `balance_list`: an entry j names the history in slot j mod 2 of the device with dp index j // 2 and the same table index. Each slot holds its own device's history of the same slot, except exactly 1 slot of each device, which holds a history of the device whose dp index is the own one XOR half the dp axis size; it is the slot whose own history goes to that device. For each table index the entries form a permutation. `owner_device`: among the 512 tokens of one device (aligned blocks in the order of histories and positions) at most 8 name the same owner, a bound that some block reaches.
All inputs are finite; a program needn't handle non-finite values.
Results may differ from a plain program's by a relative error of at most 0.017.
Values may be sent and summed in bfloat16 or wider, within the bound.
No kernel may reach another device: no remote copies, remote signals or barrier semaphores. Data moves between devices by JAX's collectives and lax.ppermute only.
A program may use at most 128 MiB of HBM per device.

v0:
```python
import jax
import jax.numpy as jnp
from jax import lax
from jax.sharding import PartitionSpec as P

HEADS = 4
HEAD = 128
MAXLEN = 256
MOVES = 1


def from_partner(value, axis, bit):
    return lax.ppermute(value, axis, [(i, i ^ 1 << bit) for i in range(lax.axis_size(axis))])


def normalize(values):
    centre = values - jnp.mean(values, axis=-1, keepdims=True)
    spread = jnp.mean(centre * centre, axis=-1, keepdims=True)
    return centre * lax.rsqrt(spread + 1e-06)


def fetch_rows(narrow_table, middle_table, wide_table, slab_rows, classes):
    amount = slab_rows.shape[0]
    packed = narrow_table[slab_rows // 2]
    halves = jnp.where((slab_rows % 2 == 0)[:, None], packed[:, :64], packed[:, 64:])
    padded_narrow = jnp.concatenate([halves, jnp.zeros((amount, 192), halves.dtype)], axis=1)
    padded_middle = jnp.concatenate(
        [middle_table[slab_rows], jnp.zeros((amount, 128), halves.dtype)], axis=1
    )
    return jnp.where(
        (classes == 2)[:, None],
        wide_table[slab_rows],
        jnp.where((classes == 1)[:, None], padded_middle, padded_narrow),
    )


def expand_rows(padded, classes):
    amount = padded.shape[0]
    return jnp.concatenate(
        [
            jnp.where((classes == 0)[:, None], padded[:, :64], 0),
            jnp.where((classes == 1)[:, None], padded[:, :128], 0),
            jnp.where((classes == 2)[:, None], padded, 0),
            jnp.zeros((amount, 64), padded.dtype),
        ],
        axis=1,
    )


def band_rows(spread_grad, classes):
    amount = spread_grad.shape[0]
    narrow_part = jnp.concatenate(
        [spread_grad[:, :64], jnp.zeros((amount, 192), jnp.float32)], axis=1
    )
    middle_part = jnp.concatenate(
        [spread_grad[:, 64:192], jnp.zeros((amount, 128), jnp.float32)], axis=1
    )
    chosen = jnp.where(
        (classes == 2)[:, None],
        spread_grad[:, 192:448],
        jnp.where((classes == 1)[:, None], middle_part, narrow_part),
    )
    return chosen.astype(jnp.bfloat16)


def add_rows(narrow_sum, middle_sum, wide_sum, row_grads, slab_rows, classes):
    widened = lax.optimization_barrier(row_grads).astype(jnp.float32)
    amount = widened.shape[0]
    wide_sum = wide_sum.at[slab_rows].add(jnp.where((classes == 2)[:, None], widened, 0.0))
    middle_sum = middle_sum.at[slab_rows].add(
        jnp.where((classes == 1)[:, None], widened[:, :128], 0.0)
    )
    narrow_part = jnp.where((classes == 0)[:, None], widened[:, :64], 0.0)
    blank = jnp.zeros((amount, 64), jnp.float32)
    placed = jnp.where(
        (slab_rows % 2 == 0)[:, None],
        jnp.concatenate([narrow_part, blank], axis=1),
        jnp.concatenate([blank, narrow_part], axis=1),
    )
    narrow_sum = narrow_sum.at[slab_rows // 2].add(placed)
    return (narrow_sum, middle_sum, wide_sum)


def layer(inputs, length, joined_weight, output_weight):
    rows_total = inputs.shape[0]
    width = inputs.shape[1]
    widened = inputs.astype(jnp.float32)
    normed = normalize(widened).astype(jnp.bfloat16)
    joined = jax.nn.silu(jnp.dot(normed, joined_weight, preferred_element_type=jnp.float32)).astype(
        jnp.bfloat16
    )
    gating = joined[:, :width]
    values_heads = joined[:, width : 2 * width].reshape(rows_total, HEADS, HEAD)
    queries = joined[:, 2 * width : 3 * width].reshape(rows_total, HEADS, HEAD)
    keys_heads = joined[:, 3 * width :].reshape(rows_total, HEADS, HEAD)
    scores = jnp.einsum("qhe,khe->hqk", queries, keys_heads, preferred_element_type=jnp.float32)
    places = jnp.arange(rows_total, dtype=jnp.int32)
    allowed = (places[None, :] <= places[:, None]) & (places[None, :] < length)
    weights = jnp.where(allowed[None], jax.nn.silu(scores) / MAXLEN, 0.0).astype(jnp.bfloat16)
    mixed = jnp.einsum(
        "hqk,khe->qhe", weights, values_heads, preferred_element_type=jnp.float32
    ).reshape(rows_total, width)
    gated = (normalize(mixed) * gating.astype(jnp.float32)).astype(jnp.bfloat16)
    result = jnp.dot(gated, output_weight, preferred_element_type=jnp.float32) + widened
    return jnp.where((places < length)[:, None], result, 0.0).astype(jnp.bfloat16)


def route_ids(requests):
    return lax.all_to_all(requests, ("dp", "table"), split_axis=0, concat_axis=0, tiled=True)


def route_rows(payload):
    return lax.all_to_all(payload, ("dp", "table"), split_axis=0, concat_axis=0, tiled=True)


def trade(block, bit_number):
    return from_partner(block, "dp", bit_number)


def body(
    history_lengths,
    balance_list,
    owner_device,
    owner_row,
    width_class,
    slab_index,
    narrow_table,
    middle_table,
    wide_table,
    narrow_lift,
    middle_lift,
    wide_lift,
    joined_weight,
    output_weight,
    cotangent,
):
    data_size = lax.axis_size("dp")
    table_size = lax.axis_size("table")
    devices = data_size * table_size
    hist_here = cotangent.shape[0]
    seq_rows = cotangent.shape[1]
    width = cotangent.shape[2]
    tokens_here = hist_here * seq_rows
    items_here = slab_index.shape[0]
    slab_here = middle_table.shape[0]
    capacity = max(2, 2 * tokens_here // devices)
    data_rank = lax.axis_index("dp")
    table_rank = lax.axis_index("table")
    self_rank = data_rank * table_size + table_rank
    owners = owner_device.reshape(tokens_here)
    local_rows = owner_row.reshape(tokens_here)
    matches = (owners[:, None] == jnp.arange(devices, dtype=jnp.int32)[None, :]).astype(jnp.int32)
    ranks = jnp.sum(jnp.cumsum(matches, axis=0) * matches, axis=1) - 1
    slots = owners * capacity + ranks
    requests = jnp.zeros((devices * capacity,), jnp.int32).at[slots].set(local_rows)
    asked = route_ids(requests)
    asked_class = width_class[self_rank * items_here + asked]
    asked_slab = slab_index[asked]
    lift_all = jnp.concatenate(
        [narrow_lift, middle_lift, wide_lift, jnp.zeros((64, width), narrow_lift.dtype)], axis=0
    )
    owned = expand_rows(
        fetch_rows(narrow_table, middle_table, wide_table, asked_slab, asked_class), asked_class
    )
    replies = jnp.dot(owned, lift_all, preferred_element_type=jnp.float32).astype(jnp.bfloat16)
    embedded = route_rows(replies)[slots]
    embedded = embedded.reshape(hist_here, seq_rows, width)
    own_list = balance_list[data_rank]
    partner = data_rank ^ data_size // 2
    partner_list = balance_list[partner]
    foreign_slots = jnp.nonzero(own_list // hist_here != data_rank, size=MOVES)[0]
    wanted_places = jnp.nonzero(partner_list // hist_here == data_rank, size=MOVES)[0]
    given_slots = partner_list[wanted_places] % hist_here
    bit_number = data_size.bit_length() - 2
    arrived = trade(embedded[given_slots], bit_number)
    here = embedded.at[foreign_slots].set(arrived)
    here_lengths = history_lengths[own_list // hist_here, own_list % hist_here]

    def layer_all(inputs):
        return jax.vmap(layer, in_axes=(0, 0, None, None))(
            inputs, here_lengths, joined_weight, output_weight
        )

    output, pullback = jax.vjp(layer_all, here)
    (here_grad,) = pullback(cotangent)
    returned = trade(here_grad[foreign_slots], bit_number)
    embed_grad = here_grad.at[given_slots].set(returned).reshape(tokens_here, width)
    outgoing = jnp.zeros((devices * capacity, width), jnp.bfloat16).at[slots].set(embed_grad)
    landed = route_rows(outgoing)
    spread_grad = lax.dot_general(
        landed, lift_all, (((1,), (1,)), ((), ())), preferred_element_type=jnp.float32
    )
    row_grads = band_rows(spread_grad, asked_class)
    lift_term = jnp.dot(owned.T, landed, preferred_element_type=jnp.float32)
    narrow_sum, middle_sum, wide_sum = add_rows(
        jnp.zeros((slab_here // 2, 128), jnp.float32),
        jnp.zeros((slab_here, 128), jnp.float32),
        jnp.zeros((slab_here, 256), jnp.float32),
        row_grads,
        asked_slab,
        asked_class,
    )
    lift_sum = lax.psum(lift_term[:448], ("dp", "table"))
    return (
        output,
        narrow_sum,
        middle_sum,
        wide_sum,
        lift_sum[:64],
        lift_sum[64:192],
        lift_sum[192:448],
    )


def solution(mesh):
    in_specs = (
        P(None, "table"),
        P(None, "table"),
        P(("dp", "table"), None, None),
        P(("dp", "table"), None),
        P(),
        P(("dp", "table")),
        P(("dp", "table"), None),
        P(("dp", "table"), None),
        P(("dp", "table"), None),
        P(),
        P(),
        P(),
        P(),
        P(),
        P(("dp", "table"), None, None),
    )
    out_specs = (
        P(("dp", "table"), None, None),
        P(("dp", "table"), None),
        P(("dp", "table"), None),
        P(("dp", "table"), None),
        P(),
        P(),
        P(),
    )
    return jax.shard_map(body, mesh=mesh, in_specs=in_specs, out_specs=out_specs, check_vma=False)
```

profile of v0, /device:TPU:1, one launch (start us, length us, event | category | flops | bytes accessed | tf_op | source)
XLA Modules:
  0.0 378.3 jit_solution(2763473944639639089)
XLA Ops:
  13.9 11.5 %all-to-all-start = ((s32[128,8,1]{1,2,0:T(1,128)}), s32[128,8,1]{1,2,0:T(1,128)S(1)}, u32[]{:S(2)}, u32[]{:S(2)}) async-start(s32[128,8,1]{1,2,0:T(1,128)} %bitcast.9), calls=%async_computation | async-start | bytes 131072 | tf_op jit(solution)/shard_map/all_to_all | solution.py:109
  26.7 8.2 %all-to-all-done = s32[128,8,1]{1,2,0:T(1,128)S(1)} async-done(((s32[128,8,1]{1,2,0:T(1,128)}), s32[128,8,1]{1,2,0:T(1,128)S(1)}, u32[]{:S(2)}, u32[]{:S(2)}) %all-to-all-start) | async-done | bytes 4128 | tf_op jit(solution)/shard_map/all_to_all | solution.py:109
  36.4 34.2 %gather_fusion.1 = s32[1024]{0:T(1024)S(1)} fusion(s32[524288]{0:T(1024)} %param.23, s32[1024]{0:T(1024)S(1)} %broadcast_clamp_fusion.3), kind=kCustom, calls=%fused_computation.1 | custom fusion | bytes 12288 | tf_op jit(solution)/shard_map/gather | solution.py:157
  70.7 6.2 %gather_fusion.2 = s32[1024]{0:T(1024)S(1)} fusion(s32[4096]{0:T(1024)S(1)} %copy-done.1, s32[1024]{0:T(1024)S(1)} %broadcast_clamp_fusion.2), kind=kCustom, calls=%fused_computation.2 | custom fusion | bytes 12288 | tf_op jit(solution)/shard_map/gather | solution.py:158
  77.5 5.2 %gather_fusion.4 = bf16[1024,128]{1,0:T(8,128)(2,1)} fusion(bf16[2048,128]{1,0:T(8,128)(2,1)} %param.26, s32[1024]{0:T(1024)S(1)} %broadcast_clamp_fusion.1), kind=kCustom, calls=%fused_computation.4 | custom fusion | bytes 528384 | tf_op jit(solution)/shard_map/gather | solution.py:28
  82.7 5.0 %gather_fusion.3 = bf16[1024,256]{1,0:T(8,128)(2,1)} fusion(bf16[2048,256]{1,0:T(8,128)(2,1)S(1)} %copy-done.5, s32[1024]{0:T(1024)S(1)} %broadcast_clamp_fusion.1), kind=kCustom, calls=%fused_computation.3 | custom fusion | bytes 1052672 | tf_op jit(solution)/shard_map/gather | solution.py:32
  87.7 3.2 gather_fusion.5
  95.9 7.5 %all-to-all-start.1 = ((bf16[128,8,512]{2,1,0:T(8,128)(2,1)}), bf16[128,8,512]{2,1,0:T(8,128)(2,1)S(1)}, u32[]{:S(2)}, u32[]{:S(2)}) async-start(bf16[128,8,512]{2,1,0:T(8,128)(2,1)} %fusion.23), calls=%async_computation.1 | async-start | bytes 2097152 | tf_op jit(solution)/shard_map/all_to_all | solution.py:113
  116.0 6.0 %all-to-all-done.1 = bf16[128,8,512]{2,1,0:T(8,128)(2,1)S(1)} async-done(((bf16[128,8,512]{2,1,0:T(8,128)(2,1)}), bf16[128,8,512]{2,1,0:T(8,128)(2,1)S(1)}, u32[]{:S(2)}, u32[]{:S(2)}) %all-to-all-start.1) | async-done | bytes 1048608 | tf_op jit(solution)/shard_map/all_to_all | solution.py:113
  122.0 2.6 gather_fusion.6
  128.2 5.4 %collective-permute-done = bf16[1,256,512]{2,1,0:T(8,128)(2,1)S(1)} collective-permute-done((bf16[1,256,512]{2,1,0:T(8,128)(2,1)S(1)}, bf16[1,256,512]{2,1,0:T(8,128)(2,1)S(1)}, u32[]{:S(2)}, u32[]{:S(2)}) %collective-permute-start) | collective-permute-done | bytes 262176 | tf_op jit(solution)/shard_map/ppermute | solution.py:13
  138.6 4.6 %multiply_convert_fusion = (bf16[2,256,2048]{2,1,0:T(8,128)(2,1)S(1)}, f32[2,256,2048]{2,1,0:T(8,128)}) fusion(bf16[512,2048]{1,0:T(8,128)(2,1)S(1)} %copy-done, bf16[2,256,512]{2,1,0:T(8,128)(2,1)} %select_dynamic-update-slice_fusion.1, f32[2,256]{1,0:T(2,128)S(1)} %fusion.89, f32[2,256]{1,0:T(2,128)S(1)} %broadcast_multiply_fusion.1), kind=kOutput, calls=%fused_computation.20 | convolution fusion | flops 1080033280 | bytes 8916992 | tf_op jit(solution)/shard_map/jvp(vmap())/dot_general | solution.py:89
  160.5 2.8 fusion.6
  170.9 5.0 %fusion.34 = (f32[2,256]{1,0:T(2,128)S(1)}, bf16[2,256,512]{2,1,0:T(8,128)(2,1)S(1)}) fusion(bf16[2,256,512]{2,1,0:T(8,128)(2,1)S(1)} %copy-done.3, f32[2,256]{1,0:T(2,128)S(1)} %broadcast_multiply_fusion.1, bf16[512,2048]{1,0:T(8,128)(2,1)S(1)} %copy-done, f32[2,256,2048]{2,1,0:T(8,128)} %get-tuple-element.85, bf16[2,256,512]{2,1,0:T(8,128)(2,1)S(1)} %copy-done.24, ...), kind=kOutput, calls=%fused_computation.65 | convolution fusion | flops 1093139968 | bytes 9441280 | tf_op jit(solution)/shard_map/transpose(jvp(vmap()))/dot_general | solution.py:89
  180.3 5.5 %collective-permute-done.1 = bf16[1,256,512]{2,1,0:T(8,128)(2,1)S(1)} collective-permute-done((bf16[1,256,512]{2,1,0:T(8,128)(2,1)S(1)}, bf16[1,256,512]{2,1,0:T(8,128)(2,1)S(1)}, u32[]{:S(2)}, u32[]{:S(2)}) %collective-permute-start.1) | collective-permute-done | bytes 262176 | tf_op jit(solution)/shard_map/ppermute | solution.py:13
  188.3 4.0 %scatter_custom_fusion.3 = bf16[1024,512]{1,0:T(8,128)(2,1)} fusion(s32[512]{0:T(512)} %bitcast.168, bf16[512,512]{1,0:T(8,128)(2,1)} %bitcast.39, bf16[]{:T(256)} %constant.238.clone.1), kind=kCustom, calls=%fused_computation.104 | custom fusion | bytes 1049088 | tf_op jit(solution)/shard_map/scatter | solution.py:188
  192.2 9.5 %all-to-all-start.2 = ((bf16[128,8,512]{2,1,0:T(8,128)(2,1)}), bf16[128,8,512]{2,1,0:T(8,128)(2,1)}, u32[]{:S(2)}, u32[]{:S(2)}) async-start(bf16[128,8,512]{2,1,0:T(8,128)(2,1)} %bitcast.143), calls=%async_computation.2 | async-start | bytes 2097152 | tf_op jit(solution)/shard_map/all_to_all | solution.py:113
  201.8 2.8 pad_maximum_fusion
  206.9 13.0 %all-to-all-done.2 = bf16[128,8,512]{2,1,0:T(8,128)(2,1)} async-done(((bf16[128,8,512]{2,1,0:T(8,128)(2,1)}), bf16[128,8,512]{2,1,0:T(8,128)(2,1)}, u32[]{:S(2)}, u32[]{:S(2)}) %all-to-all-start.2) | async-done | bytes 1048608 | tf_op jit(solution)/shard_map/all_to_all | solution.py:113
  219.9 3.2 fusion.35
  227.3 8.2 %scatter_custom_fusion.6 = f32[2048,256]{1,0:T(8,128)} fusion(s32[1024]{0:T(1024)} %bitcast.162, f32[]{:T(128)} %constant.245.clone.1, pred[1024]{0:T(1024)(128)(4,1)S(1)} %copy-done.32, bf16[1024,256]{1,0:T(8,128)(2,1)S(1)} %fusion.39), kind=kCustom, calls=%fused_computation.80 | custom fusion | flops 786432 | bytes 2623488 | tf_op jit(solution)/shard_map/scatter-add | solution.py:69
  235.5 8.0 %scatter_custom_fusion.5 = f32[2048,128]{1,0:T(8,128)} fusion(s32[1024]{0:T(1024)} %bitcast.163, f32[1024,256]{1,0:T(8,128)} %convert_element_type.146, f32[]{:T(128)} %constant.245.clone.1, pred[1024]{0:T(1024)(128)(4,1)S(1)} %get-tuple-element.77), kind=kCustom, calls=%fused_computation.91 | custom fusion | flops 262144 | bytes 1574912 | tf_op jit(solution)/shard_map/scatter-add | solution.py:70
  244.8 7.6 %scatter_custom_fusion.4 = f32[1024,128]{1,0:T(8,128)} fusion(s32[1024]{0:T(1024)} %bitcast.160, f32[1024,64]{1,0:T(8,128)S(1)} %slice_select_fusion.3, f32[]{:T(128)} %constant.245.clone.1, pred[1024]{0:T(1024)(128)(4,1)S(1)} %copy-done.38), kind=kCustom, calls=%fused_computation.98 | custom fusion | flops 262144 | bytes 788480 | tf_op jit(solution)/shard_map/scatter-add | solution.py:80
  252.4 114.0 %all-reduce.11.cloned.1.call-done = f32[448,512]{1,0:T(8,128)} async-done(((f32[448,512]{1,0:T(8,128)}), f32[448,512]{1,0:T(8,128)}) %all-reduce.11.cloned.1.call-update) | async-done | bytes 917520 | tf_op jit(solution)/shard_map/psum | solution.py:203
  (207 shorter events, 73.1 us)
Async XLA Ops:
  7.2 131.4 %copy-start = (bf16[512,2048]{1,0:T(8,128)(2,1)S(1)}, bf16[512,2048]{1,0:T(8,128)(2,1)}, u32[]{:S(2)}) copy-start(bf16[512,2048]{1,0:T(8,128)(2,1)} %param.31) | copy-start | bytes 6291460
  10.7 105.2 %copy-start.40 = (s32[512,1]{0,1:T(1,128)}, s32[512,1]{0,1:T(1,128)S(1)}, u32[]{:S(2)}) copy-start(s32[512,1]{0,1:T(1,128)S(1)} %compare_select_fusion.3) | copy-start | bytes 6148
  13.9 21.0 %all-to-all-start = ((s32[128,8,1]{1,2,0:T(1,128)}), s32[128,8,1]{1,2,0:T(1,128)S(1)}, u32[]{:S(2)}, u32[]{:S(2)}) async-start(s32[128,8,1]{1,2,0:T(1,128)} %bitcast.9), calls=%async_computation | async-start | bytes 131072 | tf_op jit(solution)/shard_map/all_to_all | solution.py:109
  26.7 65.9 %copy-start.44 = (bf16[512]{0:T(512)(128)(2,1)}, bf16[512]{0:T(512)(128)(2,1)S(1)}, u32[]{:S(2)}) copy-start(bf16[512]{0:T(512)(128)(2,1)S(1)} %pad.41.clone) | copy-start | bytes 3076
  36.4 34.2 %copy-start.1 = (s32[4096]{0:T(1024)S(1)}, s32[4096]{0:T(1024)}, u32[]{:S(2)}) copy-start(s32[4096]{0:T(1024)} %param.24) | copy-start | bytes 49156
  70.6 20.6 %copy-start.31 = (pred[1024]{0:T(1024)(128)(4,1)}, pred[1024]{0:T(1024)(128)(4,1)S(1)}, u32[]{:S(2)}) copy-start(pred[1024]{0:T(1024)(128)(4,1)S(1)} %get-tuple-element.76) | copy-start | bytes 3076
  70.6 21.7 %copy-start.35 = (pred[1024]{0:T(1024)(128)(4,1)}, pred[1024]{0:T(1024)(128)(4,1)S(1)}, u32[]{:S(2)}) copy-start(pred[1024]{0:T(1024)(128)(4,1)S(1)} %get-tuple-element.75) | copy-start | bytes 3076
  76.8 14.1 %copy-start.37 = (pred[1024]{0:T(1024)(128)(4,1)}, pred[1024]{0:T(1024)(128)(4,1)S(1)}, u32[]{:S(2)}) copy-start(pred[1024]{0:T(1024)(128)(4,1)S(1)} %fusion.86) | copy-start | bytes 3076
  76.9 10.8 %copy-start.33 = (s32[1024,1]{0,1:T(1,128)}, s32[1024,1]{0,1:T(1,128)S(1)}, u32[]{:S(2)}) copy-start(s32[1024,1]{0,1:T(1,128)S(1)} %get-tuple-element.78) | copy-start | bytes 12292
  95.9 12.4 %copy-start.41 = (s32[8,2]{0,1:T(2,128)S(1)}, s32[8,2]{0,1:T(2,128)}, u32[]{:S(2)}) copy-start(s32[8,2]{0,1:T(2,128)} %param.20) | copy-start | bytes 196
  95.9 19.4 %copy-start.2 = (s32[8,2]{0,1:T(2,128)S(1)}, s32[8,2]{0,1:T(2,128)}, u32[]{:S(2)}) copy-start(s32[8,2]{0,1:T(2,128)} %param.19) | copy-start | bytes 196
  95.9 26.1 %all-to-all-start.1 = ((bf16[128,8,512]{2,1,0:T(8,128)(2,1)}), bf16[128,8,512]{2,1,0:T(8,128)(2,1)S(1)}, u32[]{:S(2)}, u32[]{:S(2)}) async-start(bf16[128,8,512]{2,1,0:T(8,128)(2,1)} %fusion.23), calls=%async_computation.1 | async-start | bytes 2097152 | tf_op jit(solution)/shard_map/all_to_all | solution.py:113
  116.0 36.5 %copy-start.42 = (pred[2,256]{1,0:T(4,128)(4,1)}, pred[2,256]{1,0:T(4,128)(4,1)S(1)}, u32[]{:S(2)}) copy-start(pred[2,256]{1,0:T(4,128)(4,1)S(1)} %iota_compare_fusion.4) | copy-start | bytes 1540
  125.6 8.1 %collective-permute-start = (bf16[1,256,512]{2,1,0:T(8,128)(2,1)S(1)}, bf16[1,256,512]{2,1,0:T(8,128)(2,1)S(1)}, u32[]{:S(2)}, u32[]{:S(2)}) collective-permute-start(bf16[1,256,512]{2,1,0:T(8,128)(2,1)S(1)} %constant_dynamic-slice_fusion.1), channel_id=1, source_target_pairs={{0,64},{16,80},{32,96},{48,112},{64,0},{80,16},{96,32},{112,48},{1... | collective-permute-start | bytes 786440 | tf_op jit(solution)/shard_map/ppermute | solution.py:13
  178.8 22.9 %copy-start.13 = (bf16[1024,256]{1,0:T(8,128)(2,1)S(1)}, bf16[1024,256]{1,0:T(8,128)(2,1)}, u32[]{:S(2)}) copy-start(bf16[1024,256]{1,0:T(8,128)(2,1)} %copy-done.12) | copy-start | bytes 1572868
  178.8 7.0 %collective-permute-start.1 = (bf16[1,256,512]{2,1,0:T(8,128)(2,1)S(1)}, bf16[1,256,512]{2,1,0:T(8,128)(2,1)S(1)}, u32[]{:S(2)}, u32[]{:S(2)}) collective-permute-start(bf16[1,256,512]{2,1,0:T(8,128)(2,1)S(1)} %constant_dynamic-slice_fusion), channel_id=1, source_target_pairs={{0,64},{16,80},{32,96},{48,112},{64,0},{80,16},{96,32},{112,48},{1... | collective-permute-start | bytes 786440 | tf_op jit(solution)/shard_map/ppermute | solution.py:13
  192.2 27.7 %all-to-all-start.2 = ((bf16[128,8,512]{2,1,0:T(8,128)(2,1)}), bf16[128,8,512]{2,1,0:T(8,128)(2,1)}, u32[]{:S(2)}, u32[]{:S(2)}) async-start(bf16[128,8,512]{2,1,0:T(8,128)(2,1)} %bitcast.143), calls=%async_computation.2 | async-start | bytes 2097152 | tf_op jit(solution)/shard_map/all_to_all | solution.py:113
  201.7 164.7 %all-reduce.11.cloned.1.call-start = ((), (), s32[]{:S(2)}) async-start(), calls=%async_computation.3 | async-start | bytes 1835008 | tf_op jit(solution)/shard_map/psum | solution.py:203
  206.9 16.2 %copy-start.45 = (bf16[512]{0:T(512)(128)(2,1)S(1)}, bf16[512]{0:T(512)(128)(2,1)}, u32[]{:S(2)}) copy-start(bf16[512]{0:T(512)(128)(2,1)} %copy-done.44) | copy-start | bytes 3076
  206.9 16.2 %copy-start.50 = (bf16[256,512]{1,0:T(8,128)(2,1)S(1)}, bf16[256,512]{1,0:T(8,128)(2,1)}, u32[]{:S(2)}) copy-start(bf16[256,512]{1,0:T(8,128)(2,1)} %param.30) | copy-start | bytes 786436
  206.9 16.2 %copy-start.52 = (bf16[128,512]{1,0:T(8,128)(2,1)S(1)}, bf16[128,512]{1,0:T(8,128)(2,1)}, u32[]{:S(2)}) copy-start(bf16[128,512]{1,0:T(8,128)(2,1)} %param.29) | copy-start | bytes 393220
  206.9 16.2 %copy-start.54 = (bf16[64,512]{1,0:T(8,128)(2,1)S(1)}, bf16[64,512]{1,0:T(8,128)(2,1)}, u32[]{:S(2)}) copy-start(bf16[64,512]{1,0:T(8,128)(2,1)} %param.28) | copy-start | bytes 196612
  227.3 16.2 %copy-start.36 = (pred[1024]{0:T(1024)(128)(4,1)S(1)}, pred[1024]{0:T(1024)(128)(4,1)}, u32[]{:S(2)}) copy-start(pred[1024]{0:T(1024)(128)(4,1)} %copy-done.35) | copy-start | bytes 3076
  227.3 17.4 %copy-start.38 = (pred[1024]{0:T(1024)(128)(4,1)S(1)}, pred[1024]{0:T(1024)(128)(4,1)}, u32[]{:S(2)}) copy-start(pred[1024]{0:T(1024)(128)(4,1)} %copy-done.37) | copy-start | bytes 3076
  (37 other events, 113.6 us)
Sparse Core Ops, SparseCore 0:
  223.2 143.0 all-reduce.10
where the time goes:
time: 381 us; the launch traced here: 378 us
  waiting for transfers between devices  152 us (40%)
  local copies, waits for them, and re-layouts  89.6 us (24%)
  other arithmetic  52.4 us (14%)
  starting transfers between devices  31.1 us (8%)
  matrix products  30.9 us (8%)
  between operations  22.1 us (6%)
    psum x1, waiting for transfers between devices, body(): lift_sum = lax.psum(lift_term[:448], ('dp', 'table'))  114 us
    gather x1, local copies, waits for them, and re-layouts, body(): asked_class = width_class[self_rank * items_here + asked]  34.2 us
    all_to_all x2, waiting for transfers between devices, route_rows(): lax.all_to_all(payload, ('dp', 'table'), split_axis=0, concat_axis=0, til...  19 us
    all_to_all x2, starting transfers between devices, route_rows(): lax.all_to_all(payload, ('dp', 'table'), split_axis=0, concat_axis=0, til...  17 us
    all_to_all x1, starting transfers between devices, route_ids(): lax.all_to_all(requests, ('dp', 'table'), split_axis=0, concat_axis=0, ti...  11.5 us
    ppermute x2, waiting for transfers between devices, from_partner(): lax.ppermute(value, axis, [(i, i ^ 1 << bit) for i in range(lax.axis_size...  11 us
    dot_general x2, matrix products, layer(): jnp.dot(normed, joined_weight, preferred_element_type=jnp.float32)  9.66 us
    all_to_all x1, waiting for transfers between devices, route_ids(): lax.all_to_all(requests, ('dp', 'table'), split_axis=0, concat_axis=0, ti...  8.23 us
  transfers between devices with their start and end apart: 6, of which 6 were waited for; matrix products, arithmetic and copies ran while one was open for 11% of the time, Pallas kernels for 0%

commit v1 on v0

v1 whole, which is shorter than its diff:
```python
import jax
import jax.numpy as jnp
from jax import lax
from jax.experimental import pallas as pl
from jax.experimental.pallas import tpu as pltpu
from jax.sharding import PartitionSpec as P

HEADS = 4
HEAD = 128
MAXLEN = 256
WIDTH = 512
CAP = 8
LANES = 128

F32 = jnp.float32
BF16 = jnp.bfloat16
I32 = jnp.int32


def iota(shape, dim):
    return lax.broadcasted_iota(I32, shape, dim)


def one_hot(mask):
    return jnp.where(mask, 1.0, 0.0).astype(BF16)


def dot(a, b):
    return jnp.dot(a, b, preferred_element_type=F32)


def dot_nt(a, b):
    return lax.dot_general(a, b, (((1,), (1,)), ((), ())), preferred_element_type=F32)


def dot_tn(a, b):
    return lax.dot_general(a, b, (((0,), (0,)), ((), ())), preferred_element_type=F32)


def to_column(row):
    eye = iota((LANES, LANES), 0) == iota((LANES, LANES), 1)
    parts = []
    for start in range(0, row.shape[1], LANES):
        piece = row[:, start : start + LANES].astype(F32)
        parts.append(jnp.sum(jnp.where(eye, piece, 0.0), axis=1, keepdims=True))
    return jnp.concatenate(parts, axis=0).astype(I32)


def to_row(column):
    eye = iota((LANES, LANES), 0) == iota((LANES, LANES), 1)
    parts = []
    for start in range(0, column.shape[0], LANES):
        piece = column[start : start + LANES].astype(F32)
        parts.append(jnp.sum(jnp.where(eye, piece, 0.0), axis=0, keepdims=True))
    return jnp.concatenate(parts, axis=1).astype(I32)


def lane_sum(mask, values):
    return jnp.sum(jnp.where(mask, values, 0.0), axis=1, keepdims=True).astype(I32)


def flat_row(ref):
    return jnp.concatenate([ref[0:1, :], ref[1:2, :]], axis=1)


def request_kernel(owner_ref, item_ref, request_ref, slot_ref):
    devices = request_ref.shape[0]
    owner = flat_row(owner_ref)
    item = flat_row(item_ref)
    tokens = owner.shape[1]
    named = iota((devices, tokens), 0) == owner
    hot = one_hot(named)
    earlier = one_hot(iota((tokens, tokens), 0) < iota((tokens, tokens), 1))
    before = dot(hot, earlier)
    rank = jnp.sum(jnp.where(named, before, 0.0), axis=0, keepdims=True).astype(I32)
    place = iota((2 * CAP, tokens), 0)
    value = jnp.where(place < CAP, item >> 6, item & 63)
    table = jnp.where((place & (CAP - 1)) == rank, value, 0).astype(F32).astype(BF16)
    filled = dot_nt(hot, table).astype(I32)
    request_ref[...] = filled[:, :CAP] * 64 + filled[:, CAP:]
    slot = owner * CAP + rank
    half = tokens // 2
    slot_ref[0:1, :] = slot[:, :half]
    slot_ref[1:2, :] = slot[:, half:]


def class_kernel(owner_ref, item_ref, class_list_ref, class_ref):
    item = to_column(flat_row(item_ref))
    line = to_column(flat_row(owner_ref)) * (4096 // LANES) + (item >> 7)
    tokens = line.shape[0]
    lines = class_list_ref.shape[0]
    step = 512
    total = jnp.zeros((tokens, LANES), F32)
    for start in range(0, lines, step):
        hot = one_hot(iota((tokens, step), 1) + start == line)
        total += dot(hot, class_list_ref[start : start + step, :].astype(F32).astype(BF16))
    class_ref[...] = lane_sum(iota((tokens, LANES), 1) == (item & 127), total)


def owner_kernel(asked_ref, class_ref, slab_ref, narrow_ref, middle_ref, wide_ref, reply_ref, code_ref):
    asked = asked_ref[...]
    sources = asked.shape[0]
    amount = sources * CAP
    expand = one_hot((iota((amount, sources), 0) >> 3) == iota((amount, sources), 1))
    mine = (iota((amount, CAP), 0) & (CAP - 1)) == iota((amount, CAP), 1)
    high = lane_sum(mine, dot(expand, (asked >> 7).astype(F32).astype(BF16)))
    low = lane_sum(mine, dot(expand, (asked & 127).astype(F32).astype(BF16)))
    groups = slab_ref.shape[0]
    slab_list = slab_ref[...]
    marks = jnp.concatenate([slab_list & 127, (slab_list >> 7) + 16 * class_ref[...]], axis=1)
    found = dot(one_hot(iota((amount, groups), 1) == high), marks.astype(F32).astype(BF16))
    mine = iota((amount, LANES), 1) == low
    code_low = lane_sum(mine, found[:, :LANES])
    code_high = lane_sum(mine, found[:, LANES:])
    code_ref[...] = code_high * LANES + code_low
    step = 256
    lines = wide_ref.shape[0]
    packed_lines = narrow_ref.shape[0]

    @pl.loop(0, amount // step)
    def _(block):
        rows = pl.ds(pl.multiple_of(block * step, step), step)
        code = code_ref[rows, :]
        kind = code >> 11
        slab = code & 2047
        hot = one_hot(iota((step, lines), 1) == jnp.where(kind == 0, slab >> 1, slab))
        from_wide = dot(hot, wide_ref[...])
        from_middle = dot(hot, middle_ref[...])
        from_narrow = dot(hot[:, :packed_lines], narrow_ref[...])
        from_narrow = jnp.where((slab & 1) == 1, pltpu.roll(from_narrow, 64, 1), from_narrow)
        from_narrow = jnp.where(iota((step, LANES), 1) < 64, from_narrow, 0.0)
        left = jnp.where(kind == 2, from_wide[:, :LANES], jnp.where(kind == 1, from_middle, from_narrow))
        right = jnp.where(kind == 2, from_wide[:, LANES:], 0.0)
        reply_ref[rows, :] = jnp.concatenate([left, right], axis=1).astype(BF16)


def foreign_slot(rank_ref, list_ref):
    rank = rank_ref[0]
    return jnp.where((list_ref[rank, 0] >> 1) != rank, 0, 1)


def pick_rows(slot_ref, which, landed_ref):
    slot = to_column(slot_ref[pl.ds(which, 1), :])
    hot = one_hot(iota((slot.shape[0], landed_ref.shape[0]), 1) == slot)
    return dot(hot, landed_ref[...]).astype(BF16)


def give_kernel(rank_ref, list_ref, slot_ref, landed_ref, class_ref, given_ref):
    which = foreign_slot(rank_ref, list_ref)
    rows = given_ref.shape[0]
    given_ref[:, :256] = pick_rows(slot_ref, which, landed_ref)
    kind = class_ref[pl.ds(pl.multiple_of(which * rows, rows), rows), :]
    given_ref[:, 256:] = jnp.broadcast_to(kind.astype(F32).astype(BF16), (rows, LANES))


def mean(values):
    return jnp.sum(values, axis=1, keepdims=True) * (1.0 / WIDTH)


def normalize(values):
    centre = values - mean(values)
    scale = lax.rsqrt(mean(centre * centre) + 1e-06)
    return centre * scale, scale


def normalize_grad(grad, normed, scale):
    return scale * (grad - mean(grad) - normed * mean(grad * normed))


def sigmoid(values):
    return 0.5 * jnp.tanh(0.5 * values) + 0.5


def rounded(values):
    return values.astype(BF16).astype(F32)


def layer(raw, kind, length, cotangent, lift_ref, joined_weight_ref, output_weight_ref, slope_ref, curve_ref):
    rows = raw.shape[0]
    zero = jnp.zeros((), BF16)
    spread = jnp.concatenate(
        [
            jnp.where(kind == 2, raw, zero),
            jnp.where(kind == 1, raw[:, :LANES], zero),
            jnp.where(kind == 0, raw[:, :LANES], zero),
        ],
        axis=1,
    )
    widened = rounded(dot(spread, lift_ref[...]))
    normed, scale = normalize(widened)
    normed_low = normed.astype(BF16)
    joined = []
    for part in range(4):
        columns = slice(part * WIDTH, (part + 1) * WIDTH)
        before = dot(normed_low, joined_weight_ref[:, columns])
        gate = sigmoid(before)
        joined.append((before * gate).astype(BF16))
        slope_ref[:, columns] = gate * (1.0 + before * (1.0 - gate))
    gating, values, queries, keys = joined
    gating = gating.astype(F32)
    across = iota((rows, rows), 1)
    allowed = (across <= iota((rows, rows), 0)) & (across < length)
    factor = jnp.where(allowed, 1.0 / MAXLEN, 0.0)
    weights = []
    mixed = []
    for head in range(HEADS):
        columns = slice(head * HEAD, (head + 1) * HEAD)
        scores = dot_nt(queries[:, columns], keys[:, columns])
        gate = sigmoid(scores)
        scaled = gate * factor
        weights.append((scores * scaled).astype(BF16))
        curve_ref[head] = scaled * (1.0 + scores * (1.0 - gate))
        mixed.append(dot(weights[head], values[:, columns]))
    mixed_normed, mixed_scale = normalize(jnp.concatenate(mixed, axis=1))
    gated = (mixed_normed * gating).astype(BF16)
    result = dot(gated, output_weight_ref[...]) + widened
    valid = iota((rows, 1), 0) < length
    output = jnp.where(valid, result, 0.0).astype(BF16)

    result_grad = jnp.where(valid, cotangent, zero)
    gated_grad = rounded(dot_nt(result_grad, output_weight_ref[...]))
    gating_grad = (gated_grad * mixed_normed).astype(BF16)
    mixed_grad = normalize_grad(gated_grad * gating, mixed_normed, mixed_scale).astype(BF16)
    values_grad = []
    queries_grad = []
    keys_grad = []
    for head in range(HEADS):
        columns = slice(head * HEAD, (head + 1) * HEAD)
        own = mixed_grad[:, columns]
        weights_grad = rounded(dot_nt(own, values[:, columns]))
        scores_grad = (weights_grad * curve_ref[head]).astype(BF16)
        values_grad.append(dot_tn(weights[head], own).astype(BF16))
        queries_grad.append(dot(scores_grad, keys[:, columns]).astype(BF16))
        keys_grad.append(dot_tn(scores_grad, queries[:, columns]).astype(BF16))
    joined_grad = [gating_grad] + [jnp.concatenate(g, axis=1) for g in (values_grad, queries_grad, keys_grad)]
    normed_grad = jnp.zeros((rows, WIDTH), F32)
    for part in range(4):
        columns = slice(part * WIDTH, (part + 1) * WIDTH)
        before_grad = (joined_grad[part].astype(F32) * slope_ref[:, columns]).astype(BF16)
        normed_grad += dot_nt(before_grad, joined_weight_ref[:, columns])
    grad = normalize_grad(rounded(normed_grad), normed, scale) + result_grad.astype(F32)
    grad = grad.astype(BF16)
    spread_grad = dot_nt(grad, lift_ref[...])
    narrow_part = jnp.where(iota((rows, LANES), 1) < 64, spread_grad[:, 384:], 0.0)
    left = jnp.where(
        kind == 2, spread_grad[:, :LANES], jnp.where(kind == 1, spread_grad[:, 256:384], narrow_part)
    )
    right = jnp.where(kind == 2, spread_grad[:, LANES:256], 0.0)
    row_grad = jnp.concatenate([left, right], axis=1).astype(BF16)
    return output, row_grad, dot_tn(spread, grad)


def kept_kernel(
    rank_ref, list_ref, length_ref, slot_ref, landed_ref, class_ref, cotangent_ref, lift_ref,
    joined_weight_ref, output_weight_ref, output_ref, grad_ref, term_ref, slope_ref, curve_ref,
):
    rank = rank_ref[0]
    which = 1 - foreign_slot(rank_ref, list_ref)
    rows = grad_ref.shape[0]
    raw = pick_rows(slot_ref, which, landed_ref)
    kind = class_ref[pl.ds(pl.multiple_of(which * rows, rows), rows), :]
    output, row_grad, term = layer(
        raw, kind, length_ref[rank, which], cotangent_ref[which], lift_ref,
        joined_weight_ref, output_weight_ref, slope_ref, curve_ref,
    )
    output_ref[...] = output
    grad_ref[...] = row_grad
    term_ref[...] = term


def foreign_kernel(
    rank_ref, list_ref, length_ref, arrived_ref, cotangent_ref, lift_ref, joined_weight_ref,
    output_weight_ref, kept_output_ref, kept_term_ref, output_ref, grad_ref, term_ref, slope_ref, curve_ref,
):
    rank = rank_ref[0]
    which = foreign_slot(rank_ref, list_ref)
    source = list_ref[rank, which]
    kind = arrived_ref[:, 256:257].astype(F32).astype(I32)
    output, row_grad, term = layer(
        arrived_ref[:, :256], kind, length_ref[source >> 1, source & 1], cotangent_ref[which], lift_ref,
        joined_weight_ref, output_weight_ref, slope_ref, curve_ref,
    )
    output_ref[which] = output
    output_ref[1 - which] = kept_output_ref[...]
    grad_ref[...] = row_grad
    term_ref[...] = (term + kept_term_ref[...]).astype(BF16)


def send_kernel(rank_ref, list_ref, slot_ref, kept_grad_ref, returned_ref, term_ref, payload_ref):
    which = foreign_slot(rank_ref, list_ref)
    devices = payload_ref.shape[0]
    rows = kept_grad_ref.shape[0]
    places = iota((devices * CAP, rows), 0)
    total = dot(one_hot(places == slot_ref[pl.ds(1 - which, 1), :]), kept_grad_ref[...])
    total += dot(one_hot(places == slot_ref[pl.ds(which, 1), :]), returned_ref[...])
    term = term_ref[...].astype(F32).reshape(devices // 2, CAP, WIDTH)
    term = jnp.stack([term[:, :, :256], term[:, :, 256:]], axis=1).reshape(devices, CAP, 256)
    total = total.reshape(devices, CAP, 256)
    payload_ref[...] = jnp.concatenate([total, term], axis=1).astype(BF16)


def sum_kernel(landed_ref, share_ref):
    total = jnp.sum(landed_ref[...].astype(F32), axis=0)[CAP:]
    share_ref[...] = jnp.broadcast_to(total[None].astype(BF16), share_ref.shape)


def scatter_kernel(landed_ref, code_ref, narrow_ref, middle_ref, wide_ref):
    sources = landed_ref.shape[0]
    amount = sources * CAP
    grads = landed_ref[...].astype(F32)[:, :CAP, :].reshape(amount, 256)
    code = code_ref[...]
    kind = code >> 11
    slab = code & 2047
    line = to_row(jnp.where(kind == 0, slab >> 1, slab))
    wide = jnp.where(kind == 2, grads, 0.0).astype(BF16)
    middle = jnp.where(kind == 1, grads[:, :LANES], 0.0).astype(BF16)
    narrow = jnp.where((kind == 0) & (iota((amount, LANES), 1) < 64), grads[:, :LANES], 0.0)
    narrow = jnp.where((slab & 1) == 1, pltpu.roll(narrow, 64, 1), narrow).astype(BF16)
    step = 256
    for start in range(0, wide_ref.shape[0], step):
        hot = one_hot(iota((step, amount), 0) + start == line)
        wide_ref[start : start + step, :] = dot(hot, wide)
        middle_ref[start : start + step, :] = dot(hot, middle)
        if start < narrow_ref.shape[0]:
            narrow_ref[start : start + step, :] = dot(hot, narrow)


def delta_kernel(shares_ref, narrow_ref, middle_ref, wide_ref):
    devices = shares_ref.shape[0]
    shares = shares_ref[...].astype(F32).reshape(devices // 2, 2, CAP, 256)
    for half in range(2):
        columns = slice(half * 256, (half + 1) * 256)
        whole = shares[:, half].reshape(devices // 2 * CAP, 256)
        wide_ref[:, columns] = whole[:256]
        middle_ref[:, columns] = whole[256:384]
        narrow_ref[:, columns] = whole[384:448]


def call(kernel, outs, args, smem=0, scratch=(), flops=0, limit=32):
    specs = [pl.BlockSpec(memory_space=pltpu.SMEM)] * smem
    specs += [pl.BlockSpec(memory_space=pltpu.VMEM)] * (len(args) - smem)
    shapes = [jax.ShapeDtypeStruct(shape, dtype) for shape, dtype in outs]
    moved = sum(a.size * a.dtype.itemsize for a in args) + sum(s.size * s.dtype.itemsize for s in shapes)
    return pl.pallas_call(
        kernel,
        out_shape=shapes,
        in_specs=specs,
        out_specs=[pl.BlockSpec(memory_space=pltpu.VMEM)] * len(shapes),
        scratch_shapes=list(scratch),
        cost_estimate=pl.CostEstimate(flops=flops, bytes_accessed=moved, transcendentals=0),
        compiler_params=pltpu.CompilerParams(vmem_limit_bytes=limit << 20),
    )(*args)


def exchange(array):
    return lax.all_to_all(array, ("dp", "table"), split_axis=0, concat_axis=0, tiled=True)


def body(
    history_lengths,
    balance_list,
    owner_device,
    owner_row,
    width_class,
    slab_index,
    narrow_table,
    middle_table,
    wide_table,
    narrow_lift,
    middle_lift,
    wide_lift,
    joined_weight,
    output_weight,
    cotangent,
):
    data_size = lax.axis_size("dp")
    table_size = lax.axis_size("table")
    devices = data_size * table_size
    rows = cotangent.shape[1]
    items = slab_index.shape[0]
    amount = devices * CAP
    data_rank = lax.axis_index("dp")
    self_rank = data_rank * table_size + lax.axis_index("table")
    rank = data_rank.reshape(1).astype(I32)
    owner = owner_device.reshape(owner_row.shape)
    class_list = width_class.reshape(-1, LANES)
    partners = [(i, i ^ (data_size // 2)) for i in range(data_size)]

    requests, slots = call(
        request_kernel, [((devices, CAP), I32), (owner.shape, I32)], (owner, owner_row), flops=10**8
    )
    asked = exchange(requests)
    (kinds,) = call(
        class_kernel, [((2 * rows, 1), I32)], (owner, owner_row, class_list), flops=10**9
    )
    own_classes = lax.dynamic_slice(class_list, (self_rank * (items // LANES), 0), (items // LANES, LANES))
    lift_all = jnp.concatenate(
        [wide_lift, middle_lift, narrow_lift, jnp.zeros((64, WIDTH), BF16)], axis=0
    )
    replies, codes = call(
        owner_kernel,
        [((amount, 256), BF16), ((amount, 1), I32)],
        (asked, own_classes, slab_index.reshape(-1, LANES), narrow_table, middle_table, wide_table),
        flops=3 * 10**9,
    )
    landed = exchange(replies)
    (given,) = call(
        give_kernel, [((rows, 384), BF16)], (rank, balance_list, slots, landed, kinds), smem=2, flops=10**8
    )
    arrived = lax.ppermute(given, "dp", partners)
    scratch = (pltpu.VMEM((rows, 4 * WIDTH), F32), pltpu.VMEM((HEADS, rows, rows), F32))
    kept_output, kept_grad, kept_term = call(
        kept_kernel,
        [((rows, WIDTH), BF16), ((rows, 256), BF16), ((WIDTH, WIDTH), F32)],
        (rank, balance_list, history_lengths, slots, landed, kinds, cotangent, lift_all, joined_weight, output_weight),
        smem=3,
        scratch=scratch,
        flops=5 * 10**9,
    )
    output, foreign_grad, term = call(
        foreign_kernel,
        [(cotangent.shape, BF16), ((rows, 256), BF16), ((WIDTH, WIDTH), BF16)],
        (
            rank, balance_list, history_lengths, arrived, cotangent, lift_all, joined_weight, output_weight,
            kept_output, kept_term,
        ),
        smem=3,
        scratch=scratch,
        flops=5 * 10**9,
    )
    returned = lax.ppermute(foreign_grad, "dp", partners)
    (payload,) = call(
        send_kernel,
        [((devices, 2 * CAP, 256), BF16)],
        (rank, balance_list, slots, kept_grad, returned, term),
        smem=2,
        flops=10**9,
    )
    home = exchange(payload)
    (share,) = call(sum_kernel, [((devices, CAP, 256), BF16)], (home,))
    shares = exchange(share)
    narrow_grad, middle_grad, wide_grad = call(
        scatter_kernel,
        [(narrow_table.shape, F32), (middle_table.shape, F32), (wide_table.shape, F32)],
        (home, codes),
        flops=3 * 10**9,
    )
    narrow_delta, middle_delta, wide_delta = call(
        delta_kernel,
        [(narrow_lift.shape, F32), (middle_lift.shape, F32), (wide_lift.shape, F32)],
        (shares,),
    )
    return (output, narrow_grad, middle_grad, wide_grad, narrow_delta, middle_delta, wide_delta)


def solution(mesh):
    in_specs = (
        P(None, "table"),
        P(None, "table"),
        P(("dp", "table"), None, None),
        P(("dp", "table"), None),
        P(),
        P(("dp", "table")),
        P(("dp", "table"), None),
        P(("dp", "table"), None),
        P(("dp", "table"), None),
        P(),
        P(),
        P(),
        P(),
        P(),
        P(("dp", "table"), None, None),
    )
    out_specs = (
        P(("dp", "table"), None, None),
        P(("dp", "table"), None),
        P(("dp", "table"), None),
        P(("dp", "table"), None),
        P(),
        P(),
        P(),
    )
    return jax.shard_map(body, mesh=mesh, in_specs=in_specs, out_specs=out_specs, check_vma=False)
```

time: 381 us -> 122 us (0.32)
  waiting for transfers between devices: 152 us -> 30 us
  local copies, waits for them, and re-layouts: 89.6 us -> 10.7 us
  other arithmetic: 52.4 us -> 1.06 us
  matrix products: 30.9 us -> 0 us
  Pallas kernels: 0 us -> 28.9 us
  blocking collectives: 0 us -> 25.7 us
  between operations: 22.1 us -> 0.81 us
  starting transfers between devices: 31.1 us -> 24.2 us
    psum x1 -> x0, waiting for transfers between devices: 114 us -> none  [body(): lift_sum = lax.psum(lift_term[:448], ('dp', 'table'))]
    gather x10 -> x0, local copies, waits for them, and re-layouts: 59.5 us -> none  [the longest x1 34.2 us: body(): asked_class = width_class[self_rank * items_here + asked]]
    dot_general x13 -> x0, matrix products: 30.9 us -> none  [the longest x2 9.66 us: layer(): jnp.dot(normed, joined_weight, preferred_element_type=jnp.float32)]
    pallas_call x0 -> x10, Pallas kernels: none -> 28.9 us  [call(): pl.pallas_call(kernel, out_shape=shapes, in_specs=specs, out_specs=[pl.Bl...]
    scatter-add x5 -> x0, other arithmetic: 26.9 us -> none  [the longest x1 8.17 us: add_rows(): wide_sum.at[slab_rows].add(jnp.where((classes == 2)[:, None], widened, 0.0))]
    all_to_all x0 -> x1, blocking collectives: none -> 25.7 us  [exchange(): lax.all_to_all(array, ('dp', 'table'), split_axis=0, concat_axis=0, tiled...]
    reshape x7 -> x0, local copies, waits for them, and re-layouts: 9.62 us -> none  [the longest x2 3.51 us: layer(): queries = joined[:, 2 * width:3 * width].reshape(rows_total, HEADS, HEAD)]
    ppermute x2, waiting for transfers between devices: 11 us -> 3.23 us  [the longest x1 3.23 us: body(): returned = lax.ppermute(foreign_grad, 'dp', partners)]
  transfers between devices with their start and end apart: 6 -> 5, of which waited for: 6 -> 4; matrix products, arithmetic and copies ran while one was open for 11% -> 2% of each run, Pallas kernels for 0% -> 10%
where the time goes in v1:
time: 122 us; the launch traced here: 121 us
  waiting for transfers between devices  30 us (25%)
  Pallas kernels  28.9 us (24%)
  blocking collectives  25.7 us (21%)
  starting transfers between devices  24.2 us (20%)
  local copies, waits for them, and re-layouts  10.7 us (9%)
    pallas_call x10, Pallas kernels, call(): pl.pallas_call(kernel, out_shape=shapes, in_specs=specs, out_specs=[pl.Bl...  28.9 us
    all_to_all x3, waiting for transfers between devices, exchange(): lax.all_to_all(array, ('dp', 'table'), split_axis=0, concat_axis=0, tiled...  26.8 us
    all_to_all x1, blocking collectives, exchange(): lax.all_to_all(array, ('dp', 'table'), split_axis=0, concat_axis=0, tiled...  25.7 us
    all_to_all x3, starting transfers between devices, exchange(): lax.all_to_all(array, ('dp', 'table'), split_axis=0, concat_axis=0, tiled...  20.9 us
    unnamed x39, local copies, waits for them, and re-layouts  9.88 us
    ppermute x1, waiting for transfers between devices, body(): returned = lax.ppermute(foreign_grad, 'dp', partners)  3.23 us
  transfers between devices with their start and end apart: 5, of which 4 were waited for; matrix products, arithmetic and copies ran while one was open for 2% of the time, Pallas kernels for 10%

profile of v1, /device:TPU:1, one launch (start us, length us, event | category | flops | bytes accessed | tf_op | source)
XLA Modules:
  0.0 121.4 jit_solution(6268204407128767904)
XLA Ops:
  2.0 1.1 shard_map.198
  3.1 11.5 %all-to-all-start = ((s32[128,1,8]{2,1,0:T(1,128)}), s32[128,1,8]{2,1,0:T(1,128)S(1)}, u32[]{:S(2)}, u32[]{:S(2)}) async-start(s32[128,1,8]{2,1,0:T(1,128)} %bitcast.2), calls=%async_computation | async-start | bytes 131072 | tf_op jit(solution)/shard_map/all_to_all | solution.py:356
  15.4 8.8 %all-to-all-done = s32[128,1,8]{2,1,0:T(1,128)S(1)} async-done(((s32[128,1,8]{2,1,0:T(1,128)}), s32[128,1,8]{2,1,0:T(1,128)S(1)}, u32[]{:S(2)}, u32[]{:S(2)}) %all-to-all-start) | async-done | bytes 4128 | tf_op jit(solution)/shard_map/all_to_all | solution.py:356
  24.1 1.2 %copy-done.3 = bf16[2048,256]{1,0:T(8,128)(2,1)S(1)} copy-done((bf16[2048,256]{1,0:T(8,128)(2,1)S(1)}, bf16[2048,256]{1,0:T(8,128)(2,1)}, u32[]{:S(2)}) %copy-start.3) | copy-done | bytes 1048600
  25.3 1.0 copy-done.4
  28.1 5.5 %shard_map.199 = (bf16[1024,256]{1,0:T(8,128)(2,1)}, s32[1024,1]{1,0:T(8,128)S(1)}) custom-call(s32[128,8]{1,0:T(8,128)S(1)} %bitcast.14, s32[32,128]{1,0:T(8,128)S(1)} %constant_dynamic-slice_fusion.class_ref, s32[32,128]{1,0:T(8,128)S(1)} %bitcast.19, bf16[1024,128]{1,0:T(8,128)(2,1)S(1)} %copy-done.9, bf16[2048,128]{1,0:T(8,128)(2,1)S(1)} %copy-done.4, ...), custom_call_target="tpu_custom_call" | custom-call | flops 3000000000 | bytes 2400256 | tf_op jit(solution)/shard_map/pallas_call | solution.py:344
  33.6 4.5 %all-to-all-start.1 = ((bf16[128,8,256]{2,1,0:T(8,128)(2,1)}), bf16[128,8,256]{2,1,0:T(8,128)(2,1)S(1)}, u32[]{:S(2)}, u32[]{:S(2)}) async-start(bf16[128,8,256]{2,1,0:T(8,128)(2,1)} %bitcast.6), calls=%async_computation.1 | async-start | bytes 1048576 | tf_op jit(solution)/shard_map/all_to_all | solution.py:356
  39.1 1.6 %shard_map.200.class_ref = s32[512,1]{1,0:T(8,128)S(1)} custom-call(s32[2,256]{1,0:T(2,128)S(1)} %bitcast.16, s32[2,256]{1,0:T(2,128)S(1)} %copy-done.12, s32[4096,128]{1,0:T(8,128)S(1)} %bitcast.18), custom_call_target="tpu_custom_call" | custom-call | flops 1000000000 | bytes 2103296 | tf_op jit(solution)/shard_map/pallas_call | solution.py:344
  40.7 1.1 maximum_maximum_fusion.lift_ref
  41.8 9.7 %all-to-all-done.1 = bf16[128,8,256]{2,1,0:T(8,128)(2,1)S(1)} async-done(((bf16[128,8,256]{2,1,0:T(8,128)(2,1)}), bf16[128,8,256]{2,1,0:T(8,128)(2,1)S(1)}, u32[]{:S(2)}, u32[]{:S(2)}) %all-to-all-start.1) | async-done | bytes 524320 | tf_op jit(solution)/shard_map/all_to_all | solution.py:356
  51.5 1.1 shard_map.201
  52.6 1.1 collective-permute-start
  53.7 1.6 %copy-done.1 = bf16[512,2048]{1,0:T(8,128)(2,1)S(1)} copy-done((bf16[512,2048]{1,0:T(8,128)(2,1)S(1)}, bf16[512,2048]{1,0:T(8,128)(2,1)}, u32[]{:S(2)}) %copy-start.1) | copy-done | bytes 2097176
  55.3 1.0 copy-done.5
  56.3 1.0 copy-done.7
  57.4 6.0 %shard_map.202 = (bf16[256,512]{1,0:T(8,128)(2,1)S(1)}, bf16[256,256]{1,0:T(8,128)(2,1)S(1)}, f32[512,512]{1,0:T(8,128)S(1)}) custom-call(s32[1]{0:T(128)} %bitcast.rank_ref, s32[8,2]{1,0:T(8,128)S(1)} %copy.32.list_ref, s32[8,2]{1,0:T(8,128)S(1)} %copy.33.length_ref, s32[2,256]{1,0:T(2,128)S(1)} %get-tuple-element.23.slot_ref, ...), custom_call_target="tpu_custom_call" | custom-call | flops 5000000000 | bytes 5640324 | tf_op jit(solution)/shard_map/pallas_call | solution.py:344
  63.4 5.5 %shard_map.203 = (bf16[2,256,512]{2,1,0:T(8,128)(2,1)}, bf16[256,256]{1,0:T(8,128)(2,1)S(1)}, bf16[512,512]{1,0:T(8,128)(2,1)S(1)}) custom-call(s32[1]{0:T(128)} %bitcast.rank_ref, s32[8,2]{1,0:T(8,128)S(1)} %copy.32.list_ref, s32[8,2]{1,0:T(8,128)S(1)} %copy.33.length_ref, bf16[256,384]{1,0:T(8,128)(2,1)S(1)} %collective-permute-done.arrived_ref, ...), custom_call_target="tpu_custom_call" | custom-call | flops 5000000000 | bytes 6357124 | tf_op jit(solution)/shard_map/pallas_call | solution.py:344
  68.9 2.2 %collective-permute-start.1 = (bf16[256,256]{1,0:T(8,128)(2,1)S(1)}, bf16[256,256]{1,0:T(8,128)(2,1)S(1)}, u32[]{:S(2)}, u32[]{:S(2)}) collective-permute-start(bf16[256,256]{1,0:T(8,128)(2,1)S(1)} %get-tuple-element.30), channel_id=1, source_target_pairs={{0,64},{16,80},{32,96},{48,112},{64,0},{80,16},{96,32},{112,48},{1... | collective-permute-start | bytes 393224 | tf_op jit(solution)/shard_map/ppermute | solution.py:431
  71.1 3.2 %collective-permute-done.1.returned_ref = bf16[256,256]{1,0:T(8,128)(2,1)S(1)} collective-permute-done((bf16[256,256]{1,0:T(8,128)(2,1)S(1)}, bf16[256,256]{1,0:T(8,128)(2,1)S(1)}, u32[]{:S(2)}, u32[]{:S(2)}) %collective-permute-start.1) | collective-permute-done | bytes 131104 | tf_op jit(solution)/shard_map/ppermute | solution.py:431
  74.3 1.0 shard_map.204
  75.4 25.7 %all_to_all.32.landed_ref = bf16[128,16,256]{2,1,0:T(8,128)(2,1)S(1)} all-to-all(bf16[128,16,256]{2,1,0:T(8,128)(2,1)S(1)} %shard_map.204), channel_id=1, replica_groups=mesh['dp'=8,'table'=16] {'dp','table'}, dimensions={0} | all-to-all | bytes 2097152 | tf_op jit(solution)/shard_map/all_to_all | solution.py:356
  102.0 4.9 %all-to-all-start.3 = ((bf16[128,8,256]{2,1,0:T(8,128)(2,1)}), bf16[128,8,256]{2,1,0:T(8,128)(2,1)S(1)}, u32[]{:S(2)}, u32[]{:S(2)}) async-start(bf16[128,8,256]{2,1,0:T(8,128)(2,1)} %shard_map.206), calls=%async_computation.3 | async-start | bytes 1048576 | tf_op jit(solution)/shard_map/all_to_all | solution.py:356
  107.0 5.1 %shard_map.205 = (f32[1024,128]{1,0:T(8,128)}, f32[2048,128]{1,0:T(8,128)}, f32[2048,256]{1,0:T(8,128)}) custom-call(bf16[128,16,256]{2,1,0:T(8,128)(2,1)S(1)} %all_to_all.32.landed_ref, s32[1024,1]{1,0:T(8,128)S(1)} %copy-done.14), custom_call_target="tpu_custom_call" | custom-call | flops 3000000000 | bytes 4722688 | tf_op jit(solution)/shard_map/pallas_call | solution.py:344
  112.0 8.4 %all-to-all-done.3.shares_ref = bf16[128,8,256]{2,1,0:T(8,128)(2,1)S(1)} async-done(((bf16[128,8,256]{2,1,0:T(8,128)(2,1)}), bf16[128,8,256]{2,1,0:T(8,128)(2,1)S(1)}, u32[]{:S(2)}, u32[]{:S(2)}) %all-to-all-start.3) | async-done | bytes 524320 | tf_op jit(solution)/shard_map/all_to_all | solution.py:356
  (40 shorter events, 6.7 us)
Async XLA Ops:
  1.3 0.7 copy-start.11
  3.1 21.0 %all-to-all-start = ((s32[128,1,8]{2,1,0:T(1,128)}), s32[128,1,8]{2,1,0:T(1,128)S(1)}, u32[]{:S(2)}, u32[]{:S(2)}) async-start(s32[128,1,8]{2,1,0:T(1,128)} %bitcast.2), calls=%async_computation | async-start | bytes 131072 | tf_op jit(solution)/shard_map/all_to_all | solution.py:356
  24.1 1.2 %copy-start.3 = (bf16[2048,256]{1,0:T(8,128)(2,1)S(1)}, bf16[2048,256]{1,0:T(8,128)(2,1)}, u32[]{:S(2)}) copy-start(bf16[2048,256]{1,0:T(8,128)(2,1)} %wide_ref.1) | copy-start | bytes 3145732
  25.3 1.0 copy-start.4
  26.4 0.9 copy-start.9
  27.3 0.7 copy-start.10
  28.1 10.0 %copy-start.17 = (s32[8,2]{0,1:T(2,128)S(1)}, s32[8,2]{0,1:T(2,128)}, u32[]{:S(2)}) copy-start(s32[8,2]{0,1:T(2,128)} %param.16) | copy-start | bytes 196
  28.1 11.0 %copy-start = (s32[524288]{0:T(1024)S(1)}, s32[524288]{0:T(1024)}, u32[]{:S(2)}) copy-start(s32[524288]{0:T(1024)} %param.19) | copy-start | bytes 6291460
  28.1 11.0 %copy-start.12 = (s32[2,256]{1,0:T(2,128)S(1)}, s32[2,256]{1,0:T(2,128)}, u32[]{:S(2)}) copy-start(s32[2,256]{1,0:T(2,128)} %item_ref.3) | copy-start | bytes 6148
  33.6 5.4 %copy-start.13 = (s32[1024,1]{1,0:T(8,128)}, s32[1024,1]{1,0:T(8,128)S(1)}, u32[]{:S(2)}) copy-start(s32[1024,1]{1,0:T(8,128)S(1)} %get-tuple-element.32.code_ref) | copy-start | bytes 12292
  33.6 17.9 %all-to-all-start.1 = ((bf16[128,8,256]{2,1,0:T(8,128)(2,1)}), bf16[128,8,256]{2,1,0:T(8,128)(2,1)S(1)}, u32[]{:S(2)}, u32[]{:S(2)}) async-start(bf16[128,8,256]{2,1,0:T(8,128)(2,1)} %bitcast.6), calls=%async_computation.1 | async-start | bytes 1048576 | tf_op jit(solution)/shard_map/all_to_all | solution.py:356
  38.1 2.6 %copy-start.15 = (bf16[256,512]{1,0:T(8,128)(2,1)S(1)}, bf16[256,512]{1,0:T(8,128)(2,1)}, u32[]{:S(2)}) copy-start(bf16[256,512]{1,0:T(8,128)(2,1)} %param.26) | copy-start | bytes 786436
  38.1 2.6 %copy-start.16 = (bf16[64,512]{1,0:T(8,128)(2,1)S(1)}, bf16[64,512]{1,0:T(8,128)(2,1)}, u32[]{:S(2)}) copy-start(bf16[64,512]{1,0:T(8,128)(2,1)} %param.24) | copy-start | bytes 196612
  52.6 10.8 %collective-permute-start = (bf16[256,384]{1,0:T(8,128)(2,1)S(1)}, bf16[256,384]{1,0:T(8,128)(2,1)S(1)}, u32[]{:S(2)}, u32[]{:S(2)}) collective-permute-start(bf16[256,384]{1,0:T(8,128)(2,1)S(1)} %shard_map.201), channel_id=1, source_target_pairs={{0,64},{16,80},{32,96},{48,112},{64,0},{80,16},{96,32},{112,48},{1... | collective-permute-start | bytes 589832 | tf_op jit(solution)/shard_map/ppermute | solution.py:410
  53.7 1.6 %copy-start.1 = (bf16[512,2048]{1,0:T(8,128)(2,1)S(1)}, bf16[512,2048]{1,0:T(8,128)(2,1)}, u32[]{:S(2)}) copy-start(bf16[512,2048]{1,0:T(8,128)(2,1)} %joined_weight_ref.3) | copy-start | bytes 6291460
  55.3 1.0 copy-start.5
  56.3 1.0 copy-start.7
  57.4 6.0 %copy-start.2 = (bf16[512,2048]{1,0:T(8,128)(2,1)S(1)}, bf16[512,2048]{1,0:T(8,128)(2,1)}, u32[]{:S(2)}) copy-start(bf16[512,2048]{1,0:T(8,128)(2,1)} %joined_weight_ref.3) | copy-start | bytes 6291460
  57.4 6.0 %copy-start.6 = (bf16[2,256,512]{2,1,0:T(8,128)(2,1)S(1)}, bf16[2,256,512]{2,1,0:T(8,128)(2,1)}, u32[]{:S(2)}) copy-start(bf16[2,256,512]{2,1,0:T(8,128)(2,1)} %cotangent_ref.3) | copy-start | bytes 1572868
  57.4 6.1 %copy-start.8 = (bf16[512,512]{1,0:T(8,128)(2,1)S(1)}, bf16[512,512]{1,0:T(8,128)(2,1)}, u32[]{:S(2)}) copy-start(bf16[512,512]{1,0:T(8,128)(2,1)} %output_weight_ref.3) | copy-start | bytes 1572868
  68.9 5.4 %collective-permute-start.1 = (bf16[256,256]{1,0:T(8,128)(2,1)S(1)}, bf16[256,256]{1,0:T(8,128)(2,1)S(1)}, u32[]{:S(2)}, u32[]{:S(2)}) collective-permute-start(bf16[256,256]{1,0:T(8,128)(2,1)S(1)} %get-tuple-element.30), channel_id=1, source_target_pairs={{0,64},{16,80},{32,96},{48,112},{64,0},{80,16},{96,32},{112,48},{1... | collective-permute-start | bytes 393224 | tf_op jit(solution)/shard_map/ppermute | solution.py:431
  75.3 31.6 %copy-start.14 = (s32[1024,1]{1,0:T(8,128)S(1)}, s32[1024,1]{1,0:T(8,128)}, u32[]{:S(2)}) copy-start(s32[1024,1]{1,0:T(8,128)} %copy-done.13) | copy-start | bytes 12292
  102.0 18.4 %all-to-all-start.3 = ((bf16[128,8,256]{2,1,0:T(8,128)(2,1)}), bf16[128,8,256]{2,1,0:T(8,128)(2,1)S(1)}, u32[]{:S(2)}, u32[]{:S(2)}) async-start(bf16[128,8,256]{2,1,0:T(8,128)(2,1)} %shard_map.206), calls=%async_computation.3 | async-start | bytes 1048576 | tf_op jit(solution)/shard_map/all_to_all | solution.py:356

commit v2 on v1

v2 whole, which is shorter than its diff:
```python
import jax
import jax.numpy as jnp
from jax import lax
from jax.experimental import pallas as pl
from jax.experimental.pallas import tpu as pltpu
from jax.sharding import PartitionSpec as P

HEADS = 4
HEAD = 128
MAXLEN = 256
WIDTH = 512
CAP = 8
LANES = 128

F32 = jnp.float32
BF16 = jnp.bfloat16
I32 = jnp.int32


def iota(shape, dim):
    return lax.broadcasted_iota(I32, shape, dim)


def one_hot(mask):
    return jnp.where(mask, 1.0, 0.0).astype(BF16)


def dot(a, b):
    return jnp.dot(a, b, preferred_element_type=F32)


def dot_nt(a, b):
    return lax.dot_general(a, b, (((1,), (1,)), ((), ())), preferred_element_type=F32)


def dot_tn(a, b):
    return lax.dot_general(a, b, (((0,), (0,)), ((), ())), preferred_element_type=F32)


def to_column(row):
    eye = iota((LANES, LANES), 0) == iota((LANES, LANES), 1)
    parts = []
    for start in range(0, row.shape[1], LANES):
        piece = row[:, start : start + LANES].astype(F32)
        parts.append(jnp.sum(jnp.where(eye, piece, 0.0), axis=1, keepdims=True))
    return jnp.concatenate(parts, axis=0).astype(I32)


def to_row(column):
    eye = iota((LANES, LANES), 0) == iota((LANES, LANES), 1)
    parts = []
    for start in range(0, column.shape[0], LANES):
        piece = column[start : start + LANES].astype(F32)
        parts.append(jnp.sum(jnp.where(eye, piece, 0.0), axis=0, keepdims=True))
    return jnp.concatenate(parts, axis=1).astype(I32)


def lane_sum(mask, values):
    return jnp.sum(jnp.where(mask, values, 0.0), axis=1, keepdims=True).astype(I32)


def flat_row(ref):
    return jnp.concatenate([ref[0:1, :], ref[1:2, :]], axis=1)


def request_kernel(owner_ref, item_ref, request_ref, slot_ref):
    devices = request_ref.shape[0]
    owner = jnp.concatenate([owner_ref[0], owner_ref[1]], axis=1)
    item = flat_row(item_ref)
    tokens = owner.shape[1]
    named = iota((devices, tokens), 0) == owner
    hot = one_hot(named)
    earlier = one_hot(iota((tokens, tokens), 0) < iota((tokens, tokens), 1))
    before = dot(hot, earlier)
    rank = jnp.sum(jnp.where(named, before, 0.0), axis=0, keepdims=True).astype(I32)
    place = iota((2 * CAP, tokens), 0)
    value = jnp.where(place < CAP, item >> 6, item & 63)
    table = jnp.where((place & (CAP - 1)) == rank, value, 0).astype(F32).astype(BF16)
    filled = dot_nt(hot, table).astype(I32)
    request_ref[...] = filled[:, :CAP] * 64 + filled[:, CAP:]
    slot = owner * CAP + rank
    half = tokens // 2
    slot_ref[0:1, :] = slot[:, :half]
    slot_ref[1:2, :] = slot[:, half:]


def class_kernel(owner_ref, item_ref, class_list_ref, class_ref):
    item = to_column(flat_row(item_ref))
    owner = jnp.concatenate([owner_ref[0], owner_ref[1]], axis=1)
    line = to_column(owner) * (4096 // LANES) + (item >> 7)
    tokens = line.shape[0]
    lines = class_list_ref.shape[0]
    step = 512
    total = jnp.zeros((tokens, LANES), F32)
    for start in range(0, lines, step):
        hot = one_hot(iota((tokens, step), 1) + start == line)
        total += dot(hot, class_list_ref[start : start + step, :].astype(F32).astype(BF16))
    class_ref[...] = lane_sum(iota((tokens, LANES), 1) == (item & 127), total)


def owner_kernel(
    asked_ref, class_ref, slab_ref, narrow_ref, middle_ref, wide_ref, reply_ref, code_ref,
    narrow_here, middle_here, wide_here, copied,
):
    copies = [
        pltpu.make_async_copy(there, here, copied.at[k])
        for k, (there, here) in enumerate(
            [(wide_ref, wide_here), (middle_ref, middle_here), (narrow_ref, narrow_here)]
        )
    ]
    for copy in copies:
        copy.start()
    asked = asked_ref[...]
    sources = asked.shape[0]
    amount = sources * CAP
    expand = one_hot((iota((amount, sources), 0) >> 3) == iota((amount, sources), 1))
    mine = (iota((amount, CAP), 0) & (CAP - 1)) == iota((amount, CAP), 1)
    high = lane_sum(mine, dot(expand, (asked >> 7).astype(F32).astype(BF16)))
    low = lane_sum(mine, dot(expand, (asked & 127).astype(F32).astype(BF16)))
    groups = slab_ref.shape[0]
    slab_list = slab_ref[...]
    marks = jnp.concatenate([slab_list & 127, (slab_list >> 7) + 16 * class_ref[...]], axis=1)
    found = dot(one_hot(iota((amount, groups), 1) == high), marks.astype(F32).astype(BF16))
    mine = iota((amount, LANES), 1) == low
    code_low = lane_sum(mine, found[:, :LANES])
    code_high = lane_sum(mine, found[:, LANES:])
    code = code_high * LANES + code_low
    code_ref[...] = code
    kind = code >> 11
    slab = code & 2047
    line = jnp.where(kind == 0, slab >> 1, slab)
    for copy in copies:
        copy.wait()
    step = 256
    lines = wide_ref.shape[0]
    packed_lines = narrow_ref.shape[0]
    for start in range(0, amount, step):
        rows = slice(start, start + step)
        hot = one_hot(iota((step, lines), 1) == line[rows])
        from_wide = dot(hot, wide_here[...])
        from_middle = dot(hot, middle_here[...])
        from_narrow = dot(hot[:, :packed_lines], narrow_here[...])
        from_narrow = jnp.where((slab[rows] & 1) == 1, pltpu.roll(from_narrow, 64, 1), from_narrow)
        from_narrow = jnp.where(iota((step, LANES), 1) < 64, from_narrow, 0.0)
        here = kind[rows]
        left = jnp.where(here == 2, from_wide[:, :LANES], jnp.where(here == 1, from_middle, from_narrow))
        right = jnp.where(here == 2, from_wide[:, LANES:], 0.0)
        reply_ref[rows, :] = jnp.concatenate([left, right], axis=1).astype(BF16)


def traded_slot(rank_ref, list_ref):
    rank = rank_ref[0]
    return jnp.where((list_ref[0, rank] >> 1) != rank, 0, 1)


def give_kernel(rank_ref, list_ref, cotangent_ref, given_ref, copied):
    copy = pltpu.make_async_copy(cotangent_ref.at[traded_slot(rank_ref, list_ref)], given_ref, copied)
    copy.start()
    copy.wait()


def mean(values):
    return jnp.sum(values, axis=1, keepdims=True) * (1.0 / WIDTH)


def normalize(values):
    centre = values - mean(values)
    scale = lax.rsqrt(mean(centre * centre) + 1e-06)
    return centre * scale, scale


def normalize_grad(grad, normed, scale):
    return scale * (grad - mean(grad) - normed * mean(grad * normed))


def sigmoid(values):
    return 0.5 * jnp.tanh(0.5 * values) + 0.5


def rounded(values):
    return values.astype(BF16).astype(F32)


def layer_kernel(
    rank_ref, list_ref, length_ref, slot_ref, landed_ref, class_ref, cotangent_ref, arrived_ref,
    narrow_lift_ref, middle_lift_ref, wide_lift_ref, joined_weight_ref, output_weight_ref,
    kept_ref, given_ref, payload_ref,
    lift_here, joined_here, output_here, cotangent_here, slope_ref, curve_ref, copied,
):
    rank = rank_ref[0]
    traded = traded_slot(rank_ref, list_ref)
    kept = 1 - traded
    moves = [
        (wide_lift_ref, lift_here.at[0:256]),
        (middle_lift_ref, lift_here.at[256:384]),
        (narrow_lift_ref, lift_here.at[384:448]),
        (joined_weight_ref, joined_here),
        (output_weight_ref, output_here),
        (cotangent_ref.at[kept], cotangent_here.at[kept]),
        (arrived_ref, cotangent_here.at[traded]),
    ]
    copies = [pltpu.make_async_copy(there, here, copied.at[k]) for k, (there, here) in enumerate(moves)]
    for copy in copies:
        copy.start()
    lift_here[448:, :] = jnp.zeros((64, WIDTH), BF16)
    zero = jnp.zeros((), BF16)
    rows = kept_ref.shape[0]
    hists = slot_ref.shape[0]
    tokens = hists * rows
    devices = payload_ref.shape[0]
    amount = devices * CAP
    slot = flat_row(slot_ref)
    raw = dot(one_hot(iota((tokens, amount), 1) == to_column(slot)), landed_ref[...]).astype(BF16)
    kind = class_ref[...]
    spread = jnp.concatenate(
        [
            jnp.where(kind == 2, raw, zero),
            jnp.where(kind == 1, raw[:, :LANES], zero),
            jnp.where(kind == 0, raw[:, :LANES], zero),
        ],
        axis=1,
    )
    for copy in copies[:3]:
        copy.wait()
    widened = rounded(dot(spread, lift_here[...]))
    normed, scale = normalize(widened)
    normed_low = normed.astype(BF16)
    copies[3].wait()
    joined = []
    for part in range(4):
        columns = slice(part * WIDTH, (part + 1) * WIDTH)
        before = dot(normed_low, joined_here[:, columns])
        gate = sigmoid(before)
        joined.append((before * gate).astype(BF16))
        slope_ref[:, columns] = gate * (1.0 + before * (1.0 - gate))
    gating, values, queries, keys = joined
    gating = gating.astype(F32)
    place = iota((tokens, 1), 0)
    lengths = [length_ref[hist, rank] for hist in range(hists)]
    valid = place < jnp.where(place < rows, lengths[0], rows + lengths[1])
    across = iota((rows, rows), 1)
    causal = across <= iota((rows, rows), 0)
    weights = {}
    mixed = []
    for hist in range(hists):
        lines = slice(hist * rows, (hist + 1) * rows)
        factor = jnp.where(causal & (across < lengths[hist]), 1.0 / MAXLEN, 0.0)
        heads = []
        for head in range(HEADS):
            columns = slice(head * HEAD, (head + 1) * HEAD)
            scores = dot_nt(queries[lines, columns], keys[lines, columns])
            gate = sigmoid(scores)
            scaled = gate * factor
            weights[hist, head] = (scores * scaled).astype(BF16)
            curve_ref[hist, head] = scaled * (1.0 + scores * (1.0 - gate))
            heads.append(dot(weights[hist, head], values[lines, columns]))
        mixed.append(jnp.concatenate(heads, axis=1))
    mixed_normed, mixed_scale = normalize(jnp.concatenate(mixed, axis=0))
    gated = (mixed_normed * gating).astype(BF16)
    for copy in copies[4:]:
        copy.wait()
    result = dot(gated, output_here[...]) + widened
    output = jnp.where(valid, result, 0.0).astype(BF16)
    kept_ref[...] = jnp.where(traded == 0, output[rows:], output[:rows])
    given_ref[...] = jnp.where(traded == 0, output[:rows], output[rows:])

    cotangent = jnp.concatenate([cotangent_here[0], cotangent_here[1]], axis=0)
    result_grad = jnp.where(valid, cotangent, zero)
    gated_grad = rounded(dot_nt(result_grad, output_here[...]))
    gating_grad = (gated_grad * mixed_normed).astype(BF16)
    mixed_grad = normalize_grad(gated_grad * gating, mixed_normed, mixed_scale).astype(BF16)
    grads = [[], [], []]
    for hist in range(hists):
        lines = slice(hist * rows, (hist + 1) * rows)
        heads = [[], [], []]
        for head in range(HEADS):
            columns = slice(head * HEAD, (head + 1) * HEAD)
            own = mixed_grad[lines, columns]
            weights_grad = rounded(dot_nt(own, values[lines, columns]))
            scores_grad = (weights_grad * curve_ref[hist, head]).astype(BF16)
            heads[0].append(dot_tn(weights[hist, head], own))
            heads[1].append(dot(scores_grad, keys[lines, columns]))
            heads[2].append(dot_tn(scores_grad, queries[lines, columns]))
        for part in range(3):
            grads[part].append(jnp.concatenate(heads[part], axis=1).astype(BF16))
    joined_grad = [gating_grad] + [jnp.concatenate(g, axis=0) for g in grads]
    normed_grad = jnp.zeros((tokens, WIDTH), F32)
    for part in range(4):
        columns = slice(part * WIDTH, (part + 1) * WIDTH)
        before_grad = (joined_grad[part].astype(F32) * slope_ref[:, columns]).astype(BF16)
        normed_grad += dot_nt(before_grad, joined_here[:, columns])
    grad = normalize_grad(rounded(normed_grad), normed, scale) + result_grad.astype(F32)
    grad = grad.astype(BF16)
    spread_grad = dot_nt(grad, lift_here[...])
    narrow_part = jnp.where(iota((tokens, LANES), 1) < 64, spread_grad[:, 384:], 0.0)
    left = jnp.where(
        kind == 2, spread_grad[:, :LANES], jnp.where(kind == 1, spread_grad[:, 256:384], narrow_part)
    )
    right = jnp.where(kind == 2, spread_grad[:, LANES:256], 0.0)
    row_grad = jnp.concatenate([left, right], axis=1).astype(BF16)
    term = dot_tn(spread, grad).reshape(devices // 2, CAP, WIDTH)
    term = jnp.stack([term[:, :, :256], term[:, :, 256:]], axis=1).reshape(devices, CAP, 256)
    placed = dot(one_hot(iota((amount, tokens), 0) == slot), row_grad).reshape(devices, CAP, 256)
    payload_ref[...] = jnp.concatenate([placed, term], axis=1).astype(BF16)


def sum_kernel(landed_ref, share_ref):
    total = jnp.sum(landed_ref[...].astype(F32), axis=0)[CAP:]
    share_ref[...] = jnp.broadcast_to(total[None].astype(BF16), share_ref.shape)


def scatter_kernel(landed_ref, code_ref, narrow_ref, middle_ref, wide_ref):
    sources = landed_ref.shape[0]
    amount = sources * CAP
    grads = landed_ref[...].astype(F32)[:, :CAP, :].reshape(amount, 256)
    code = code_ref[...]
    kind = code >> 11
    slab = code & 2047
    line = to_row(jnp.where(kind == 0, slab >> 1, slab))
    wide = jnp.where(kind == 2, grads, 0.0).astype(BF16)
    middle = jnp.where(kind == 1, grads[:, :LANES], 0.0).astype(BF16)
    narrow = jnp.where((kind == 0) & (iota((amount, LANES), 1) < 64), grads[:, :LANES], 0.0)
    narrow = jnp.where((slab & 1) == 1, pltpu.roll(narrow, 64, 1), narrow).astype(BF16)
    step = 256
    for start in range(0, wide_ref.shape[0], step):
        hot = one_hot(iota((step, amount), 0) + start == line)
        wide_ref[start : start + step, :] = dot(hot, wide)
        middle_ref[start : start + step, :] = dot(hot, middle)
        if start < narrow_ref.shape[0]:
            narrow_ref[start : start + step, :] = dot(hot, narrow)


def place_kernel(rank_ref, list_ref, kept_ref, arrived_ref, output_ref):
    traded = traded_slot(rank_ref, list_ref)
    output_ref[1 - traded] = kept_ref[...]
    output_ref[traded] = arrived_ref[...]


def delta_kernel(shares_ref, narrow_ref, middle_ref, wide_ref):
    devices = shares_ref.shape[0]
    shares = shares_ref[...].astype(F32).reshape(devices // 2, 2, CAP, 256)
    for half in range(2):
        columns = slice(half * 256, (half + 1) * 256)
        whole = shares[:, half].reshape(devices // 2 * CAP, 256)
        wide_ref[:, columns] = whole[:256]
        middle_ref[:, columns] = whole[256:384]
        narrow_ref[:, columns] = whole[384:448]


SMEM = pl.BlockSpec(memory_space=pltpu.SMEM)
VMEM = pl.BlockSpec(memory_space=pltpu.VMEM)
HBM = pl.BlockSpec(memory_space=pltpu.HBM)


def call(kernel, outs, args, scratch=(), flops=0, limit=32):
    shapes = [jax.ShapeDtypeStruct(shape, dtype) for shape, dtype in outs]
    arrays = [array for _, array in args]
    moved = sum(a.size * a.dtype.itemsize for a in arrays + shapes)
    return pl.pallas_call(
        kernel,
        out_shape=shapes,
        in_specs=[space for space, _ in args],
        out_specs=[VMEM] * len(shapes),
        scratch_shapes=list(scratch),
        cost_estimate=pl.CostEstimate(flops=flops, bytes_accessed=moved, transcendentals=0),
        compiler_params=pltpu.CompilerParams(vmem_limit_bytes=limit << 20),
    )(*arrays)


def exchange(array):
    return lax.all_to_all(array, ("dp", "table"), split_axis=0, concat_axis=0, tiled=True)


def body(
    history_lengths,
    balance_list,
    owner_device,
    owner_row,
    width_class,
    slab_index,
    narrow_table,
    middle_table,
    wide_table,
    narrow_lift,
    middle_lift,
    wide_lift,
    joined_weight,
    output_weight,
    cotangent,
):
    data_size = lax.axis_size("dp")
    table_size = lax.axis_size("table")
    devices = data_size * table_size
    rows = cotangent.shape[1]
    items = slab_index.shape[0]
    amount = devices * CAP
    data_rank = lax.axis_index("dp")
    self_rank = data_rank * table_size + lax.axis_index("table")
    rank = (SMEM, data_rank.reshape(1).astype(I32))
    plan = (SMEM, balance_list.T)
    owner = owner_device.transpose(0, 2, 1)
    class_list = width_class.reshape(-1, LANES)
    partners = [(i, i ^ (data_size // 2)) for i in range(data_size)]

    requests, slots = call(
        request_kernel,
        [((devices, CAP), I32), (owner_row.shape, I32)],
        [(VMEM, owner), (VMEM, owner_row)],
        flops=10**8,
    )
    asked = exchange(requests)
    (kinds,) = call(
        class_kernel,
        [((2 * rows, 1), I32)],
        [(VMEM, owner), (VMEM, owner_row), (VMEM, class_list)],
        flops=10**9,
    )
    (given_cotangent,) = call(
        give_kernel,
        [((rows, WIDTH), BF16)],
        [rank, plan, (HBM, cotangent)],
        scratch=[pltpu.SemaphoreType.DMA],
    )
    arrived_cotangent = lax.ppermute(given_cotangent, "dp", partners)
    own_classes = lax.dynamic_slice(class_list, (self_rank * (items // LANES), 0), (items // LANES, LANES))
    replies, codes = call(
        owner_kernel,
        [((amount, 256), BF16), ((amount, 1), I32)],
        [
            (VMEM, asked), (VMEM, own_classes), (VMEM, slab_index.reshape(-1, LANES)),
            (HBM, narrow_table), (HBM, middle_table), (HBM, wide_table),
        ],
        scratch=[
            pltpu.VMEM(narrow_table.shape, BF16),
            pltpu.VMEM(middle_table.shape, BF16),
            pltpu.VMEM(wide_table.shape, BF16),
            pltpu.SemaphoreType.DMA((3,)),
        ],
        flops=3 * 10**9,
    )
    landed = exchange(replies)
    kept_output, given_output, payload = call(
        layer_kernel,
        [((rows, WIDTH), BF16), ((rows, WIDTH), BF16), ((devices, 2 * CAP, 256), BF16)],
        [
            rank, plan, (SMEM, history_lengths.T), (VMEM, slots), (VMEM, landed), (VMEM, kinds),
            (HBM, cotangent), (HBM, arrived_cotangent), (HBM, narrow_lift), (HBM, middle_lift),
            (HBM, wide_lift), (HBM, joined_weight), (HBM, output_weight),
        ],
        scratch=[
            pltpu.VMEM((WIDTH, WIDTH), BF16),
            pltpu.VMEM((WIDTH, 4 * WIDTH), BF16),
            pltpu.VMEM((WIDTH, WIDTH), BF16),
            pltpu.VMEM((2, rows, WIDTH), BF16),
            pltpu.VMEM((2 * rows, 4 * WIDTH), F32),
            pltpu.VMEM((2, HEADS, rows, rows), F32),
            pltpu.SemaphoreType.DMA((7,)),
        ],
        flops=10**10,
        limit=40,
    )
    home = exchange(payload)
    (share,) = call(sum_kernel, [((devices, CAP, 256), BF16)], [(VMEM, home)])
    shares = exchange(share)
    given_output, _ = lax.optimization_barrier((given_output, share))
    arrived_output = lax.ppermute(given_output, "dp", partners)
    narrow_grad, middle_grad, wide_grad = call(
        scatter_kernel,
        [(narrow_table.shape, F32), (middle_table.shape, F32), (wide_table.shape, F32)],
        [(VMEM, home), (VMEM, codes)],
        flops=3 * 10**9,
    )
    (output,) = call(
        place_kernel, [(cotangent.shape, BF16)], [rank, plan, (VMEM, kept_output), (VMEM, arrived_output)]
    )
    narrow_delta, middle_delta, wide_delta = call(
        delta_kernel,
        [(narrow_lift.shape, F32), (middle_lift.shape, F32), (wide_lift.shape, F32)],
        [(VMEM, shares)],
    )
    return (output, narrow_grad, middle_grad, wide_grad, narrow_delta, middle_delta, wide_delta)


def solution(mesh):
    in_specs = (
        P(None, "table"),
        P(None, "table"),
        P(("dp", "table"), None, None),
        P(("dp", "table"), None),
        P(),
        P(("dp", "table")),
        P(("dp", "table"), None),
        P(("dp", "table"), None),
        P(("dp", "table"), None),
        P(),
        P(),
        P(),
        P(),
        P(),
        P(("dp", "table"), None, None),
    )
    out_specs = (
        P(("dp", "table"), None, None),
        P(("dp", "table"), None),
        P(("dp", "table"), None),
        P(("dp", "table"), None),
        P(),
        P(),
        P(),
    )
    return jax.shard_map(body, mesh=mesh, in_specs=in_specs, out_specs=out_specs, check_vma=False)
```

time: 122 us -> 116 us (0.951)
  waiting for transfers between devices: 30 us -> 23.1 us
  starting transfers between devices: 24.2 us -> 28.2 us
  Pallas kernels: 28.9 us -> 27.5 us
    all_to_all x3, waiting for transfers between devices: 26.8 us -> 8.77 us  [exchange(): lax.all_to_all(array, ('dp', 'table'), split_axis=0, concat_axis=0, tiled...]
    ppermute x2, waiting for transfers between devices: 3.23 us -> 14.3 us  [the longest x1 8.01 us: body(): arrived_cotangent = lax.ppermute(given_cotangent, 'dp', partners)]
    ppermute x2, starting transfers between devices: 3.31 us -> 7.31 us  [the longest x1 3.72 us: body(): arrived_output = lax.ppermute(given_output, 'dp', partners)]
    pallas_call x10 -> x9, Pallas kernels: 28.9 us -> 27.5 us  [call(): pl.pallas_call(kernel, out_shape=shapes, in_specs=[space for space, _ in...]
    unnamed x39 -> x38, local copies, waits for them, and re-layouts: 9.88 us -> 9.3 us
  transfers between devices with their start and end apart: 5 -> 5, of which waited for: 4 -> 3; matrix products, arithmetic and copies ran while one was open for 2% -> 1% of each run, Pallas kernels for 10% -> 8%
where the time goes in v2:
time: 116 us; the launch traced here: 115 us
  starting transfers between devices  28.2 us (24%)
  Pallas kernels  27.5 us (24%)
  blocking collectives  25.3 us (22%)
  waiting for transfers between devices  23.1 us (20%)
  local copies, waits for them, and re-layouts  10 us (9%)
    pallas_call x9, Pallas kernels, call(): pl.pallas_call(kernel, out_shape=shapes, in_specs=[space for space, _ in...  27.5 us
    all_to_all x1, blocking collectives, exchange(): lax.all_to_all(array, ('dp', 'table'), split_axis=0, concat_axis=0, tiled...  25.3 us
    all_to_all x3, starting transfers between devices, exchange(): lax.all_to_all(array, ('dp', 'table'), split_axis=0, concat_axis=0, tiled...  20.9 us
    unnamed x38, local copies, waits for them, and re-layouts  9.3 us
    all_to_all x3, waiting for transfers between devices, exchange(): lax.all_to_all(array, ('dp', 'table'), split_axis=0, concat_axis=0, tiled...  8.77 us
    ppermute x1, waiting for transfers between devices, body(): arrived_cotangent = lax.ppermute(given_cotangent, 'dp', partners)  8.01 us
    ppermute x1, waiting for transfers between devices, body(): arrived_output = lax.ppermute(given_output, 'dp', partners)  6.32 us
    ppermute x1, starting transfers between devices, body(): arrived_output = lax.ppermute(given_output, 'dp', partners)  3.72 us
  transfers between devices with their start and end apart: 5, of which 3 were waited for; matrix products, arithmetic and copies ran while one was open for 1% of the time, Pallas kernels for 8%

profile of v2, /device:TPU:1, one launch (start us, length us, event | category | flops | bytes accessed | tf_op | source)
XLA Modules:
  0.0 115.0 jit_solution(7877985111921412595)
XLA Ops:
  2.0 1.1 shard_map.198
  3.1 11.5 %all-to-all-start = ((s32[128,1,8]{2,1,0:T(1,128)}), s32[128,1,8]{2,1,0:T(1,128)S(1)}, u32[]{:S(2)}, u32[]{:S(2)}) async-start(s32[128,1,8]{2,1,0:T(1,128)} %bitcast.5), calls=%async_computation | async-start | bytes 131072 | tf_op jit(solution)/shard_map/all_to_all | solution.py:371
  14.6 0.7 constant_dynamic-slice_fusion.class_ref
  15.4 8.8 %all-to-all-done = s32[128,1,8]{2,1,0:T(1,128)S(1)} async-done(((s32[128,1,8]{2,1,0:T(1,128)}), s32[128,1,8]{2,1,0:T(1,128)S(1)}, u32[]{:S(2)}, u32[]{:S(2)}) %all-to-all-start) | async-done | bytes 4128 | tf_op jit(solution)/shard_map/all_to_all | solution.py:371
  24.1 1.2 %copy-done.4 = bf16[2048,256]{1,0:T(8,128)(2,1)S(1)} copy-done((bf16[2048,256]{1,0:T(8,128)(2,1)S(1)}, bf16[2048,256]{1,0:T(8,128)(2,1)}, u32[]{:S(2)}) %copy-start.4) | copy-done | bytes 1048600
  25.3 1.0 copy-done.5
  26.4 0.9 copy-done.7
  28.1 4.9 %shard_map.199 = (bf16[1024,256]{1,0:T(8,128)(2,1)}, s32[1024,1]{1,0:T(8,128)S(1)}) custom-call(s32[128,8]{1,0:T(8,128)S(1)} %bitcast.13, s32[32,128]{1,0:T(8,128)S(1)} %constant_dynamic-slice_fusion.class_ref, s32[32,128]{1,0:T(8,128)S(1)} %bitcast.19, bf16[1024,128]{1,0:T(8,128)(2,1)S(1)} %copy-done.7, bf16[2048,128]{1,0:T(8,128)(2,1)S(1)} %copy-done.5, ...), custom_call_target="tpu_custom_call" | custom-call | flops 3000000000 | bytes 2400256 | tf_op jit(solution)/shard_map/pallas_call | solution.py:359
  33.0 0.8 copy-done.17
  33.8 4.5 %all-to-all-start.1 = ((bf16[128,8,256]{2,1,0:T(8,128)(2,1)}), bf16[128,8,256]{2,1,0:T(8,128)(2,1)S(1)}, u32[]{:S(2)}, u32[]{:S(2)}) async-start(bf16[128,8,256]{2,1,0:T(8,128)(2,1)} %bitcast.9), calls=%async_computation.1 | async-start | bytes 1048576 | tf_op jit(solution)/shard_map/all_to_all | solution.py:371
  38.9 3.6 %collective-permute-start = (bf16[256,512]{1,0:T(8,128)(2,1)S(1)}, bf16[256,512]{1,0:T(8,128)(2,1)S(1)}, u32[]{:S(2)}, u32[]{:S(2)}) collective-permute-start(bf16[256,512]{1,0:T(8,128)(2,1)S(1)} %shard_map.201), channel_id=1, source_target_pairs={{0,64},{16,80},{32,96},{48,112},{64,0},{80,16},{96,32},{112,48},{1... | collective-permute-start | bytes 786440 | tf_op jit(solution)/shard_map/ppermute | solution.py:424
  42.5 1.6 %copy-done.2 = s32[524288]{0:T(1024)S(1)} copy-done((s32[524288]{0:T(1024)S(1)}, s32[524288]{0:T(1024)}, u32[]{:S(2)}) %copy-start.2) | copy-done | bytes 2097176
  44.1 1.6 %shard_map.200.class_ref = s32[512,1]{1,0:T(8,128)S(1)} custom-call(s32[2,1,256]{2,1,0:T(1,128)S(1)} %bitcast.21, s32[2,256]{1,0:T(2,128)S(1)} %copy-done.15, s32[4096,128]{1,0:T(8,128)S(1)} %bitcast.18), custom_call_target="tpu_custom_call" | custom-call | flops 1000000000 | bytes 2103296 | tf_op jit(solution)/shard_map/pallas_call | solution.py:359
  45.7 8.0 %collective-permute-done.arrived_ref = bf16[256,512]{1,0:T(8,128)(2,1)S(1)} collective-permute-done((bf16[256,512]{1,0:T(8,128)(2,1)S(1)}, bf16[256,512]{1,0:T(8,128)(2,1)S(1)}, u32[]{:S(2)}, u32[]{:S(2)}) %collective-permute-start) | collective-permute-done | bytes 262176 | tf_op jit(solution)/shard_map/ppermute | solution.py:424
  53.8 1.6 %copy-done.3 = bf16[512,2048]{1,0:T(8,128)(2,1)S(1)} copy-done((bf16[512,2048]{1,0:T(8,128)(2,1)S(1)}, bf16[512,2048]{1,0:T(8,128)(2,1)}, u32[]{:S(2)}) %copy-start.3) | copy-done | bytes 2097176
  55.4 10.9 %shard_map.202 = (bf16[256,512]{1,0:T(8,128)(2,1)S(1)}, bf16[256,512]{1,0:T(8,128)(2,1)S(1)}, bf16[128,16,256]{2,1,0:T(8,128)(2,1)S(1)}) custom-call(s32[1]{0:T(128)} %bitcast.rank_ref, s32[2,8]{1,0:T(2,128)S(1)} %bitcast.15, s32[2,8]{1,0:T(2,128)S(1)} %bitcast.22, s32[2,256]{1,0:T(2,128)S(1)} %get-tuple-element.21.slot_ref, bf16[1024,256]{1,0:T(8,128)(2,1)S(1)} %bitcast.12, ...), custom_call_target="tpu_custom_call" | custom-call | flops 10000000000 | bytes 5968004 | tf_op jit(solution)/shard_map/pallas_call | solution.py:359
  66.3 25.3 %all_to_all.32.landed_ref = bf16[128,16,256]{2,1,0:T(8,128)(2,1)S(1)} all-to-all(bf16[128,16,256]{2,1,0:T(8,128)(2,1)S(1)} %get-tuple-element.26), channel_id=1, replica_groups=mesh['dp'=8,'table'=16] {'dp','table'}, dimensions={0} | all-to-all | bytes 2097152 | tf_op jit(solution)/shard_map/all_to_all | solution.py:371
  91.6 1.0 shard_map.203
  92.6 4.9 %all-to-all-start.3 = ((bf16[128,8,256]{2,1,0:T(8,128)(2,1)}), bf16[128,8,256]{2,1,0:T(8,128)(2,1)S(1)}, u32[]{:S(2)}, u32[]{:S(2)}) async-start(bf16[128,8,256]{2,1,0:T(8,128)(2,1)} %shard_map.203), calls=%async_computation.3 | async-start | bytes 1048576 | tf_op jit(solution)/shard_map/all_to_all | solution.py:371
  97.5 3.7 %collective-permute-start.1 = (bf16[256,512]{1,0:T(8,128)(2,1)S(1)}, bf16[256,512]{1,0:T(8,128)(2,1)S(1)}, u32[]{:S(2)}, u32[]{:S(2)}) collective-permute-start(bf16[256,512]{1,0:T(8,128)(2,1)S(1)} %get-tuple-element.27), channel_id=1, source_target_pairs={{0,64},{16,80},{32,96},{48,112},{64,0},{80,16},{96,32},{112,48},{1... | collective-permute-start | bytes 786440 | tf_op jit(solution)/shard_map/ppermute | solution.py:466
  101.2 5.1 %shard_map.205 = (f32[1024,128]{1,0:T(8,128)}, f32[2048,128]{1,0:T(8,128)}, f32[2048,256]{1,0:T(8,128)}) custom-call(bf16[128,16,256]{2,1,0:T(8,128)(2,1)S(1)} %all_to_all.32.landed_ref, s32[1024,1]{1,0:T(8,128)S(1)} %copy-done.18), custom_call_target="tpu_custom_call" | custom-call | flops 3000000000 | bytes 4722688 | tf_op jit(solution)/shard_map/pallas_call | solution.py:359
  106.3 6.3 %collective-permute-done.1.arrived_ref = bf16[256,512]{1,0:T(8,128)(2,1)S(1)} collective-permute-done((bf16[256,512]{1,0:T(8,128)(2,1)S(1)}, bf16[256,512]{1,0:T(8,128)(2,1)S(1)}, u32[]{:S(2)}, u32[]{:S(2)}) %collective-permute-start.1) | collective-permute-done | bytes 262176 | tf_op jit(solution)/shard_map/ppermute | solution.py:466
  112.6 1.4 %shard_map.204 = bf16[2,256,512]{2,1,0:T(8,128)(2,1)} custom-call(s32[1]{0:T(128)} %bitcast.rank_ref, s32[2,8]{1,0:T(2,128)S(1)} %bitcast.16, bf16[256,512]{1,0:T(8,128)(2,1)S(1)} %get-tuple-element.24.kept_ref, bf16[256,512]{1,0:T(8,128)(2,1)S(1)} %collective-permute-done.1.arrived_ref), custom_call_target="tpu_custom_call" | custom-call | bytes 1048644 | tf_op jit(solution)/shard_map/pallas_call | solution.py:359
  114.0 1.0 shard_map.206
  (35 shorter events, 2.7 us)
Async XLA Ops:
  0.6 0.7 copy-start.12
  1.3 0.7 copy-start.14
  3.1 21.0 %all-to-all-start = ((s32[128,1,8]{2,1,0:T(1,128)}), s32[128,1,8]{2,1,0:T(1,128)S(1)}, u32[]{:S(2)}, u32[]{:S(2)}) async-start(s32[128,1,8]{2,1,0:T(1,128)} %bitcast.5), calls=%async_computation | async-start | bytes 131072 | tf_op jit(solution)/shard_map/all_to_all | solution.py:371
  24.1 1.2 %copy-start.4 = (bf16[2048,256]{1,0:T(8,128)(2,1)S(1)}, bf16[2048,256]{1,0:T(8,128)(2,1)}, u32[]{:S(2)}) copy-start(bf16[2048,256]{1,0:T(8,128)(2,1)} %wide_ref.1) | copy-start | bytes 3145732
  25.3 1.0 copy-start.5
  26.4 0.9 copy-start.7
  27.3 0.7 copy-start.11
  28.1 10.2 %copy-start = (bf16[2,256,512]{2,1,0:T(8,128)(2,1)S(1)}, bf16[2,256,512]{2,1,0:T(8,128)(2,1)}, u32[]{:S(2)}) copy-start(bf16[2,256,512]{2,1,0:T(8,128)(2,1)} %cotangent_ref.3) | copy-start | bytes 1572868
  28.1 10.2 %copy-start.1 = (s32[8,2]{0,1:T(2,128)S(1)}, s32[8,2]{0,1:T(2,128)}, u32[]{:S(2)}) copy-start(s32[8,2]{0,1:T(2,128)} %param.16) | copy-start | bytes 196
  28.1 14.5 %copy-start.13 = (s32[2,256,1]{1,2,0:T(1,128)S(1)}, s32[2,256,1]{1,2,0:T(1,128)}, u32[]{:S(2)}) copy-start(s32[2,256,1]{1,2,0:T(1,128)} %param.17) | copy-start | bytes 6148
  28.1 14.5 %copy-start.15 = (s32[2,256]{1,0:T(2,128)S(1)}, s32[2,256]{1,0:T(2,128)}, u32[]{:S(2)}) copy-start(s32[2,256]{1,0:T(2,128)} %item_ref.3) | copy-start | bytes 6148
  33.0 0.8 copy-start.17
  33.8 20.0 %all-to-all-start.1 = ((bf16[128,8,256]{2,1,0:T(8,128)(2,1)}), bf16[128,8,256]{2,1,0:T(8,128)(2,1)S(1)}, u32[]{:S(2)}, u32[]{:S(2)}) async-start(bf16[128,8,256]{2,1,0:T(8,128)(2,1)} %bitcast.9), calls=%async_computation.1 | async-start | bytes 1048576 | tf_op jit(solution)/shard_map/all_to_all | solution.py:371
  38.3 15.5 %copy-start.6 = (bf16[512,512]{1,0:T(8,128)(2,1)S(1)}, bf16[512,512]{1,0:T(8,128)(2,1)}, u32[]{:S(2)}) copy-start(bf16[512,512]{1,0:T(8,128)(2,1)} %output_weight_ref.1) | copy-start | bytes 1572868
  38.3 15.5 %copy-start.8 = (bf16[256,512]{1,0:T(8,128)(2,1)S(1)}, bf16[256,512]{1,0:T(8,128)(2,1)}, u32[]{:S(2)}) copy-start(bf16[256,512]{1,0:T(8,128)(2,1)} %wide_lift_ref.1) | copy-start | bytes 786436
  38.3 15.4 %copy-start.16 = (s32[8,2]{0,1:T(2,128)S(1)}, s32[8,2]{0,1:T(2,128)}, u32[]{:S(2)}) copy-start(s32[8,2]{0,1:T(2,128)} %param.15) | copy-start | bytes 196
  38.9 14.8 %collective-permute-start = (bf16[256,512]{1,0:T(8,128)(2,1)S(1)}, bf16[256,512]{1,0:T(8,128)(2,1)S(1)}, u32[]{:S(2)}, u32[]{:S(2)}) collective-permute-start(bf16[256,512]{1,0:T(8,128)(2,1)S(1)} %shard_map.201), channel_id=1, source_target_pairs={{0,64},{16,80},{32,96},{48,112},{64,0},{80,16},{96,32},{112,48},{1... | collective-permute-start | bytes 786440 | tf_op jit(solution)/shard_map/ppermute | solution.py:424
  42.5 1.6 %copy-start.2 = (s32[524288]{0:T(1024)S(1)}, s32[524288]{0:T(1024)}, u32[]{:S(2)}) copy-start(s32[524288]{0:T(1024)} %param.19) | copy-start | bytes 6291460
  44.1 9.7 %copy-start.9 = (bf16[128,512]{1,0:T(8,128)(2,1)S(1)}, bf16[128,512]{1,0:T(8,128)(2,1)}, u32[]{:S(2)}) copy-start(bf16[128,512]{1,0:T(8,128)(2,1)} %middle_lift_ref.1) | copy-start | bytes 393220
  44.1 9.7 %copy-start.10 = (bf16[64,512]{1,0:T(8,128)(2,1)S(1)}, bf16[64,512]{1,0:T(8,128)(2,1)}, u32[]{:S(2)}) copy-start(bf16[64,512]{1,0:T(8,128)(2,1)} %narrow_lift_ref.1) | copy-start | bytes 196612
  53.8 1.6 %copy-start.3 = (bf16[512,2048]{1,0:T(8,128)(2,1)S(1)}, bf16[512,2048]{1,0:T(8,128)(2,1)}, u32[]{:S(2)}) copy-start(bf16[512,2048]{1,0:T(8,128)(2,1)} %joined_weight_ref.1) | copy-start | bytes 6291460
  66.3 34.9 %copy-start.18 = (s32[1024,1]{1,0:T(8,128)S(1)}, s32[1024,1]{1,0:T(8,128)}, u32[]{:S(2)}) copy-start(s32[1024,1]{1,0:T(8,128)} %copy-done.17) | copy-start | bytes 12292
  92.6 21.4 %all-to-all-start.3 = ((bf16[128,8,256]{2,1,0:T(8,128)(2,1)}), bf16[128,8,256]{2,1,0:T(8,128)(2,1)S(1)}, u32[]{:S(2)}, u32[]{:S(2)}) async-start(bf16[128,8,256]{2,1,0:T(8,128)(2,1)} %shard_map.203), calls=%async_computation.3 | async-start | bytes 1048576 | tf_op jit(solution)/shard_map/all_to_all | solution.py:371
  97.5 15.1 %collective-permute-start.1 = (bf16[256,512]{1,0:T(8,128)(2,1)S(1)}, bf16[256,512]{1,0:T(8,128)(2,1)S(1)}, u32[]{:S(2)}, u32[]{:S(2)}) collective-permute-start(bf16[256,512]{1,0:T(8,128)(2,1)S(1)} %get-tuple-element.27), channel_id=1, source_target_pairs={{0,64},{16,80},{32,96},{48,112},{64,0},{80,16},{96,32},{112,48},{1... | collective-permute-start | bytes 786440 | tf_op jit(solution)/shard_map/ppermute | solution.py:466

commit v3 on v2

--- a/solution.py
+++ b/solution.py
@@ -11,6 +11,8 @@
 WIDTH = 512
 CAP = 8
 LANES = 128
+OWNER_STEP = 256
+LIMIT = 32
 
 F32 = jnp.float32
 BF16 = jnp.bfloat16
@@ -84,7 +86,9 @@
     slot_ref[1:2, :] = slot[:, half:]
 
 
-def class_kernel(owner_ref, item_ref, class_list_ref, class_ref):
+def class_kernel(owner_ref, item_ref, class_list_ref, class_ref, list_here, copied):
+    copy = pltpu.make_async_copy(class_list_ref, list_here, copied)
+    copy.start()
     item = to_column(flat_row(item_ref))
     owner = jnp.concatenate([owner_ref[0], owner_ref[1]], axis=1)
     line = to_column(owner) * (4096 // LANES) + (item >> 7)
@@ -92,24 +96,16 @@
     lines = class_list_ref.shape[0]
     step = 512
     total = jnp.zeros((tokens, LANES), F32)
+    copy.wait()
     for start in range(0, lines, step):
         hot = one_hot(iota((tokens, step), 1) + start == line)
-        total += dot(hot, class_list_ref[start : start + step, :].astype(F32).astype(BF16))
-    class_ref[...] = lane_sum(iota((tokens, LANES), 1) == (item & 127), total)
-
-
-def owner_kernel(
-    asked_ref, class_ref, slab_ref, narrow_ref, middle_ref, wide_ref, reply_ref, code_ref,
-    narrow_here, middle_here, wide_here, copied,
-):
-    copies = [
-        pltpu.make_async_copy(there, here, copied.at[k])
-        for k, (there, here) in enumerate(
-            [(wide_ref, wide_here), (middle_ref, middle_here), (narrow_ref, narrow_here)]
-        )
-    ]
-    for copy in copies:
-        copy.start()
+        total += dot(hot, list_here[start : start + step, :].astype(F32).astype(BF16))
+    kind = to_row(lane_sum(iota((tokens, LANES), 1) == (item & 127), total))
+    class_ref[0:1, :] = kind[:, : tokens // 2]
+    class_ref[1:2, :] = kind[:, tokens // 2 :]
+
+
+def request_codes(asked_ref, marks):
     asked = asked_ref[...]
     sources = asked.shape[0]
     amount = sources * CAP
@@ -117,34 +113,55 @@
     mine = (iota((amount, CAP), 0) & (CAP - 1)) == iota((amount, CAP), 1)
     high = lane_sum(mine, dot(expand, (asked >> 7).astype(F32).astype(BF16)))
     low = lane_sum(mine, dot(expand, (asked & 127).astype(F32).astype(BF16)))
-    groups = slab_ref.shape[0]
-    slab_list = slab_ref[...]
-    marks = jnp.concatenate([slab_list & 127, (slab_list >> 7) + 16 * class_ref[...]], axis=1)
-    found = dot(one_hot(iota((amount, groups), 1) == high), marks.astype(F32).astype(BF16))
+    found = dot(one_hot(iota((amount, marks.shape[0]), 1) == high), marks)
     mine = iota((amount, LANES), 1) == low
-    code_low = lane_sum(mine, found[:, :LANES])
-    code_high = lane_sum(mine, found[:, LANES:])
-    code = code_high * LANES + code_low
-    code_ref[...] = code
+    return lane_sum(mine, found[:, LANES:]) * LANES + lane_sum(mine, found[:, :LANES])
+
+
+def stage_rows_kernel(
+    rank_ref, after_ref, class_list_ref, slab_ref, narrow_ref, middle_ref, wide_ref, table_ref, marks_ref,
+    class_here, slab_here, copied,
+):
+    del after_ref
+    groups = slab_here.shape[0]
+    lines = narrow_ref.shape[0]
+    moves = [
+        (class_list_ref.at[pl.ds(pl.multiple_of(rank_ref[1] * groups, groups), groups)], class_here),
+        (slab_ref, slab_here),
+        (wide_ref, table_ref.at[:, 0:256]),
+        (middle_ref, table_ref.at[:, 256:384]),
+        (narrow_ref, table_ref.at[0:lines, 384:512]),
+    ]
+    copies = [pltpu.make_async_copy(there, here, copied.at[k]) for k, (there, here) in enumerate(moves)]
+    for copy in copies:
+        copy.start()
+    table_ref[lines:, 384:] = jnp.zeros((table_ref.shape[0] - lines, LANES), BF16)
+    for copy in copies:
+        copy.wait()
+    slab = slab_here[...]
+    marks = jnp.concatenate([slab & 127, (slab >> 7) + 16 * class_here[...]], axis=1)
+    marks_ref[...] = marks.astype(F32).astype(BF16)
+
+
+def owner_kernel(asked_ref, marks_ref, table_ref, reply_ref):
+    amount = reply_ref.shape[0]
+    code = request_codes(asked_ref, marks_ref[...])
     kind = code >> 11
     slab = code & 2047
     line = jnp.where(kind == 0, slab >> 1, slab)
-    for copy in copies:
-        copy.wait()
-    step = 256
-    lines = wide_ref.shape[0]
-    packed_lines = narrow_ref.shape[0]
-    for start in range(0, amount, step):
-        rows = slice(start, start + step)
-        hot = one_hot(iota((step, lines), 1) == line[rows])
-        from_wide = dot(hot, wide_here[...])
-        from_middle = dot(hot, middle_here[...])
-        from_narrow = dot(hot[:, :packed_lines], narrow_here[...])
-        from_narrow = jnp.where((slab[rows] & 1) == 1, pltpu.roll(from_narrow, 64, 1), from_narrow)
-        from_narrow = jnp.where(iota((step, LANES), 1) < 64, from_narrow, 0.0)
+    lines = table_ref.shape[0]
+    for start in range(0, amount, OWNER_STEP):
+        rows = slice(start, start + OWNER_STEP)
+        hot = one_hot(iota((OWNER_STEP, lines), 1) == line[rows])
         here = kind[rows]
-        left = jnp.where(here == 2, from_wide[:, :LANES], jnp.where(here == 1, from_middle, from_narrow))
-        right = jnp.where(here == 2, from_wide[:, LANES:], 0.0)
+        side = dot(hot, table_ref[:, 256:])
+        narrow = side[:, LANES:]
+        narrow = jnp.where((slab[rows] & 1) == 1, pltpu.roll(narrow, 64, 1), narrow)
+        narrow = jnp.where(iota((OWNER_STEP, LANES), 1) < 64, narrow, 0.0)
+        side = jnp.where(here == 1, side[:, :LANES], narrow)
+        wide = dot(hot, table_ref[:, :256])
+        left = jnp.where(here == 2, wide[:, :LANES], side)
+        right = jnp.where(here == 2, wide[:, LANES:], 0.0)
         reply_ref[rows, :] = jnp.concatenate([left, right], axis=1).astype(BF16)
 
 
@@ -153,10 +170,23 @@
     return jnp.where((list_ref[0, rank] >> 1) != rank, 0, 1)
 
 
-def give_kernel(rank_ref, list_ref, cotangent_ref, given_ref, copied):
-    copy = pltpu.make_async_copy(cotangent_ref.at[traded_slot(rank_ref, list_ref)], given_ref, copied)
-    copy.start()
-    copy.wait()
+def stage_layer_kernel(
+    after_ref, narrow_ref, middle_ref, wide_ref, joined_ref, lift_here, gating_here, values_here, copied
+):
+    del after_ref
+    moves = [
+        (wide_ref, lift_here.at[0:256]),
+        (middle_ref, lift_here.at[256:384]),
+        (narrow_ref, lift_here.at[384:448]),
+    ]
+    for part, here in enumerate([gating_here, values_here]):
+        moves.append((joined_ref.at[:, part * WIDTH : (part + 1) * WIDTH], here))
+    copies = [pltpu.make_async_copy(there, here, copied.at[k]) for k, (there, here) in enumerate(moves)]
+    for copy in copies:
+        copy.start()
+    lift_here[448:, :] = jnp.zeros((64, WIDTH), BF16)
+    for copy in copies:
+        copy.wait()
 
 
 def mean(values):
@@ -182,27 +212,23 @@
 
 
 def layer_kernel(
-    rank_ref, list_ref, length_ref, slot_ref, landed_ref, class_ref, cotangent_ref, arrived_ref,
-    narrow_lift_ref, middle_lift_ref, wide_lift_ref, joined_weight_ref, output_weight_ref,
-    kept_ref, given_ref, payload_ref,
-    lift_here, joined_here, output_here, cotangent_here, slope_ref, curve_ref, copied,
+    rank_ref, list_ref, length_ref, slot_ref, landed_ref, class_ref, lift_here, gating_here, values_here,
+    cotangent_ref, arrived_ref, joined_ref, output_weight_ref, kept_ref, given_ref, payload_ref,
+    queries_here, keys_here, output_here, cotangent_here, slope_ref, curve_ref, copied,
 ):
     rank = rank_ref[0]
     traded = traded_slot(rank_ref, list_ref)
     kept = 1 - traded
     moves = [
-        (wide_lift_ref, lift_here.at[0:256]),
-        (middle_lift_ref, lift_here.at[256:384]),
-        (narrow_lift_ref, lift_here.at[384:448]),
-        (joined_weight_ref, joined_here),
+        (joined_ref.at[:, 2 * WIDTH : 3 * WIDTH], queries_here),
+        (joined_ref.at[:, 3 * WIDTH :], keys_here),
         (output_weight_ref, output_here),
         (cotangent_ref.at[kept], cotangent_here.at[kept]),
-        (arrived_ref, cotangent_here.at[traded]),
+        (arrived_ref.at[list_ref[traded, rank] & 1], cotangent_here.at[traded]),
     ]
     copies = [pltpu.make_async_copy(there, here, copied.at[k]) for k, (there, here) in enumerate(moves)]
     for copy in copies:
         copy.start()
-    lift_here[448:, :] = jnp.zeros((64, WIDTH), BF16)
     zero = jnp.zeros((), BF16)
     rows = kept_ref.shape[0]
     hists = slot_ref.shape[0]
@@ -211,7 +237,7 @@
     amount = devices * CAP
     slot = flat_row(slot_ref)
     raw = dot(one_hot(iota((tokens, amount), 1) == to_column(slot)), landed_ref[...]).astype(BF16)
-    kind = class_ref[...]
+    kind = to_column(flat_row(class_ref))
     spread = jnp.concatenate(
         [
             jnp.where(kind == 2, raw, zero),
@@ -220,16 +246,16 @@
         ],
         axis=1,
     )
-    for copy in copies[:3]:
-        copy.wait()
     widened = rounded(dot(spread, lift_here[...]))
     normed, scale = normalize(widened)
     normed_low = normed.astype(BF16)
-    copies[3].wait()
+    joined_here = [gating_here, values_here, queries_here, keys_here]
     joined = []
     for part in range(4):
         columns = slice(part * WIDTH, (part + 1) * WIDTH)
-        before = dot(normed_low, joined_here[:, columns])
+        if part >= 2:
+            copies[part - 2].wait()
+        before = dot(normed_low, joined_here[part][...])
         gate = sigmoid(before)
         joined.append((before * gate).astype(BF16))
         slope_ref[:, columns] = gate * (1.0 + before * (1.0 - gate))
@@ -257,7 +283,7 @@
         mixed.append(jnp.concatenate(heads, axis=1))
     mixed_normed, mixed_scale = normalize(jnp.concatenate(mixed, axis=0))
     gated = (mixed_normed * gating).astype(BF16)
-    for copy in copies[4:]:
+    for copy in copies[2:]:
         copy.wait()
     result = dot(gated, output_here[...]) + widened
     output = jnp.where(valid, result, 0.0).astype(BF16)
@@ -288,7 +314,7 @@
     for part in range(4):
         columns = slice(part * WIDTH, (part + 1) * WIDTH)
         before_grad = (joined_grad[part].astype(F32) * slope_ref[:, columns]).astype(BF16)
-        normed_grad += dot_nt(before_grad, joined_here[:, columns])
+        normed_grad += dot_nt(before_grad, joined_here[part][...])
     grad = normalize_grad(rounded(normed_grad), normed, scale) + result_grad.astype(F32)
     grad = grad.astype(BF16)
     spread_grad = dot_nt(grad, lift_here[...])
@@ -309,11 +335,11 @@
     share_ref[...] = jnp.broadcast_to(total[None].astype(BF16), share_ref.shape)
 
 
-def scatter_kernel(landed_ref, code_ref, narrow_ref, middle_ref, wide_ref):
+def scatter_kernel(landed_ref, asked_ref, marks_ref, narrow_ref, middle_ref, wide_ref):
     sources = landed_ref.shape[0]
     amount = sources * CAP
     grads = landed_ref[...].astype(F32)[:, :CAP, :].reshape(amount, 256)
-    code = code_ref[...]
+    code = request_codes(asked_ref, marks_ref[...])
     kind = code >> 11
     slab = code & 2047
     line = to_row(jnp.where(kind == 0, slab >> 1, slab))
@@ -330,13 +356,12 @@
             narrow_ref[start : start + step, :] = dot(hot, narrow)
 
 
-def place_kernel(rank_ref, list_ref, kept_ref, arrived_ref, output_ref):
+def finish_kernel(
+    rank_ref, list_ref, kept_ref, arrived_ref, shares_ref, output_ref, narrow_ref, middle_ref, wide_ref
+):
     traded = traded_slot(rank_ref, list_ref)
     output_ref[1 - traded] = kept_ref[...]
     output_ref[traded] = arrived_ref[...]
-
-
-def delta_kernel(shares_ref, narrow_ref, middle_ref, wide_ref):
     devices = shares_ref.shape[0]
     shares = shares_ref[...].astype(F32).reshape(devices // 2, 2, CAP, 256)
     for half in range(2):
@@ -350,12 +375,21 @@
 SMEM = pl.BlockSpec(memory_space=pltpu.SMEM)
 VMEM = pl.BlockSpec(memory_space=pltpu.VMEM)
 HBM = pl.BlockSpec(memory_space=pltpu.HBM)
-
-
-def call(kernel, outs, args, scratch=(), flops=0, limit=32):
-    shapes = [jax.ShapeDtypeStruct(shape, dtype) for shape, dtype in outs]
-    arrays = [array for _, array in args]
-    moved = sum(a.size * a.dtype.itemsize for a in arrays + shapes)
+KEPT = pl.BlockSpec(memory_space=pltpu.VMEM)
+
+
+def call(kernel, outs, args, scratch=(), flops=0, limit=LIMIT):
+    arrays = []
+    for space, array in args:
+        if space is KEPT:
+            array = pltpu.with_memory_space_constraint(array, pltpu.VMEM)
+        elif space is not VMEM:
+            array = pltpu.with_memory_space_constraint(array, pltpu.HBM)
+        arrays.append(array)
+    shapes = [
+        pltpu.VMEM(out[0], out[1]) if KEPT in out[2:] else jax.ShapeDtypeStruct(out[0], out[1]) for out in outs
+    ]
+    moved = sum(a.size * a.dtype.itemsize for _, a in args)
     return pl.pallas_call(
         kernel,
         out_shape=shapes,
@@ -363,7 +397,7 @@
         out_specs=[VMEM] * len(shapes),
         scratch_shapes=list(scratch),
         cost_estimate=pl.CostEstimate(flops=flops, bytes_accessed=moved, transcendentals=0),
-        compiler_params=pltpu.CompilerParams(vmem_limit_bytes=limit << 20),
+        compiler_params=pltpu.CompilerParams(vmem_limit_bytes=int(limit * 2**20)),
     )(*arrays)
 
 
@@ -392,11 +426,10 @@
     table_size = lax.axis_size("table")
     devices = data_size * table_size
     rows = cotangent.shape[1]
-    items = slab_index.shape[0]
     amount = devices * CAP
     data_rank = lax.axis_index("dp")
     self_rank = data_rank * table_size + lax.axis_index("table")
-    rank = (SMEM, data_rank.reshape(1).astype(I32))
+    rank = (SMEM, jnp.stack([data_rank, self_rank]).astype(I32))
     plan = (SMEM, balance_list.T)
     owner = owner_device.transpose(0, 2, 1)
     class_list = width_class.reshape(-1, LANES)
@@ -407,57 +440,60 @@
         [((devices, CAP), I32), (owner_row.shape, I32)],
         [(VMEM, owner), (VMEM, owner_row)],
         flops=10**8,
+        limit=62,
     )
     asked = exchange(requests)
-    (kinds,) = call(
-        class_kernel,
-        [((2 * rows, 1), I32)],
-        [(VMEM, owner), (VMEM, owner_row), (VMEM, class_list)],
-        flops=10**9,
-    )
-    (given_cotangent,) = call(
-        give_kernel,
-        [((rows, WIDTH), BF16)],
-        [rank, plan, (HBM, cotangent)],
-        scratch=[pltpu.SemaphoreType.DMA],
-    )
-    arrived_cotangent = lax.ppermute(given_cotangent, "dp", partners)
-    own_classes = lax.dynamic_slice(class_list, (self_rank * (items // LANES), 0), (items // LANES, LANES))
-    replies, codes = call(
-        owner_kernel,
-        [((amount, 256), BF16), ((amount, 1), I32)],
+    slab_list = slab_index.reshape(-1, LANES)
+    ready_cotangent, slots = lax.optimization_barrier((cotangent, slots))
+    arrived_cotangent = lax.ppermute(ready_cotangent, "dp", partners)
+    table, marks = call(
+        stage_rows_kernel,
+        [((middle_table.shape[0], 512), BF16, KEPT), ((slab_list.shape[0], 256), BF16, KEPT)],
         [
-            (VMEM, asked), (VMEM, own_classes), (VMEM, slab_index.reshape(-1, LANES)),
+            rank, (HBM, slots), (HBM, class_list), (HBM, slab_list),
             (HBM, narrow_table), (HBM, middle_table), (HBM, wide_table),
         ],
         scratch=[
-            pltpu.VMEM(narrow_table.shape, BF16),
-            pltpu.VMEM(middle_table.shape, BF16),
-            pltpu.VMEM(wide_table.shape, BF16),
-            pltpu.SemaphoreType.DMA((3,)),
+            pltpu.VMEM(slab_list.shape, I32), pltpu.VMEM(slab_list.shape, I32), pltpu.SemaphoreType.DMA((5,)),
         ],
+    )
+    (replies,) = call(
+        owner_kernel,
+        [((amount, 256), BF16)],
+        [(VMEM, asked), (KEPT, marks), (KEPT, table)],
         flops=3 * 10**9,
     )
+    replies, arrived_cotangent = lax.optimization_barrier((replies, arrived_cotangent))
     landed = exchange(replies)
+    (kinds,) = call(
+        class_kernel,
+        [(owner_row.shape, I32)],
+        [(VMEM, owner), (VMEM, owner_row), (HBM, class_list)],
+        scratch=[pltpu.VMEM(class_list.shape, I32), pltpu.SemaphoreType.DMA],
+        flops=10**9,
+    )
+    staged = call(
+        stage_layer_kernel,
+        [((WIDTH, WIDTH), BF16, KEPT)] * 3,
+        [(HBM, slots), (HBM, narrow_lift), (HBM, middle_lift), (HBM, wide_lift), (HBM, joined_weight)],
+        scratch=[pltpu.SemaphoreType.DMA((5,))],
+    )
     kept_output, given_output, payload = call(
         layer_kernel,
         [((rows, WIDTH), BF16), ((rows, WIDTH), BF16), ((devices, 2 * CAP, 256), BF16)],
-        [
-            rank, plan, (SMEM, history_lengths.T), (VMEM, slots), (VMEM, landed), (VMEM, kinds),
-            (HBM, cotangent), (HBM, arrived_cotangent), (HBM, narrow_lift), (HBM, middle_lift),
-            (HBM, wide_lift), (HBM, joined_weight), (HBM, output_weight),
-        ],
+        [rank, plan, (SMEM, history_lengths.T), (VMEM, slots), (VMEM, landed), (VMEM, kinds)]
+        + [(KEPT, array) for array in staged]
+        + [(HBM, cotangent), (VMEM, arrived_cotangent), (HBM, joined_weight), (HBM, output_weight)],
         scratch=[
             pltpu.VMEM((WIDTH, WIDTH), BF16),
-            pltpu.VMEM((WIDTH, 4 * WIDTH), BF16),
+            pltpu.VMEM((WIDTH, WIDTH), BF16),
             pltpu.VMEM((WIDTH, WIDTH), BF16),
             pltpu.VMEM((2, rows, WIDTH), BF16),
             pltpu.VMEM((2 * rows, 4 * WIDTH), F32),
             pltpu.VMEM((2, HEADS, rows, rows), F32),
-            pltpu.SemaphoreType.DMA((7,)),
+            pltpu.SemaphoreType.DMA((5,)),
         ],
         flops=10**10,
-        limit=40,
     )
     home = exchange(payload)
     (share,) = call(sum_kernel, [((devices, CAP, 256), BF16)], [(VMEM, home)])
@@ -467,16 +503,15 @@
     narrow_grad, middle_grad, wide_grad = call(
         scatter_kernel,
         [(narrow_table.shape, F32), (middle_table.shape, F32), (wide_table.shape, F32)],
-        [(VMEM, home), (VMEM, codes)],
+        [(VMEM, home), (VMEM, asked), (KEPT, marks)],
         flops=3 * 10**9,
     )
-    (output,) = call(
-        place_kernel, [(cotangent.shape, BF16)], [rank, plan, (VMEM, kept_output), (VMEM, arrived_output)]
-    )
-    narrow_delta, middle_delta, wide_delta = call(
-        delta_kernel,
-        [(narrow_lift.shape, F32), (middle_lift.shape, F32), (wide_lift.shape, F32)],
-        [(VMEM, shares)],
+    output, narrow_delta, middle_delta, wide_delta = call(
+        finish_kernel,
+        [
+            (cotangent.shape, BF16), (narrow_lift.shape, F32), (middle_lift.shape, F32), (wide_lift.shape, F32),
+        ],
+        [rank, plan, (VMEM, kept_output), (VMEM, arrived_output), (VMEM, shares)],
     )
     return (output, narrow_grad, middle_grad, wide_grad, narrow_delta, middle_delta, wide_delta)
 

time: 116 us -> 104 us (0.90)
  local copies, waits for them, and re-layouts: 10 us -> 0.01 us
  Pallas kernels: 27.5 us -> 31.5 us
  blocking collectives: 25.3 us -> 23.1 us
  waiting for transfers between devices: 23.1 us -> 21.3 us
  starting transfers between devices: 28.2 us -> 26.8 us
    unnamed x38 -> x6, local copies, waits for them, and re-layouts: 9.3 us -> 0.01 us
    ppermute x1, waiting for transfers between devices: 8.01 us -> 0.01 us  [body(): arrived_cotangent = lax.ppermute(ready_cotangent, 'dp', partners)]
    all_to_all x3, waiting for transfers between devices: 8.77 us -> 15.5 us  [exchange(): lax.all_to_all(array, ('dp', 'table'), split_axis=0, concat_axis=0, tiled...]
    pallas_call x9, Pallas kernels: 27.5 us -> 31.5 us  [call(): pl.pallas_call(kernel, out_shape=shapes, in_specs=[space for space, _ in...]
    all_to_all x3, starting transfers between devices: 20.9 us -> 18.6 us  [exchange(): lax.all_to_all(array, ('dp', 'table'), split_axis=0, concat_axis=0, tiled...]
    all_to_all x1, blocking collectives: 25.3 us -> 23.1 us  [exchange(): lax.all_to_all(array, ('dp', 'table'), split_axis=0, concat_axis=0, tiled...]
  transfers between devices with their start and end apart: 5 -> 5, of which waited for: 3 -> 3; matrix products, arithmetic and copies ran while one was open for 1% -> 1% of each run, Pallas kernels for 8% -> 15%
where the time goes in v3:
time: 104 us
  Pallas kernels  31.5 us (30%)
  starting transfers between devices  26.8 us (26%)
  blocking collectives  23.1 us (22%)
  waiting for transfers between devices  21.3 us (20%)
    pallas_call x9, Pallas kernels, call(): pl.pallas_call(kernel, out_shape=shapes, in_specs=[space for space, _ in...  31.5 us
    all_to_all x1, blocking collectives, exchange(): lax.all_to_all(array, ('dp', 'table'), split_axis=0, concat_axis=0, tiled...  23.1 us
    all_to_all x3, starting transfers between devices, exchange(): lax.all_to_all(array, ('dp', 'table'), split_axis=0, concat_axis=0, tiled...  18.6 us
    all_to_all x3, waiting for transfers between devices, exchange(): lax.all_to_all(array, ('dp', 'table'), split_axis=0, concat_axis=0, tiled...  15.5 us
    ppermute x1, waiting for transfers between devices, body(): arrived_output = lax.ppermute(given_output, 'dp', partners)  5.86 us
    ppermute x1, starting transfers between devices, body(): arrived_cotangent = lax.ppermute(ready_cotangent, 'dp', partners)  4.42 us
    ppermute x1, starting transfers between devices, body(): arrived_output = lax.ppermute(given_output, 'dp', partners)  3.72 us
  transfers between devices with their start and end apart: 5, of which 3 were waited for; matrix products, arithmetic and copies ran while one was open for 1% of the time, Pallas kernels for 15%

profile of v3, /device:TPU:1, one launch (start us, length us, event | category | flops | bytes accessed | tf_op | source)
XLA Modules:
  0.0 104.0 jit_solution(11027484203900018308)
XLA Ops:
  0.6 1.8 %shard_map.198 = (s32[128,8]{1,0:T(8,128)}, s32[2,256]{1,0:T(2,128)}) custom-call(s32[2,1,256]{2,1,0:T(1,128)} %bitcast.16, s32[2,256]{1,0:T(2,128)} %item_ref.3), custom_call_target="tpu_custom_call" | custom-call | flops 100000000 | bytes 4096 | tf_op jit(solution)/shard_map/pallas_call | solution.py:393
  2.4 4.4 %collective-permute-start = (bf16[2,256,512]{2,1,0:T(8,128)(2,1)}, bf16[2,256,512]{2,1,0:T(8,128)(2,1)S(1)}, u32[]{:S(2)}, u32[]{:S(2)}) collective-permute-start(bf16[2,256,512]{2,1,0:T(8,128)(2,1)} %cotangent_ref.1), channel_id=1, source_target_pairs={{0,64},{16,80},{32,96},{48,112},{64,0},{80,16},{96,32},{112,48},{1... | collective-permute-start | bytes 1572872 | tf_op jit(solution)/shard_map/ppermute | solution.py:448
  6.9 7.9 %all-to-all-start = ((s32[128,1,8]{2,1,0:T(1,128)}), s32[128,1,8]{2,1,0:T(1,128)S(1)}, u32[]{:S(2)}, u32[]{:S(2)}) async-start(s32[128,1,8]{2,1,0:T(1,128)} %bitcast.20), calls=%async_computation | async-start | bytes 131072 | tf_op jit(solution)/shard_map/all_to_all | solution.py:405
  14.8 0.6 pad_add_fusion.rank_ref
  15.4 2.2 %shard_map.199 = (bf16[2048,512]{1,0:T(8,128)(2,1)S(1)}, bf16[32,256]{1,0:T(8,128)(2,1)S(1)}) custom-call(s32[2]{0:T(128)} %pad_add_fusion.rank_ref, s32[2,256]{1,0:T(2,128)} %get-tuple-element.30.after_ref.slot_ref, s32[4096,128]{1,0:T(8,128)} %bitcast.18, s32[32,128]{1,0:T(8,128)} %bitcast.21, bf16[1024,128]{1,0:T(8,128)(2,1)} %narrow_ref.2, ...), custom_call_target="tpu_custom_call" | custom-call | bytes 3950600 | tf_op jit(solution)/shard_map/pallas_call | solution.py:393
  17.6 6.7 %all-to-all-done = s32[128,1,8]{2,1,0:T(1,128)S(1)} async-done(((s32[128,1,8]{2,1,0:T(1,128)}), s32[128,1,8]{2,1,0:T(1,128)S(1)}, u32[]{:S(2)}, u32[]{:S(2)}) %all-to-all-start) | async-done | bytes 4128 | tf_op jit(solution)/shard_map/all_to_all | solution.py:405
  24.3 3.7 %shard_map.200 = bf16[1024,256]{1,0:T(8,128)(2,1)} custom-call(s32[128,8]{1,0:T(8,128)S(1)} %bitcast.14, bf16[32,256]{1,0:T(8,128)(2,1)S(1)} %get-tuple-element.32.marks_ref, bf16[2048,512]{1,0:T(8,128)(2,1)S(1)} %get-tuple-element.33.table_ref), custom_call_target="tpu_custom_call" | custom-call | flops 3000000000 | bytes 2117632 | tf_op jit(solution)/shard_map/pallas_call | solution.py:393
  28.0 0.0 collective-permute-done.arrived_ref
  28.0 5.8 %all-to-all-start.1 = ((bf16[128,8,256]{2,1,0:T(8,128)(2,1)}), bf16[128,8,256]{2,1,0:T(8,128)(2,1)S(1)}, u32[]{:S(2)}, u32[]{:S(2)}) async-start(bf16[128,8,256]{2,1,0:T(8,128)(2,1)} %bitcast.10), calls=%async_computation.1 | async-start | bytes 1048576 | tf_op jit(solution)/shard_map/all_to_all | solution.py:405
  33.8 1.4 %shard_map.202 = (bf16[512,512]{1,0:T(8,128)(2,1)S(1)}, bf16[512,512]{1,0:T(8,128)(2,1)S(1)}, bf16[512,512]{1,0:T(8,128)(2,1)S(1)}) custom-call(s32[2,256]{1,0:T(2,128)} %get-tuple-element.30.after_ref.slot_ref, bf16[64,512]{1,0:T(8,128)(2,1)} %narrow_ref.3, bf16[128,512]{1,0:T(8,128)(2,1)} %middle_ref.3, bf16[256,512]{1,0:T(8,128)(2,1)} %wide_ref.3, ...), custom_call_target="tpu_custom_call" | custom-call | bytes 2557952 | tf_op jit(solution)/shard_map/pallas_call | solution.py:393
  35.2 0.0 copy-done.1
  35.2 0.0 copy-start
  35.3 3.1 %shard_map.201.class_ref = s32[2,256]{1,0:T(2,128)S(1)} custom-call(s32[2,1,256]{2,1,0:T(1,128)S(1)} %bitcast.17, s32[2,256]{1,0:T(2,128)S(1)} %copy-done.2, s32[4096,128]{1,0:T(8,128)} %bitcast.19), custom_call_target="tpu_custom_call" | custom-call | flops 1000000000 | bytes 2101248 | tf_op jit(solution)/shard_map/pallas_call | solution.py:393
  38.4 8.8 %all-to-all-done.1 = bf16[128,8,256]{2,1,0:T(8,128)(2,1)S(1)} async-done(((bf16[128,8,256]{2,1,0:T(8,128)(2,1)}), bf16[128,8,256]{2,1,0:T(8,128)(2,1)S(1)}, u32[]{:S(2)}, u32[]{:S(2)}) %all-to-all-start.1) | async-done | bytes 524320 | tf_op jit(solution)/shard_map/all_to_all | solution.py:405
  47.1 0.0 copy-done
  47.1 10.9 %shard_map.203 = (bf16[256,512]{1,0:T(8,128)(2,1)S(1)}, bf16[256,512]{1,0:T(8,128)(2,1)S(1)}, bf16[128,16,256]{2,1,0:T(8,128)(2,1)S(1)}) custom-call(s32[2]{0:T(128)} %pad_add_fusion.rank_ref, s32[2,8]{1,0:T(2,128)} %bitcast.22, s32[2,8]{1,0:T(2,128)} %bitcast.24, s32[2,256]{1,0:T(2,128)S(1)} %copy-done, bf16[1024,256]{1,0:T(8,128)(2,1)S(1)} %bitcast.13, ...), custom_call_target="tpu_custom_call" | custom-call | flops 10000000000 | bytes 5771400 | tf_op jit(solution)/shard_map/pallas_call | solution.py:393
  58.1 23.1 %all_to_all.32.landed_ref = bf16[128,16,256]{2,1,0:T(8,128)(2,1)S(1)} all-to-all(bf16[128,16,256]{2,1,0:T(8,128)(2,1)S(1)} %get-tuple-element.42), channel_id=1, replica_groups=mesh['dp'=8,'table'=16] {'dp','table'}, dimensions={0} | all-to-all | bytes 2097152 | tf_op jit(solution)/shard_map/all_to_all | solution.py:405
  81.2 1.0 shard_map.204
  82.1 4.9 %all-to-all-start.3 = ((bf16[128,8,256]{2,1,0:T(8,128)(2,1)}), bf16[128,8,256]{2,1,0:T(8,128)(2,1)S(1)}, u32[]{:S(2)}, u32[]{:S(2)}) async-start(bf16[128,8,256]{2,1,0:T(8,128)(2,1)} %shard_map.204), calls=%async_computation.3 | async-start | bytes 1048576 | tf_op jit(solution)/shard_map/all_to_all | solution.py:405
  87.1 3.7 %collective-permute-start.1 = (bf16[256,512]{1,0:T(8,128)(2,1)S(1)}, bf16[256,512]{1,0:T(8,128)(2,1)S(1)}, u32[]{:S(2)}, u32[]{:S(2)}) collective-permute-start(bf16[256,512]{1,0:T(8,128)(2,1)S(1)} %get-tuple-element.43), channel_id=1, source_target_pairs={{0,64},{16,80},{32,96},{48,112},{64,0},{80,16},{96,32},{112,48},{1... | collective-permute-start | bytes 786440 | tf_op jit(solution)/shard_map/ppermute | solution.py:502
  90.8 5.5 %shard_map.206 = (f32[1024,128]{1,0:T(8,128)}, f32[2048,128]{1,0:T(8,128)}, f32[2048,256]{1,0:T(8,128)}) custom-call(bf16[128,16,256]{2,1,0:T(8,128)(2,1)S(1)} %all_to_all.32.landed_ref, s32[128,8]{1,0:T(8,128)S(1)} %bitcast.15, bf16[32,256]{1,0:T(8,128)(2,1)S(1)} %get-tuple-element.32.marks_ref), custom_call_target="tpu_custom_call" | custom-call | flops 3000000000 | bytes 1069056 | tf_op jit(solution)/shard_map/pallas_call | solution.py:393
  96.3 5.9 %collective-permute-done.1.arrived_ref = bf16[256,512]{1,0:T(8,128)(2,1)S(1)} collective-permute-done((bf16[256,512]{1,0:T(8,128)(2,1)S(1)}, bf16[256,512]{1,0:T(8,128)(2,1)S(1)}, u32[]{:S(2)}, u32[]{:S(2)}) %collective-permute-start.1) | collective-permute-done | bytes 262176 | tf_op jit(solution)/shard_map/ppermute | solution.py:502
  102.2 0.0 all-to-all-done.3.shares_ref
  102.2 1.8 %shard_map.205 = (bf16[2,256,512]{2,1,0:T(8,128)(2,1)}, f32[64,512]{1,0:T(8,128)}, f32[128,512]{1,0:T(8,128)}, f32[256,512]{1,0:T(8,128)}) custom-call(s32[2]{0:T(128)} %pad_add_fusion.rank_ref, s32[2,8]{1,0:T(2,128)} %bitcast.23, bf16[256,512]{1,0:T(8,128)(2,1)S(1)} %get-tuple-element.40.kept_ref, bf16[256,512]{1,0:T(8,128)(2,1)S(1)} %collective-permute-done.1.arrived_ref, ...), custom_call_target="tpu_custom_call" | custom-call | bytes 1048648 | tf_op jit(solution)/shard_map/pallas_call | solution.py:393
  (3 shorter events, 0.0 us)
Async XLA Ops:
  2.4 25.6 %collective-permute-start = (bf16[2,256,512]{2,1,0:T(8,128)(2,1)}, bf16[2,256,512]{2,1,0:T(8,128)(2,1)S(1)}, u32[]{:S(2)}, u32[]{:S(2)}) collective-permute-start(bf16[2,256,512]{2,1,0:T(8,128)(2,1)} %cotangent_ref.1), channel_id=1, source_target_pairs={{0,64},{16,80},{32,96},{48,112},{64,0},{80,16},{96,32},{112,48},{1... | collective-permute-start | bytes 1572872 | tf_op jit(solution)/shard_map/ppermute | solution.py:448
  6.9 17.4 %all-to-all-start = ((s32[128,1,8]{2,1,0:T(1,128)}), s32[128,1,8]{2,1,0:T(1,128)S(1)}, u32[]{:S(2)}, u32[]{:S(2)}) async-start(s32[128,1,8]{2,1,0:T(1,128)} %bitcast.20), calls=%async_computation | async-start | bytes 131072 | tf_op jit(solution)/shard_map/all_to_all | solution.py:405
  28.0 7.2 %copy-start.1 = (s32[2,256,1]{1,2,0:T(1,128)S(1)}, s32[2,256,1]{1,2,0:T(1,128)}, u32[]{:S(2)}) copy-start(s32[2,256,1]{1,2,0:T(1,128)} %param.17) | copy-start | bytes 6148
  28.0 7.2 %copy-start.2 = (s32[2,256]{1,0:T(2,128)S(1)}, s32[2,256]{1,0:T(2,128)}, u32[]{:S(2)}) copy-start(s32[2,256]{1,0:T(2,128)} %item_ref.3) | copy-start | bytes 6148
  28.0 19.1 %all-to-all-start.1 = ((bf16[128,8,256]{2,1,0:T(8,128)(2,1)}), bf16[128,8,256]{2,1,0:T(8,128)(2,1)S(1)}, u32[]{:S(2)}, u32[]{:S(2)}) async-start(bf16[128,8,256]{2,1,0:T(8,128)(2,1)} %bitcast.10), calls=%async_computation.1 | async-start | bytes 1048576 | tf_op jit(solution)/shard_map/all_to_all | solution.py:405
  35.2 11.9 %copy-start = (s32[2,256]{1,0:T(2,128)S(1)}, s32[2,256]{1,0:T(2,128)}, u32[]{:S(2)}) copy-start(s32[2,256]{1,0:T(2,128)} %get-tuple-element.30.after_ref.slot_ref) | copy-start | bytes 6148
  82.1 20.0 %all-to-all-start.3 = ((bf16[128,8,256]{2,1,0:T(8,128)(2,1)}), bf16[128,8,256]{2,1,0:T(8,128)(2,1)S(1)}, u32[]{:S(2)}, u32[]{:S(2)}) async-start(bf16[128,8,256]{2,1,0:T(8,128)(2,1)} %shard_map.204), calls=%async_computation.3 | async-start | bytes 1048576 | tf_op jit(solution)/shard_map/all_to_all | solution.py:405
  87.1 15.1 %collective-permute-start.1 = (bf16[256,512]{1,0:T(8,128)(2,1)S(1)}, bf16[256,512]{1,0:T(8,128)(2,1)S(1)}, u32[]{:S(2)}, u32[]{:S(2)}) collective-permute-start(bf16[256,512]{1,0:T(8,128)(2,1)S(1)} %get-tuple-element.43), channel_id=1, source_target_pairs={{0,64},{16,80},{32,96},{48,112},{64,0},{80,16},{96,32},{112,48},{1... | collective-permute-start | bytes 786440 | tf_op jit(solution)/shard_map/ppermute | solution.py:502

commit v4 on v3

--- a/solution.py
+++ b/solution.py
@@ -236,7 +236,8 @@
     devices = payload_ref.shape[0]
     amount = devices * CAP
     slot = flat_row(slot_ref)
-    raw = dot(one_hot(iota((tokens, amount), 1) == to_column(slot)), landed_ref[...]).astype(BF16)
+    placing = one_hot(iota((amount, tokens), 0) == slot)
+    raw = dot_tn(placing, landed_ref[...]).astype(BF16)
     kind = to_column(flat_row(class_ref))
     spread = jnp.concatenate(
         [
@@ -249,16 +250,17 @@
     widened = rounded(dot(spread, lift_here[...]))
     normed, scale = normalize(widened)
     normed_low = normed.astype(BF16)
+    for copy in copies:
+        copy.wait()
     joined_here = [gating_here, values_here, queries_here, keys_here]
     joined = []
     for part in range(4):
         columns = slice(part * WIDTH, (part + 1) * WIDTH)
-        if part >= 2:
-            copies[part - 2].wait()
         before = dot(normed_low, joined_here[part][...])
         gate = sigmoid(before)
-        joined.append((before * gate).astype(BF16))
-        slope_ref[:, columns] = gate * (1.0 + before * (1.0 - gate))
+        active = before * gate
+        joined.append(active.astype(BF16))
+        slope_ref[:, columns] = gate + active * (1.0 - gate)
     gating, values, queries, keys = joined
     gating = gating.astype(F32)
     place = iota((tokens, 1), 0)
@@ -277,14 +279,13 @@
             scores = dot_nt(queries[lines, columns], keys[lines, columns])
             gate = sigmoid(scores)
             scaled = gate * factor
-            weights[hist, head] = (scores * scaled).astype(BF16)
-            curve_ref[hist, head] = scaled * (1.0 + scores * (1.0 - gate))
+            active = scores * scaled
+            weights[hist, head] = active.astype(BF16)
+            curve_ref[hist, head] = scaled + active * (1.0 - gate)
             heads.append(dot(weights[hist, head], values[lines, columns]))
         mixed.append(jnp.concatenate(heads, axis=1))
     mixed_normed, mixed_scale = normalize(jnp.concatenate(mixed, axis=0))
     gated = (mixed_normed * gating).astype(BF16)
-    for copy in copies[2:]:
-        copy.wait()
     result = dot(gated, output_here[...]) + widened
     output = jnp.where(valid, result, 0.0).astype(BF16)
     kept_ref[...] = jnp.where(traded == 0, output[rows:], output[:rows])
@@ -326,7 +327,7 @@
     row_grad = jnp.concatenate([left, right], axis=1).astype(BF16)
     term = dot_tn(spread, grad).reshape(devices // 2, CAP, WIDTH)
     term = jnp.stack([term[:, :, :256], term[:, :, 256:]], axis=1).reshape(devices, CAP, 256)
-    placed = dot(one_hot(iota((amount, tokens), 0) == slot), row_grad).reshape(devices, CAP, 256)
+    placed = dot(placing, row_grad).reshape(devices, CAP, 256)
     payload_ref[...] = jnp.concatenate([placed, term], axis=1).astype(BF16)
 
 

time: 104 us -> 103 us (level)
  Pallas kernels: 31.5 us -> 30.4 us
    pallas_call x9, Pallas kernels: 31.5 us -> 30.4 us  [call(): pl.pallas_call(kernel, out_shape=shapes, in_specs=[space for space, _ in...]
where the time goes in v4:
time: 103 us
  Pallas kernels  30.4 us (30%)
  starting transfers between devices  26.8 us (26%)
  blocking collectives  23.1 us (22%)
  waiting for transfers between devices  21.3 us (21%)
    pallas_call x9, Pallas kernels, call(): pl.pallas_call(kernel, out_shape=shapes, in_specs=[space for space, _ in...  30.4 us
    all_to_all x1, blocking collectives, exchange(): lax.all_to_all(array, ('dp', 'table'), split_axis=0, concat_axis=0, tiled...  23.1 us
    all_to_all x3, starting transfers between devices, exchange(): lax.all_to_all(array, ('dp', 'table'), split_axis=0, concat_axis=0, tiled...  18.6 us
    all_to_all x3, waiting for transfers between devices, exchange(): lax.all_to_all(array, ('dp', 'table'), split_axis=0, concat_axis=0, tiled...  15.5 us
    ppermute x1, waiting for transfers between devices, body(): arrived_output = lax.ppermute(given_output, 'dp', partners)  5.87 us
    ppermute x1, starting transfers between devices, body(): arrived_cotangent = lax.ppermute(ready_cotangent, 'dp', partners)  4.42 us
    ppermute x1, starting transfers between devices, body(): arrived_output = lax.ppermute(given_output, 'dp', partners)  3.72 us
  transfers between devices with their start and end apart: 5, of which 3 were waited for; matrix products, arithmetic and copies ran while one was open for 1% of the time, Pallas kernels for 15%

profile of v4, /device:TPU:1, one launch (start us, length us, event | category | flops | bytes accessed | tf_op | source)
XLA Modules:
  0.0 102.9 jit_solution(17187530299856040401)
XLA Ops:
  0.6 1.8 %shard_map.198 = (s32[128,8]{1,0:T(8,128)}, s32[2,256]{1,0:T(2,128)}) custom-call(s32[2,1,256]{2,1,0:T(1,128)} %bitcast.16, s32[2,256]{1,0:T(2,128)} %item_ref.3), custom_call_target="tpu_custom_call" | custom-call | flops 100000000 | bytes 4096 | tf_op jit(solution)/shard_map/pallas_call | solution.py:394
  2.4 4.4 %collective-permute-start = (bf16[2,256,512]{2,1,0:T(8,128)(2,1)}, bf16[2,256,512]{2,1,0:T(8,128)(2,1)S(1)}, u32[]{:S(2)}, u32[]{:S(2)}) collective-permute-start(bf16[2,256,512]{2,1,0:T(8,128)(2,1)} %cotangent_ref.1), channel_id=1, source_target_pairs={{0,64},{16,80},{32,96},{48,112},{64,0},{80,16},{96,32},{112,48},{1... | collective-permute-start | bytes 1572872 | tf_op jit(solution)/shard_map/ppermute | solution.py:449
  6.9 7.9 %all-to-all-start = ((s32[128,1,8]{2,1,0:T(1,128)}), s32[128,1,8]{2,1,0:T(1,128)S(1)}, u32[]{:S(2)}, u32[]{:S(2)}) async-start(s32[128,1,8]{2,1,0:T(1,128)} %bitcast.20), calls=%async_computation | async-start | bytes 131072 | tf_op jit(solution)/shard_map/all_to_all | solution.py:406
  14.8 0.6 pad_add_fusion.rank_ref
  15.4 2.2 %shard_map.199 = (bf16[2048,512]{1,0:T(8,128)(2,1)S(1)}, bf16[32,256]{1,0:T(8,128)(2,1)S(1)}) custom-call(s32[2]{0:T(128)} %pad_add_fusion.rank_ref, s32[2,256]{1,0:T(2,128)} %get-tuple-element.30.after_ref.slot_ref, s32[4096,128]{1,0:T(8,128)} %bitcast.18, s32[32,128]{1,0:T(8,128)} %bitcast.21, bf16[1024,128]{1,0:T(8,128)(2,1)} %narrow_ref.2, ...), custom_call_target="tpu_custom_call" | custom-call | bytes 3950600 | tf_op jit(solution)/shard_map/pallas_call | solution.py:394
  17.6 6.7 %all-to-all-done = s32[128,1,8]{2,1,0:T(1,128)S(1)} async-done(((s32[128,1,8]{2,1,0:T(1,128)}), s32[128,1,8]{2,1,0:T(1,128)S(1)}, u32[]{:S(2)}, u32[]{:S(2)}) %all-to-all-start) | async-done | bytes 4128 | tf_op jit(solution)/shard_map/all_to_all | solution.py:406
  24.3 3.7 %shard_map.200 = bf16[1024,256]{1,0:T(8,128)(2,1)} custom-call(s32[128,8]{1,0:T(8,128)S(1)} %bitcast.14, bf16[32,256]{1,0:T(8,128)(2,1)S(1)} %get-tuple-element.32.marks_ref, bf16[2048,512]{1,0:T(8,128)(2,1)S(1)} %get-tuple-element.33.table_ref), custom_call_target="tpu_custom_call" | custom-call | flops 3000000000 | bytes 2117632 | tf_op jit(solution)/shard_map/pallas_call | solution.py:394
  28.0 0.0 collective-permute-done.arrived_ref
  28.0 5.8 %all-to-all-start.1 = ((bf16[128,8,256]{2,1,0:T(8,128)(2,1)}), bf16[128,8,256]{2,1,0:T(8,128)(2,1)S(1)}, u32[]{:S(2)}, u32[]{:S(2)}) async-start(bf16[128,8,256]{2,1,0:T(8,128)(2,1)} %bitcast.10), calls=%async_computation.1 | async-start | bytes 1048576 | tf_op jit(solution)/shard_map/all_to_all | solution.py:406
  33.8 1.4 %shard_map.202 = (bf16[512,512]{1,0:T(8,128)(2,1)S(1)}, bf16[512,512]{1,0:T(8,128)(2,1)S(1)}, bf16[512,512]{1,0:T(8,128)(2,1)S(1)}) custom-call(s32[2,256]{1,0:T(2,128)} %get-tuple-element.30.after_ref.slot_ref, bf16[64,512]{1,0:T(8,128)(2,1)} %narrow_ref.3, bf16[128,512]{1,0:T(8,128)(2,1)} %middle_ref.3, bf16[256,512]{1,0:T(8,128)(2,1)} %wide_ref.3, ...), custom_call_target="tpu_custom_call" | custom-call | bytes 2557952 | tf_op jit(solution)/shard_map/pallas_call | solution.py:394
  35.2 0.0 copy-done.1
  35.2 0.0 copy-start
  35.3 3.1 %shard_map.201.class_ref = s32[2,256]{1,0:T(2,128)S(1)} custom-call(s32[2,1,256]{2,1,0:T(1,128)S(1)} %bitcast.17, s32[2,256]{1,0:T(2,128)S(1)} %copy-done.2, s32[4096,128]{1,0:T(8,128)} %bitcast.19), custom_call_target="tpu_custom_call" | custom-call | flops 1000000000 | bytes 2101248 | tf_op jit(solution)/shard_map/pallas_call | solution.py:394
  38.4 8.8 %all-to-all-done.1 = bf16[128,8,256]{2,1,0:T(8,128)(2,1)S(1)} async-done(((bf16[128,8,256]{2,1,0:T(8,128)(2,1)}), bf16[128,8,256]{2,1,0:T(8,128)(2,1)S(1)}, u32[]{:S(2)}, u32[]{:S(2)}) %all-to-all-start.1) | async-done | bytes 524320 | tf_op jit(solution)/shard_map/all_to_all | solution.py:406
  47.1 0.0 copy-done
  47.1 9.9 %shard_map.203 = (bf16[256,512]{1,0:T(8,128)(2,1)S(1)}, bf16[256,512]{1,0:T(8,128)(2,1)S(1)}, bf16[128,16,256]{2,1,0:T(8,128)(2,1)S(1)}) custom-call(s32[2]{0:T(128)} %pad_add_fusion.rank_ref, s32[2,8]{1,0:T(2,128)} %bitcast.22, s32[2,8]{1,0:T(2,128)} %bitcast.24, s32[2,256]{1,0:T(2,128)S(1)} %copy-done, bf16[1024,256]{1,0:T(8,128)(2,1)S(1)} %bitcast.13, ...), custom_call_target="tpu_custom_call" | custom-call | flops 10000000000 | bytes 5771400 | tf_op jit(solution)/shard_map/pallas_call | solution.py:394
  57.0 23.1 %all_to_all.32.landed_ref = bf16[128,16,256]{2,1,0:T(8,128)(2,1)S(1)} all-to-all(bf16[128,16,256]{2,1,0:T(8,128)(2,1)S(1)} %get-tuple-element.42), channel_id=1, replica_groups=mesh['dp'=8,'table'=16] {'dp','table'}, dimensions={0} | all-to-all | bytes 2097152 | tf_op jit(solution)/shard_map/all_to_all | solution.py:406
  80.1 1.0 shard_map.204
  81.0 4.9 %all-to-all-start.3 = ((bf16[128,8,256]{2,1,0:T(8,128)(2,1)}), bf16[128,8,256]{2,1,0:T(8,128)(2,1)S(1)}, u32[]{:S(2)}, u32[]{:S(2)}) async-start(bf16[128,8,256]{2,1,0:T(8,128)(2,1)} %shard_map.204), calls=%async_computation.3 | async-start | bytes 1048576 | tf_op jit(solution)/shard_map/all_to_all | solution.py:406
  86.0 3.7 %collective-permute-start.1 = (bf16[256,512]{1,0:T(8,128)(2,1)S(1)}, bf16[256,512]{1,0:T(8,128)(2,1)S(1)}, u32[]{:S(2)}, u32[]{:S(2)}) collective-permute-start(bf16[256,512]{1,0:T(8,128)(2,1)S(1)} %get-tuple-element.43), channel_id=1, source_target_pairs={{0,64},{16,80},{32,96},{48,112},{64,0},{80,16},{96,32},{112,48},{1... | collective-permute-start | bytes 786440 | tf_op jit(solution)/shard_map/ppermute | solution.py:503
  89.7 5.5 %shard_map.206 = (f32[1024,128]{1,0:T(8,128)}, f32[2048,128]{1,0:T(8,128)}, f32[2048,256]{1,0:T(8,128)}) custom-call(bf16[128,16,256]{2,1,0:T(8,128)(2,1)S(1)} %all_to_all.32.landed_ref, s32[128,8]{1,0:T(8,128)S(1)} %bitcast.15, bf16[32,256]{1,0:T(8,128)(2,1)S(1)} %get-tuple-element.32.marks_ref), custom_call_target="tpu_custom_call" | custom-call | flops 3000000000 | bytes 1069056 | tf_op jit(solution)/shard_map/pallas_call | solution.py:394
  95.2 5.9 %collective-permute-done.1.arrived_ref = bf16[256,512]{1,0:T(8,128)(2,1)S(1)} collective-permute-done((bf16[256,512]{1,0:T(8,128)(2,1)S(1)}, bf16[256,512]{1,0:T(8,128)(2,1)S(1)}, u32[]{:S(2)}, u32[]{:S(2)}) %collective-permute-start.1) | collective-permute-done | bytes 262176 | tf_op jit(solution)/shard_map/ppermute | solution.py:503
  101.1 0.0 all-to-all-done.3.shares_ref
  101.1 1.8 %shard_map.205 = (bf16[2,256,512]{2,1,0:T(8,128)(2,1)}, f32[64,512]{1,0:T(8,128)}, f32[128,512]{1,0:T(8,128)}, f32[256,512]{1,0:T(8,128)}) custom-call(s32[2]{0:T(128)} %pad_add_fusion.rank_ref, s32[2,8]{1,0:T(2,128)} %bitcast.23, bf16[256,512]{1,0:T(8,128)(2,1)S(1)} %get-tuple-element.40.kept_ref, bf16[256,512]{1,0:T(8,128)(2,1)S(1)} %collective-permute-done.1.arrived_ref, ...), custom_call_target="tpu_custom_call" | custom-call | bytes 1048648 | tf_op jit(solution)/shard_map/pallas_call | solution.py:394
  (3 shorter events, 0.0 us)
Async XLA Ops:
  2.4 25.6 %collective-permute-start = (bf16[2,256,512]{2,1,0:T(8,128)(2,1)}, bf16[2,256,512]{2,1,0:T(8,128)(2,1)S(1)}, u32[]{:S(2)}, u32[]{:S(2)}) collective-permute-start(bf16[2,256,512]{2,1,0:T(8,128)(2,1)} %cotangent_ref.1), channel_id=1, source_target_pairs={{0,64},{16,80},{32,96},{48,112},{64,0},{80,16},{96,32},{112,48},{1... | collective-permute-start | bytes 1572872 | tf_op jit(solution)/shard_map/ppermute | solution.py:449
  6.9 17.4 %all-to-all-start = ((s32[128,1,8]{2,1,0:T(1,128)}), s32[128,1,8]{2,1,0:T(1,128)S(1)}, u32[]{:S(2)}, u32[]{:S(2)}) async-start(s32[128,1,8]{2,1,0:T(1,128)} %bitcast.20), calls=%async_computation | async-start | bytes 131072 | tf_op jit(solution)/shard_map/all_to_all | solution.py:406
  28.0 7.2 %copy-start.1 = (s32[2,256,1]{1,2,0:T(1,128)S(1)}, s32[2,256,1]{1,2,0:T(1,128)}, u32[]{:S(2)}) copy-start(s32[2,256,1]{1,2,0:T(1,128)} %param.17) | copy-start | bytes 6148
  28.0 7.2 %copy-start.2 = (s32[2,256]{1,0:T(2,128)S(1)}, s32[2,256]{1,0:T(2,128)}, u32[]{:S(2)}) copy-start(s32[2,256]{1,0:T(2,128)} %item_ref.3) | copy-start | bytes 6148
  28.0 19.1 %all-to-all-start.1 = ((bf16[128,8,256]{2,1,0:T(8,128)(2,1)}), bf16[128,8,256]{2,1,0:T(8,128)(2,1)S(1)}, u32[]{:S(2)}, u32[]{:S(2)}) async-start(bf16[128,8,256]{2,1,0:T(8,128)(2,1)} %bitcast.10), calls=%async_computation.1 | async-start | bytes 1048576 | tf_op jit(solution)/shard_map/all_to_all | solution.py:406
  35.2 11.9 %copy-start = (s32[2,256]{1,0:T(2,128)S(1)}, s32[2,256]{1,0:T(2,128)}, u32[]{:S(2)}) copy-start(s32[2,256]{1,0:T(2,128)} %get-tuple-element.30.after_ref.slot_ref) | copy-start | bytes 6148
  81.0 20.0 %all-to-all-start.3 = ((bf16[128,8,256]{2,1,0:T(8,128)(2,1)}), bf16[128,8,256]{2,1,0:T(8,128)(2,1)S(1)}, u32[]{:S(2)}, u32[]{:S(2)}) async-start(bf16[128,8,256]{2,1,0:T(8,128)(2,1)} %shard_map.204), calls=%async_computation.3 | async-start | bytes 1048576 | tf_op jit(solution)/shard_map/all_to_all | solution.py:406
  86.0 15.1 %collective-permute-start.1 = (bf16[256,512]{1,0:T(8,128)(2,1)S(1)}, bf16[256,512]{1,0:T(8,128)(2,1)S(1)}, u32[]{:S(2)}, u32[]{:S(2)}) collective-permute-start(bf16[256,512]{1,0:T(8,128)(2,1)S(1)} %get-tuple-element.43), channel_id=1, source_target_pairs={{0,64},{16,80},{32,96},{48,112},{64,0},{80,16},{96,32},{112,48},{1... | collective-permute-start | bytes 786440 | tf_op jit(solution)/shard_map/ppermute | solution.py:503

commit v5 on v4

--- a/solution.py
+++ b/solution.py
@@ -171,9 +171,15 @@
 
 
 def stage_layer_kernel(
-    after_ref, narrow_ref, middle_ref, wide_ref, joined_ref, lift_here, gating_here, values_here, copied
+    rank_ref, list_ref, length_ref, after_ref, narrow_ref, middle_ref, wide_ref, joined_ref,
+    facts_ref, lift_here, gating_here, values_here, copied,
 ):
     del after_ref
+    rank = rank_ref[0]
+    traded = traded_slot(rank_ref, list_ref)
+    facts = [traded, list_ref[traded, rank] & 1, length_ref[0, rank], length_ref[1, rank]]
+    for row, fact in enumerate(facts):
+        facts_ref[row : row + 1, :] = jnp.full((1, LANES), fact, I32)
     moves = [
         (wide_ref, lift_here.at[0:256]),
         (middle_ref, lift_here.at[256:384]),
@@ -212,19 +218,15 @@
 
 
 def layer_kernel(
-    rank_ref, list_ref, length_ref, slot_ref, landed_ref, class_ref, lift_here, gating_here, values_here,
+    facts_ref, slot_ref, landed_ref, class_ref, lift_here, gating_here, values_here,
     cotangent_ref, arrived_ref, joined_ref, output_weight_ref, kept_ref, given_ref, payload_ref,
     queries_here, keys_here, output_here, cotangent_here, slope_ref, curve_ref, copied,
 ):
-    rank = rank_ref[0]
-    traded = traded_slot(rank_ref, list_ref)
-    kept = 1 - traded
     moves = [
         (joined_ref.at[:, 2 * WIDTH : 3 * WIDTH], queries_here),
         (joined_ref.at[:, 3 * WIDTH :], keys_here),
         (output_weight_ref, output_here),
-        (cotangent_ref.at[kept], cotangent_here.at[kept]),
-        (arrived_ref.at[list_ref[traded, rank] & 1], cotangent_here.at[traded]),
+        (cotangent_ref, cotangent_here),
     ]
     copies = [pltpu.make_async_copy(there, here, copied.at[k]) for k, (there, here) in enumerate(moves)]
     for copy in copies:
@@ -264,7 +266,9 @@
     gating, values, queries, keys = joined
     gating = gating.astype(F32)
     place = iota((tokens, 1), 0)
-    lengths = [length_ref[hist, rank] for hist in range(hists)]
+    lengths = [facts_ref[2 + hist : 3 + hist, 0:1] for hist in range(hists)]
+    traded = jnp.broadcast_to(facts_ref[0:1, 0:1], (rows, 1))
+    source = jnp.broadcast_to(facts_ref[1:2, 0:1], (rows, 1))
     valid = place < jnp.where(place < rows, lengths[0], rows + lengths[1])
     across = iota((rows, rows), 1)
     causal = across <= iota((rows, rows), 0)
@@ -291,7 +295,10 @@
     kept_ref[...] = jnp.where(traded == 0, output[rows:], output[:rows])
     given_ref[...] = jnp.where(traded == 0, output[:rows], output[rows:])
 
-    cotangent = jnp.concatenate([cotangent_here[0], cotangent_here[1]], axis=0)
+    came = jnp.where(source == 0, arrived_ref[0], arrived_ref[1])
+    cotangent = jnp.concatenate(
+        [jnp.where(traded == 0, came, cotangent_here[0]), jnp.where(traded == 0, cotangent_here[1], came)], axis=0
+    )
     result_grad = jnp.where(valid, cotangent, zero)
     gated_grad = rounded(dot_nt(result_grad, output_here[...]))
     gating_grad = (gated_grad * mixed_normed).astype(BF16)
@@ -358,11 +365,13 @@
 
 
 def finish_kernel(
-    rank_ref, list_ref, kept_ref, arrived_ref, shares_ref, output_ref, narrow_ref, middle_ref, wide_ref
+    facts_ref, kept_ref, arrived_ref, shares_ref, output_ref, narrow_ref, middle_ref, wide_ref
 ):
-    traded = traded_slot(rank_ref, list_ref)
-    output_ref[1 - traded] = kept_ref[...]
-    output_ref[traded] = arrived_ref[...]
+    traded = jnp.broadcast_to(facts_ref[0:1, 0:1], (kept_ref.shape[0], 1))
+    kept = kept_ref[...]
+    arrived = arrived_ref[...]
+    output_ref[0] = jnp.where(traded == 0, arrived, kept)
+    output_ref[1] = jnp.where(traded == 0, kept, arrived)
     devices = shares_ref.shape[0]
     shares = shares_ref[...].astype(F32).reshape(devices // 2, 2, CAP, 256)
     for half in range(2):
@@ -473,16 +482,16 @@
         scratch=[pltpu.VMEM(class_list.shape, I32), pltpu.SemaphoreType.DMA],
         flops=10**9,
     )
-    staged = call(
+    facts, *staged = call(
         stage_layer_kernel,
-        [((WIDTH, WIDTH), BF16, KEPT)] * 3,
-        [(HBM, slots), (HBM, narrow_lift), (HBM, middle_lift), (HBM, wide_lift), (HBM, joined_weight)],
+        [((8, LANES), I32, KEPT)] + [((WIDTH, WIDTH), BF16, KEPT)] * 3,
+        [rank, plan, (SMEM, history_lengths.T), (HBM, slots), (HBM, narrow_lift), (HBM, middle_lift), (HBM, wide_lift), (HBM, joined_weight)],
         scratch=[pltpu.SemaphoreType.DMA((5,))],
     )
     kept_output, given_output, payload = call(
         layer_kernel,
         [((rows, WIDTH), BF16), ((rows, WIDTH), BF16), ((devices, 2 * CAP, 256), BF16)],
-        [rank, plan, (SMEM, history_lengths.T), (VMEM, slots), (VMEM, landed), (VMEM, kinds)]
+        [(KEPT, facts), (VMEM, slots), (VMEM, landed), (VMEM, kinds)]
         + [(KEPT, array) for array in staged]
         + [(HBM, cotangent), (VMEM, arrived_cotangent), (HBM, joined_weight), (HBM, output_weight)],
         scratch=[
@@ -492,7 +501,7 @@
             pltpu.VMEM((2, rows, WIDTH), BF16),
             pltpu.VMEM((2 * rows, 4 * WIDTH), F32),
             pltpu.VMEM((2, HEADS, rows, rows), F32),
-            pltpu.SemaphoreType.DMA((5,)),
+            pltpu.SemaphoreType.DMA((4,)),
         ],
         flops=10**10,
     )
@@ -512,7 +521,7 @@
         [
             (cotangent.shape, BF16), (narrow_lift.shape, F32), (middle_lift.shape, F32), (wide_lift.shape, F32),
         ],
-        [rank, plan, (VMEM, kept_output), (VMEM, arrived_output), (VMEM, shares)],
+        [(KEPT, facts), (VMEM, kept_output), (VMEM, arrived_output), (VMEM, shares)],
     )
     return (output, narrow_grad, middle_grad, wide_grad, narrow_delta, middle_delta, wide_delta)
 

time: 103 us -> 103 us (level)
  transfers between devices with their start and end apart: 5 -> 5, of which waited for: 3 -> 3; matrix products, arithmetic and copies ran while one was open for 1% -> 1% of each run, Pallas kernels for 15% -> 16%
where the time goes in v5:
time: 103 us; the launch traced here: 102 us
  Pallas kernels  30.3 us (29%)
  starting transfers between devices  26.8 us (26%)
  blocking collectives  23.1 us (22%)
  waiting for transfers between devices  20.6 us (20%)
    pallas_call x9, Pallas kernels, call(): pl.pallas_call(kernel, out_shape=shapes, in_specs=[space for space, _ in...  30.3 us
    all_to_all x1, blocking collectives, exchange(): lax.all_to_all(array, ('dp', 'table'), split_axis=0, concat_axis=0, tiled...  23.1 us
    all_to_all x3, starting transfers between devices, exchange(): lax.all_to_all(array, ('dp', 'table'), split_axis=0, concat_axis=0, tiled...  18.6 us
    all_to_all x3, waiting for transfers between devices, exchange(): lax.all_to_all(array, ('dp', 'table'), split_axis=0, concat_axis=0, tiled...  14.8 us
    ppermute x1, waiting for transfers between devices, body(): arrived_output = lax.ppermute(given_output, 'dp', partners)  5.86 us
    ppermute x1, starting transfers between devices, body(): arrived_cotangent = lax.ppermute(ready_cotangent, 'dp', partners)  4.42 us
    ppermute x1, starting transfers between devices, body(): arrived_output = lax.ppermute(given_output, 'dp', partners)  3.72 us
  transfers between devices with their start and end apart: 5, of which 3 were waited for; matrix products, arithmetic and copies ran while one was open for 1% of the time, Pallas kernels for 16%

profile of v5, /device:TPU:1, one launch (start us, length us, event | category | flops | bytes accessed | tf_op | source)
XLA Modules:
  0.0 102.1 jit_solution(1322666671078345274)
XLA Ops:
  0.6 1.8 %shard_map.198 = (s32[128,8]{1,0:T(8,128)}, s32[2,256]{1,0:T(2,128)}) custom-call(s32[2,1,256]{2,1,0:T(1,128)} %bitcast.16, s32[2,256]{1,0:T(2,128)} %item_ref.3), custom_call_target="tpu_custom_call" | custom-call | flops 100000000 | bytes 4096 | tf_op jit(solution)/shard_map/pallas_call | solution.py:403
  2.5 4.4 %collective-permute-start = (bf16[2,256,512]{2,1,0:T(8,128)(2,1)}, bf16[2,256,512]{2,1,0:T(8,128)(2,1)S(1)}, u32[]{:S(2)}, u32[]{:S(2)}) collective-permute-start(bf16[2,256,512]{2,1,0:T(8,128)(2,1)} %cotangent_ref.1), channel_id=1, source_target_pairs={{0,64},{16,80},{32,96},{48,112},{64,0},{80,16},{96,32},{112,48},{1... | collective-permute-start | bytes 1572872 | tf_op jit(solution)/shard_map/ppermute | solution.py:458
  6.9 7.9 %all-to-all-start = ((s32[128,1,8]{2,1,0:T(1,128)}), s32[128,1,8]{2,1,0:T(1,128)S(1)}, u32[]{:S(2)}, u32[]{:S(2)}) async-start(s32[128,1,8]{2,1,0:T(1,128)} %bitcast.20), calls=%async_computation | async-start | bytes 131072 | tf_op jit(solution)/shard_map/all_to_all | solution.py:415
  14.8 0.6 pad_add_fusion.rank_ref
  15.4 2.2 %shard_map.200 = (bf16[2048,512]{1,0:T(8,128)(2,1)S(1)}, bf16[32,256]{1,0:T(8,128)(2,1)S(1)}) custom-call(s32[2]{0:T(128)} %pad_add_fusion.rank_ref, s32[2,256]{1,0:T(2,128)} %get-tuple-element.31.after_ref.slot_ref, s32[4096,128]{1,0:T(8,128)} %bitcast.18, s32[32,128]{1,0:T(8,128)} %bitcast.21, bf16[1024,128]{1,0:T(8,128)(2,1)} %narrow_ref.3, ...), custom_call_target="tpu_custom_call" | custom-call | bytes 3950600 | tf_op jit(solution)/shard_map/pallas_call | solution.py:403
  17.6 6.7 %all-to-all-done = s32[128,1,8]{2,1,0:T(1,128)S(1)} async-done(((s32[128,1,8]{2,1,0:T(1,128)}), s32[128,1,8]{2,1,0:T(1,128)S(1)}, u32[]{:S(2)}, u32[]{:S(2)}) %all-to-all-start) | async-done | bytes 4128 | tf_op jit(solution)/shard_map/all_to_all | solution.py:415
  24.3 3.7 %shard_map.201 = bf16[1024,256]{1,0:T(8,128)(2,1)} custom-call(s32[128,8]{1,0:T(8,128)S(1)} %bitcast.14, bf16[32,256]{1,0:T(8,128)(2,1)S(1)} %get-tuple-element.34.marks_ref, bf16[2048,512]{1,0:T(8,128)(2,1)S(1)} %get-tuple-element.35.table_ref), custom_call_target="tpu_custom_call" | custom-call | flops 3000000000 | bytes 2117632 | tf_op jit(solution)/shard_map/pallas_call | solution.py:403
  28.0 0.0 collective-permute-done.arrived_ref
  28.0 5.8 %all-to-all-start.1 = ((bf16[128,8,256]{2,1,0:T(8,128)(2,1)}), bf16[128,8,256]{2,1,0:T(8,128)(2,1)S(1)}, u32[]{:S(2)}, u32[]{:S(2)}) async-start(bf16[128,8,256]{2,1,0:T(8,128)(2,1)} %bitcast.10), calls=%async_computation.1 | async-start | bytes 1048576 | tf_op jit(solution)/shard_map/all_to_all | solution.py:415
  33.8 2.1 %shard_map.199 = (s32[8,128]{1,0:T(8,128)S(1)}, bf16[512,512]{1,0:T(8,128)(2,1)S(1)}, bf16[512,512]{1,0:T(8,128)(2,1)S(1)}, bf16[512,512]{1,0:T(8,128)(2,1)S(1)}) custom-call(s32[2]{0:T(128)} %pad_add_fusion.rank_ref, s32[2,8]{1,0:T(2,128)} %bitcast.22, s32[2,8]{1,0:T(2,128)} %bitcast.23, s32[2,256]{1,0:T(2,128)} %get-tuple-element.31.after_ref.slot_ref, ...), custom_call_target="tpu_custom_call" | custom-call | bytes 2558088 | tf_op jit(solution)/shard_map/pallas_call | solution.py:403
  35.9 0.0 copy-done.1
  36.0 0.0 copy-start
  36.0 3.1 %shard_map.202.class_ref = s32[2,256]{1,0:T(2,128)S(1)} custom-call(s32[2,1,256]{2,1,0:T(1,128)S(1)} %bitcast.17, s32[2,256]{1,0:T(2,128)S(1)} %copy-done.2, s32[4096,128]{1,0:T(8,128)} %bitcast.19), custom_call_target="tpu_custom_call" | custom-call | flops 1000000000 | bytes 2101248 | tf_op jit(solution)/shard_map/pallas_call | solution.py:403
  39.1 8.0 %all-to-all-done.1 = bf16[128,8,256]{2,1,0:T(8,128)(2,1)S(1)} async-done(((bf16[128,8,256]{2,1,0:T(8,128)(2,1)}), bf16[128,8,256]{2,1,0:T(8,128)(2,1)S(1)}, u32[]{:S(2)}, u32[]{:S(2)}) %all-to-all-start.1) | async-done | bytes 524320 | tf_op jit(solution)/shard_map/all_to_all | solution.py:415
  47.1 0.0 copy-done
  47.1 9.8 %shard_map.203 = (bf16[256,512]{1,0:T(8,128)(2,1)S(1)}, bf16[256,512]{1,0:T(8,128)(2,1)S(1)}, bf16[128,16,256]{2,1,0:T(8,128)(2,1)S(1)}) custom-call(s32[8,128]{1,0:T(8,128)S(1)} %get-tuple-element.32.facts_ref, s32[2,256]{1,0:T(2,128)S(1)} %copy-done, bf16[1024,256]{1,0:T(8,128)(2,1)S(1)} %bitcast.13, s32[2,256]{1,0:T(2,128)S(1)} %shard_map.202.class_ref, ...), custom_call_target="tpu_custom_call" | custom-call | flops 10000000000 | bytes 5775360 | tf_op jit(solution)/shard_map/pallas_call | solution.py:403
  56.9 23.1 %all_to_all.32.landed_ref = bf16[128,16,256]{2,1,0:T(8,128)(2,1)S(1)} all-to-all(bf16[128,16,256]{2,1,0:T(8,128)(2,1)S(1)} %get-tuple-element.44), channel_id=1, replica_groups=mesh['dp'=8,'table'=16] {'dp','table'}, dimensions={0} | all-to-all | bytes 2097152 | tf_op jit(solution)/shard_map/all_to_all | solution.py:415
  80.0 1.0 shard_map.204
  81.0 4.9 %all-to-all-start.3 = ((bf16[128,8,256]{2,1,0:T(8,128)(2,1)}), bf16[128,8,256]{2,1,0:T(8,128)(2,1)S(1)}, u32[]{:S(2)}, u32[]{:S(2)}) async-start(bf16[128,8,256]{2,1,0:T(8,128)(2,1)} %shard_map.204), calls=%async_computation.3 | async-start | bytes 1048576 | tf_op jit(solution)/shard_map/all_to_all | solution.py:415
  85.9 3.7 %collective-permute-start.1 = (bf16[256,512]{1,0:T(8,128)(2,1)S(1)}, bf16[256,512]{1,0:T(8,128)(2,1)S(1)}, u32[]{:S(2)}, u32[]{:S(2)}) collective-permute-start(bf16[256,512]{1,0:T(8,128)(2,1)S(1)} %get-tuple-element.45), channel_id=1, source_target_pairs={{0,64},{16,80},{32,96},{48,112},{64,0},{80,16},{96,32},{112,48},{1... | collective-permute-start | bytes 786440 | tf_op jit(solution)/shard_map/ppermute | solution.py:512
  89.6 5.5 %shard_map.206 = (f32[1024,128]{1,0:T(8,128)}, f32[2048,128]{1,0:T(8,128)}, f32[2048,256]{1,0:T(8,128)}) custom-call(bf16[128,16,256]{2,1,0:T(8,128)(2,1)S(1)} %all_to_all.32.landed_ref, s32[128,8]{1,0:T(8,128)S(1)} %bitcast.15, bf16[32,256]{1,0:T(8,128)(2,1)S(1)} %get-tuple-element.34.marks_ref), custom_call_target="tpu_custom_call" | custom-call | flops 3000000000 | bytes 1069056 | tf_op jit(solution)/shard_map/pallas_call | solution.py:403
  95.2 5.9 %collective-permute-done.1.arrived_ref = bf16[256,512]{1,0:T(8,128)(2,1)S(1)} collective-permute-done((bf16[256,512]{1,0:T(8,128)(2,1)S(1)}, bf16[256,512]{1,0:T(8,128)(2,1)S(1)}, u32[]{:S(2)}, u32[]{:S(2)}) %collective-permute-start.1) | collective-permute-done | bytes 262176 | tf_op jit(solution)/shard_map/ppermute | solution.py:512
  101.0 0.0 all-to-all-done.3.shares_ref
  101.0 1.1 %shard_map.205 = (bf16[2,256,512]{2,1,0:T(8,128)(2,1)}, f32[64,512]{1,0:T(8,128)}, f32[128,512]{1,0:T(8,128)}, f32[256,512]{1,0:T(8,128)}) custom-call(s32[8,128]{1,0:T(8,128)S(1)} %get-tuple-element.32.facts_ref, bf16[256,512]{1,0:T(8,128)(2,1)S(1)} %get-tuple-element.42.kept_ref, bf16[256,512]{1,0:T(8,128)(2,1)S(1)} %collective-permute-done.1.arrived_ref, ...), custom_call_target="tpu_custom_call" | custom-call | bytes 1052672 | tf_op jit(solution)/shard_map/pallas_call | solution.py:403
  (3 shorter events, 0.0 us)
Async XLA Ops:
  2.5 25.6 %collective-permute-start = (bf16[2,256,512]{2,1,0:T(8,128)(2,1)}, bf16[2,256,512]{2,1,0:T(8,128)(2,1)S(1)}, u32[]{:S(2)}, u32[]{:S(2)}) collective-permute-start(bf16[2,256,512]{2,1,0:T(8,128)(2,1)} %cotangent_ref.1), channel_id=1, source_target_pairs={{0,64},{16,80},{32,96},{48,112},{64,0},{80,16},{96,32},{112,48},{1... | collective-permute-start | bytes 1572872 | tf_op jit(solution)/shard_map/ppermute | solution.py:458
  6.9 17.4 %all-to-all-start = ((s32[128,1,8]{2,1,0:T(1,128)}), s32[128,1,8]{2,1,0:T(1,128)S(1)}, u32[]{:S(2)}, u32[]{:S(2)}) async-start(s32[128,1,8]{2,1,0:T(1,128)} %bitcast.20), calls=%async_computation | async-start | bytes 131072 | tf_op jit(solution)/shard_map/all_to_all | solution.py:415
  28.0 7.9 %copy-start.1 = (s32[2,256,1]{1,2,0:T(1,128)S(1)}, s32[2,256,1]{1,2,0:T(1,128)}, u32[]{:S(2)}) copy-start(s32[2,256,1]{1,2,0:T(1,128)} %param.17) | copy-start | bytes 6148
  28.0 8.0 %copy-start.2 = (s32[2,256]{1,0:T(2,128)S(1)}, s32[2,256]{1,0:T(2,128)}, u32[]{:S(2)}) copy-start(s32[2,256]{1,0:T(2,128)} %item_ref.3) | copy-start | bytes 6148
  28.0 19.1 %all-to-all-start.1 = ((bf16[128,8,256]{2,1,0:T(8,128)(2,1)}), bf16[128,8,256]{2,1,0:T(8,128)(2,1)S(1)}, u32[]{:S(2)}, u32[]{:S(2)}) async-start(bf16[128,8,256]{2,1,0:T(8,128)(2,1)} %bitcast.10), calls=%async_computation.1 | async-start | bytes 1048576 | tf_op jit(solution)/shard_map/all_to_all | solution.py:415
  36.0 11.2 %copy-start = (s32[2,256]{1,0:T(2,128)S(1)}, s32[2,256]{1,0:T(2,128)}, u32[]{:S(2)}) copy-start(s32[2,256]{1,0:T(2,128)} %get-tuple-element.31.after_ref.slot_ref) | copy-start | bytes 6148
  81.0 20.0 %all-to-all-start.3 = ((bf16[128,8,256]{2,1,0:T(8,128)(2,1)}), bf16[128,8,256]{2,1,0:T(8,128)(2,1)S(1)}, u32[]{:S(2)}, u32[]{:S(2)}) async-start(bf16[128,8,256]{2,1,0:T(8,128)(2,1)} %shard_map.204), calls=%async_computation.3 | async-start | bytes 1048576 | tf_op jit(solution)/shard_map/all_to_all | solution.py:415
  85.9 15.1 %collective-permute-start.1 = (bf16[256,512]{1,0:T(8,128)(2,1)S(1)}, bf16[256,512]{1,0:T(8,128)(2,1)S(1)}, u32[]{:S(2)}, u32[]{:S(2)}) collective-permute-start(bf16[256,512]{1,0:T(8,128)(2,1)S(1)} %get-tuple-element.45), channel_id=1, source_target_pairs={{0,64},{16,80},{32,96},{48,112},{64,0},{80,16},{96,32},{112,48},{1... | collective-permute-start | bytes 786440 | tf_op jit(solution)/shard_map/ppermute | solution.py:512

commit v6 on v5

--- a/solution.py
+++ b/solution.py
@@ -454,8 +454,7 @@
     )
     asked = exchange(requests)
     slab_list = slab_index.reshape(-1, LANES)
-    ready_cotangent, slots = lax.optimization_barrier((cotangent, slots))
-    arrived_cotangent = lax.ppermute(ready_cotangent, "dp", partners)
+    arrived_cotangent = lax.ppermute(cotangent, "dp", partners)
     table, marks = call(
         stage_rows_kernel,
         [((middle_table.shape[0], 512), BF16, KEPT), ((slab_list.shape[0], 256), BF16, KEPT)],

time: 103 us -> 102 us (level)
  starting transfers between devices: 26.8 us -> 25.6 us
    all_to_all x3, starting transfers between devices: 18.6 us -> 17.4 us  [exchange(): lax.all_to_all(array, ('dp', 'table'), split_axis=0, concat_axis=0, tiled...]
  transfers between devices with their start and end apart: 5 -> 5, of which waited for: 3 -> 3; matrix products, arithmetic and copies ran while one was open for 1% -> 1% of each run, Pallas kernels for 16% -> 18%
where the time goes in v6:
time: 102 us; the launch traced here: 101 us
  Pallas kernels  30.3 us (30%)
  starting transfers between devices  25.6 us (25%)
  blocking collectives  23.1 us (23%)
  waiting for transfers between devices  20.8 us (20%)
    pallas_call x9, Pallas kernels, call(): pl.pallas_call(kernel, out_shape=shapes, in_specs=[space for space, _ in...  30.3 us
    all_to_all x1, blocking collectives, exchange(): lax.all_to_all(array, ('dp', 'table'), split_axis=0, concat_axis=0, tiled...  23.1 us
    all_to_all x3, starting transfers between devices, exchange(): lax.all_to_all(array, ('dp', 'table'), split_axis=0, concat_axis=0, tiled...  17.4 us
    all_to_all x3, waiting for transfers between devices, exchange(): lax.all_to_all(array, ('dp', 'table'), split_axis=0, concat_axis=0, tiled...  14.9 us
    ppermute x1, waiting for transfers between devices, body(): arrived_output = lax.ppermute(given_output, 'dp', partners)  5.86 us
    ppermute x1, starting transfers between devices, body(): arrived_cotangent = lax.ppermute(cotangent, 'dp', partners)  4.51 us
    ppermute x1, starting transfers between devices, body(): arrived_output = lax.ppermute(given_output, 'dp', partners)  3.72 us
  transfers between devices with their start and end apart: 5, of which 3 were waited for; matrix products, arithmetic and copies ran while one was open for 1% of the time, Pallas kernels for 18%

profile of v6, /device:TPU:1, one launch (start us, length us, event | category | flops | bytes accessed | tf_op | source)
XLA Modules:
  0.0 101.1 jit_solution(1718775210103340299)
XLA Ops:
  0.6 4.5 %collective-permute-start = (bf16[2,256,512]{2,1,0:T(8,128)(2,1)}, bf16[2,256,512]{2,1,0:T(8,128)(2,1)S(1)}, u32[]{:S(2)}, u32[]{:S(2)}) collective-permute-start(bf16[2,256,512]{2,1,0:T(8,128)(2,1)} %cotangent_ref.1), channel_id=1, source_target_pairs={{0,64},{16,80},{32,96},{48,112},{64,0},{80,16},{96,32},{112,48},{1... | collective-permute-start | bytes 1572872 | tf_op jit(solution)/shard_map/ppermute | solution.py:457
  5.1 1.8 %shard_map.198 = (s32[128,8]{1,0:T(8,128)}, s32[2,256]{1,0:T(2,128)}) custom-call(s32[2,1,256]{2,1,0:T(1,128)} %bitcast.16, s32[2,256]{1,0:T(2,128)} %item_ref.3), custom_call_target="tpu_custom_call" | custom-call | flops 100000000 | bytes 4096 | tf_op jit(solution)/shard_map/pallas_call | solution.py:403
  7.0 7.9 %all-to-all-start = ((s32[128,1,8]{2,1,0:T(1,128)}), s32[128,1,8]{2,1,0:T(1,128)S(1)}, u32[]{:S(2)}, u32[]{:S(2)}) async-start(s32[128,1,8]{2,1,0:T(1,128)} %bitcast.20), calls=%async_computation | async-start | bytes 131072 | tf_op jit(solution)/shard_map/all_to_all | solution.py:415
  14.9 0.6 pad_add_fusion.rank_ref
  15.5 2.2 %shard_map.200 = (bf16[2048,512]{1,0:T(8,128)(2,1)S(1)}, bf16[32,256]{1,0:T(8,128)(2,1)S(1)}) custom-call(s32[2]{0:T(128)} %pad_add_fusion.rank_ref, s32[2,256]{1,0:T(2,128)} %get-tuple-element.28.after_ref.slot_ref, s32[4096,128]{1,0:T(8,128)} %bitcast.18, s32[32,128]{1,0:T(8,128)} %bitcast.21, bf16[1024,128]{1,0:T(8,128)(2,1)} %narrow_ref.3, ...), custom_call_target="tpu_custom_call" | custom-call | bytes 3950600 | tf_op jit(solution)/shard_map/pallas_call | solution.py:403
  17.7 6.7 %all-to-all-done = s32[128,1,8]{2,1,0:T(1,128)S(1)} async-done(((s32[128,1,8]{2,1,0:T(1,128)}), s32[128,1,8]{2,1,0:T(1,128)S(1)}, u32[]{:S(2)}, u32[]{:S(2)}) %all-to-all-start) | async-done | bytes 4128 | tf_op jit(solution)/shard_map/all_to_all | solution.py:415
  24.4 3.7 %shard_map.201 = bf16[1024,256]{1,0:T(8,128)(2,1)} custom-call(s32[128,8]{1,0:T(8,128)S(1)} %bitcast.14, bf16[32,256]{1,0:T(8,128)(2,1)S(1)} %get-tuple-element.31.marks_ref, bf16[2048,512]{1,0:T(8,128)(2,1)S(1)} %get-tuple-element.32.table_ref), custom_call_target="tpu_custom_call" | custom-call | flops 3000000000 | bytes 2117632 | tf_op jit(solution)/shard_map/pallas_call | solution.py:403
  28.1 0.0 collective-permute-done.arrived_ref
  28.1 4.5 %all-to-all-start.1 = ((bf16[128,8,256]{2,1,0:T(8,128)(2,1)}), bf16[128,8,256]{2,1,0:T(8,128)(2,1)S(1)}, u32[]{:S(2)}, u32[]{:S(2)}) async-start(bf16[128,8,256]{2,1,0:T(8,128)(2,1)} %bitcast.10), calls=%async_computation.1 | async-start | bytes 1048576 | tf_op jit(solution)/shard_map/all_to_all | solution.py:415
  32.6 2.1 %shard_map.199 = (s32[8,128]{1,0:T(8,128)S(1)}, bf16[512,512]{1,0:T(8,128)(2,1)S(1)}, bf16[512,512]{1,0:T(8,128)(2,1)S(1)}, bf16[512,512]{1,0:T(8,128)(2,1)S(1)}) custom-call(s32[2]{0:T(128)} %pad_add_fusion.rank_ref, s32[2,8]{1,0:T(2,128)} %bitcast.22, s32[2,8]{1,0:T(2,128)} %bitcast.23, s32[2,256]{1,0:T(2,128)} %get-tuple-element.28.after_ref.slot_ref, ...), custom_call_target="tpu_custom_call" | custom-call | bytes 2558088 | tf_op jit(solution)/shard_map/pallas_call | solution.py:403
  34.8 0.0 copy-done.1
  34.8 0.0 copy-start
  34.8 3.1 %shard_map.202.class_ref = s32[2,256]{1,0:T(2,128)S(1)} custom-call(s32[2,1,256]{2,1,0:T(1,128)S(1)} %bitcast.17, s32[2,256]{1,0:T(2,128)S(1)} %copy-done.2, s32[4096,128]{1,0:T(8,128)} %bitcast.19), custom_call_target="tpu_custom_call" | custom-call | flops 1000000000 | bytes 2101248 | tf_op jit(solution)/shard_map/pallas_call | solution.py:403
  37.9 8.2 %all-to-all-done.1 = bf16[128,8,256]{2,1,0:T(8,128)(2,1)S(1)} async-done(((bf16[128,8,256]{2,1,0:T(8,128)(2,1)}), bf16[128,8,256]{2,1,0:T(8,128)(2,1)S(1)}, u32[]{:S(2)}, u32[]{:S(2)}) %all-to-all-start.1) | async-done | bytes 524320 | tf_op jit(solution)/shard_map/all_to_all | solution.py:415
  46.1 0.0 copy-done
  46.1 9.8 %shard_map.203 = (bf16[256,512]{1,0:T(8,128)(2,1)S(1)}, bf16[256,512]{1,0:T(8,128)(2,1)S(1)}, bf16[128,16,256]{2,1,0:T(8,128)(2,1)S(1)}) custom-call(s32[8,128]{1,0:T(8,128)S(1)} %get-tuple-element.29.facts_ref, s32[2,256]{1,0:T(2,128)S(1)} %copy-done, bf16[1024,256]{1,0:T(8,128)(2,1)S(1)} %bitcast.13, s32[2,256]{1,0:T(2,128)S(1)} %shard_map.202.class_ref, ...), custom_call_target="tpu_custom_call" | custom-call | flops 10000000000 | bytes 5775360 | tf_op jit(solution)/shard_map/pallas_call | solution.py:403
  55.9 23.1 %all_to_all.32.landed_ref = bf16[128,16,256]{2,1,0:T(8,128)(2,1)S(1)} all-to-all(bf16[128,16,256]{2,1,0:T(8,128)(2,1)S(1)} %get-tuple-element.40), channel_id=1, replica_groups=mesh['dp'=8,'table'=16] {'dp','table'}, dimensions={0} | all-to-all | bytes 2097152 | tf_op jit(solution)/shard_map/all_to_all | solution.py:415
  79.0 1.0 shard_map.204
  79.9 4.9 %all-to-all-start.3 = ((bf16[128,8,256]{2,1,0:T(8,128)(2,1)}), bf16[128,8,256]{2,1,0:T(8,128)(2,1)S(1)}, u32[]{:S(2)}, u32[]{:S(2)}) async-start(bf16[128,8,256]{2,1,0:T(8,128)(2,1)} %shard_map.204), calls=%async_computation.3 | async-start | bytes 1048576 | tf_op jit(solution)/shard_map/all_to_all | solution.py:415
  84.9 3.7 %collective-permute-start.1 = (bf16[256,512]{1,0:T(8,128)(2,1)S(1)}, bf16[256,512]{1,0:T(8,128)(2,1)S(1)}, u32[]{:S(2)}, u32[]{:S(2)}) collective-permute-start(bf16[256,512]{1,0:T(8,128)(2,1)S(1)} %get-tuple-element.41), channel_id=1, source_target_pairs={{0,64},{16,80},{32,96},{48,112},{64,0},{80,16},{96,32},{112,48},{1... | collective-permute-start | bytes 786440 | tf_op jit(solution)/shard_map/ppermute | solution.py:511
  88.6 5.5 %shard_map.206 = (f32[1024,128]{1,0:T(8,128)}, f32[2048,128]{1,0:T(8,128)}, f32[2048,256]{1,0:T(8,128)}) custom-call(bf16[128,16,256]{2,1,0:T(8,128)(2,1)S(1)} %all_to_all.32.landed_ref, s32[128,8]{1,0:T(8,128)S(1)} %bitcast.15, bf16[32,256]{1,0:T(8,128)(2,1)S(1)} %get-tuple-element.31.marks_ref), custom_call_target="tpu_custom_call" | custom-call | flops 3000000000 | bytes 1069056 | tf_op jit(solution)/shard_map/pallas_call | solution.py:403
  94.1 5.9 %collective-permute-done.1.arrived_ref = bf16[256,512]{1,0:T(8,128)(2,1)S(1)} collective-permute-done((bf16[256,512]{1,0:T(8,128)(2,1)S(1)}, bf16[256,512]{1,0:T(8,128)(2,1)S(1)}, u32[]{:S(2)}, u32[]{:S(2)}) %collective-permute-start.1) | collective-permute-done | bytes 262176 | tf_op jit(solution)/shard_map/ppermute | solution.py:511
  100.0 0.0 all-to-all-done.3.shares_ref
  100.0 1.1 %shard_map.205 = (bf16[2,256,512]{2,1,0:T(8,128)(2,1)}, f32[64,512]{1,0:T(8,128)}, f32[128,512]{1,0:T(8,128)}, f32[256,512]{1,0:T(8,128)}) custom-call(s32[8,128]{1,0:T(8,128)S(1)} %get-tuple-element.29.facts_ref, bf16[256,512]{1,0:T(8,128)(2,1)S(1)} %get-tuple-element.38.kept_ref, bf16[256,512]{1,0:T(8,128)(2,1)S(1)} %collective-permute-done.1.arrived_ref, ...), custom_call_target="tpu_custom_call" | custom-call | bytes 1052672 | tf_op jit(solution)/shard_map/pallas_call | solution.py:403
  (3 shorter events, 0.0 us)
Async XLA Ops:
  0.6 27.5 %collective-permute-start = (bf16[2,256,512]{2,1,0:T(8,128)(2,1)}, bf16[2,256,512]{2,1,0:T(8,128)(2,1)S(1)}, u32[]{:S(2)}, u32[]{:S(2)}) collective-permute-start(bf16[2,256,512]{2,1,0:T(8,128)(2,1)} %cotangent_ref.1), channel_id=1, source_target_pairs={{0,64},{16,80},{32,96},{48,112},{64,0},{80,16},{96,32},{112,48},{1... | collective-permute-start | bytes 1572872 | tf_op jit(solution)/shard_map/ppermute | solution.py:457
  7.0 17.4 %all-to-all-start = ((s32[128,1,8]{2,1,0:T(1,128)}), s32[128,1,8]{2,1,0:T(1,128)S(1)}, u32[]{:S(2)}, u32[]{:S(2)}) async-start(s32[128,1,8]{2,1,0:T(1,128)} %bitcast.20), calls=%async_computation | async-start | bytes 131072 | tf_op jit(solution)/shard_map/all_to_all | solution.py:415
  28.1 6.7 %copy-start.1 = (s32[2,256,1]{1,2,0:T(1,128)S(1)}, s32[2,256,1]{1,2,0:T(1,128)}, u32[]{:S(2)}) copy-start(s32[2,256,1]{1,2,0:T(1,128)} %param.17) | copy-start | bytes 6148
  28.1 6.7 %copy-start.2 = (s32[2,256]{1,0:T(2,128)S(1)}, s32[2,256]{1,0:T(2,128)}, u32[]{:S(2)}) copy-start(s32[2,256]{1,0:T(2,128)} %item_ref.3) | copy-start | bytes 6148
  28.1 18.0 %all-to-all-start.1 = ((bf16[128,8,256]{2,1,0:T(8,128)(2,1)}), bf16[128,8,256]{2,1,0:T(8,128)(2,1)S(1)}, u32[]{:S(2)}, u32[]{:S(2)}) async-start(bf16[128,8,256]{2,1,0:T(8,128)(2,1)} %bitcast.10), calls=%async_computation.1 | async-start | bytes 1048576 | tf_op jit(solution)/shard_map/all_to_all | solution.py:415
  34.8 11.3 %copy-start = (s32[2,256]{1,0:T(2,128)S(1)}, s32[2,256]{1,0:T(2,128)}, u32[]{:S(2)}) copy-start(s32[2,256]{1,0:T(2,128)} %get-tuple-element.28.after_ref.slot_ref) | copy-start | bytes 6148
  79.9 20.0 %all-to-all-start.3 = ((bf16[128,8,256]{2,1,0:T(8,128)(2,1)}), bf16[128,8,256]{2,1,0:T(8,128)(2,1)S(1)}, u32[]{:S(2)}, u32[]{:S(2)}) async-start(bf16[128,8,256]{2,1,0:T(8,128)(2,1)} %shard_map.204), calls=%async_computation.3 | async-start | bytes 1048576 | tf_op jit(solution)/shard_map/all_to_all | solution.py:415
  84.9 15.1 %collective-permute-start.1 = (bf16[256,512]{1,0:T(8,128)(2,1)S(1)}, bf16[256,512]{1,0:T(8,128)(2,1)S(1)}, u32[]{:S(2)}, u32[]{:S(2)}) collective-permute-start(bf16[256,512]{1,0:T(8,128)(2,1)S(1)} %get-tuple-element.41), channel_id=1, source_target_pairs={{0,64},{16,80},{32,96},{48,112},{64,0},{80,16},{96,32},{112,48},{1... | collective-permute-start | bytes 786440 | tf_op jit(solution)/shard_map/ppermute | solution.py:511

commit v7 on v6

--- a/solution.py
+++ b/solution.py
@@ -339,7 +339,7 @@
 
 
 def sum_kernel(landed_ref, share_ref):
-    total = jnp.sum(landed_ref[...].astype(F32), axis=0)[CAP:]
+    total = jnp.sum(landed_ref[...].astype(F32)[:, CAP:, :], axis=0)
     share_ref[...] = jnp.broadcast_to(total[None].astype(BF16), share_ref.shape)
 
 
@@ -472,7 +472,6 @@
         [(VMEM, asked), (KEPT, marks), (KEPT, table)],
         flops=3 * 10**9,
     )
-    replies, arrived_cotangent = lax.optimization_barrier((replies, arrived_cotangent))
     landed = exchange(replies)
     (kinds,) = call(
         class_kernel,

time: 102 us -> 101 us (level)
  waiting for transfers between devices: 20.8 us -> 17.4 us
  starting transfers between devices: 25.6 us -> 28 us
    all_to_all x3, starting transfers between devices: 17.4 us -> 20.9 us  [exchange(): lax.all_to_all(array, ('dp', 'table'), split_axis=0, concat_axis=0, tiled...]
    all_to_all x3, waiting for transfers between devices: 14.9 us -> 11.6 us  [exchange(): lax.all_to_all(array, ('dp', 'table'), split_axis=0, concat_axis=0, tiled...]
    ppermute x1, starting transfers between devices: 4.51 us -> 3.36 us  [body(): arrived_cotangent = lax.ppermute(cotangent, 'dp', partners)]
  transfers between devices with their start and end apart: 5 -> 5, of which waited for: 3 -> 3; matrix products, arithmetic and copies ran while one was open for 1% -> 1% of each run, Pallas kernels for 18% -> 17%
where the time goes in v7:
time: 101 us; the launch traced here: 100 us
  Pallas kernels  30.3 us (30%)
  starting transfers between devices  28 us (28%)
  blocking collectives  23.1 us (23%)
  waiting for transfers between devices  17.4 us (17%)
    pallas_call x9, Pallas kernels, call(): pl.pallas_call(kernel, out_shape=shapes, in_specs=[space for space, _ in...  30.3 us
    all_to_all x1, blocking collectives, exchange(): lax.all_to_all(array, ('dp', 'table'), split_axis=0, concat_axis=0, tiled...  23.1 us
    all_to_all x3, starting transfers between devices, exchange(): lax.all_to_all(array, ('dp', 'table'), split_axis=0, concat_axis=0, tiled...  20.9 us
    all_to_all x3, waiting for transfers between devices, exchange(): lax.all_to_all(array, ('dp', 'table'), split_axis=0, concat_axis=0, tiled...  11.6 us
    ppermute x1, waiting for transfers between devices, body(): arrived_output = lax.ppermute(given_output, 'dp', partners)  5.86 us
    ppermute x1, starting transfers between devices, body(): arrived_output = lax.ppermute(given_output, 'dp', partners)  3.72 us
    ppermute x1, starting transfers between devices, body(): arrived_cotangent = lax.ppermute(cotangent, 'dp', partners)  3.36 us
  transfers between devices with their start and end apart: 5, of which 3 were waited for; matrix products, arithmetic and copies ran while one was open for 1% of the time, Pallas kernels for 17%

profile of v7, /device:TPU:1, one launch (start us, length us, event | category | flops | bytes accessed | tf_op | source)
XLA Modules:
  0.0 100.2 jit_solution(5353945128321937004)
XLA Ops:
  0.6 1.8 %shard_map.198 = (s32[128,8]{1,0:T(8,128)}, s32[2,256]{1,0:T(2,128)}) custom-call(s32[2,1,256]{2,1,0:T(1,128)} %bitcast.16, s32[2,256]{1,0:T(2,128)} %item_ref.3), custom_call_target="tpu_custom_call" | custom-call | flops 100000000 | bytes 4096 | tf_op jit(solution)/shard_map/pallas_call | solution.py:403
  2.5 11.5 %all-to-all-start = ((s32[128,1,8]{2,1,0:T(1,128)}), s32[128,1,8]{2,1,0:T(1,128)S(1)}, u32[]{:S(2)}, u32[]{:S(2)}) async-start(s32[128,1,8]{2,1,0:T(1,128)} %bitcast.20), calls=%async_computation | async-start | bytes 131072 | tf_op jit(solution)/shard_map/all_to_all | solution.py:415
  14.0 3.4 %collective-permute-start = (bf16[2,256,512]{2,1,0:T(8,128)(2,1)}, bf16[2,256,512]{2,1,0:T(8,128)(2,1)S(1)}, u32[]{:S(2)}, u32[]{:S(2)}) collective-permute-start(bf16[2,256,512]{2,1,0:T(8,128)(2,1)} %cotangent_ref.1), channel_id=1, source_target_pairs={{0,64},{16,80},{32,96},{48,112},{64,0},{80,16},{96,32},{112,48},{1... | collective-permute-start | bytes 1572872 | tf_op jit(solution)/shard_map/ppermute | solution.py:457
  17.3 0.6 pad_add_fusion.rank_ref
  17.9 2.2 %shard_map.200 = (bf16[2048,512]{1,0:T(8,128)(2,1)S(1)}, bf16[32,256]{1,0:T(8,128)(2,1)S(1)}) custom-call(s32[2]{0:T(128)} %pad_add_fusion.rank_ref, s32[2,256]{1,0:T(2,128)} %get-tuple-element.26.after_ref.slot_ref, s32[4096,128]{1,0:T(8,128)} %bitcast.18, s32[32,128]{1,0:T(8,128)} %bitcast.21, bf16[1024,128]{1,0:T(8,128)(2,1)} %narrow_ref.3, ...), custom_call_target="tpu_custom_call" | custom-call | bytes 3950600 | tf_op jit(solution)/shard_map/pallas_call | solution.py:403
  20.1 3.4 %all-to-all-done = s32[128,1,8]{2,1,0:T(1,128)S(1)} async-done(((s32[128,1,8]{2,1,0:T(1,128)}), s32[128,1,8]{2,1,0:T(1,128)S(1)}, u32[]{:S(2)}, u32[]{:S(2)}) %all-to-all-start) | async-done | bytes 4128 | tf_op jit(solution)/shard_map/all_to_all | solution.py:415
  23.5 3.7 %shard_map.201 = bf16[1024,256]{1,0:T(8,128)(2,1)} custom-call(s32[128,8]{1,0:T(8,128)S(1)} %bitcast.14, bf16[32,256]{1,0:T(8,128)(2,1)S(1)} %get-tuple-element.29.marks_ref, bf16[2048,512]{1,0:T(8,128)(2,1)S(1)} %get-tuple-element.30.table_ref), custom_call_target="tpu_custom_call" | custom-call | flops 3000000000 | bytes 2117632 | tf_op jit(solution)/shard_map/pallas_call | solution.py:403
  27.1 4.5 %all-to-all-start.1 = ((bf16[128,8,256]{2,1,0:T(8,128)(2,1)}), bf16[128,8,256]{2,1,0:T(8,128)(2,1)S(1)}, u32[]{:S(2)}, u32[]{:S(2)}) async-start(bf16[128,8,256]{2,1,0:T(8,128)(2,1)} %bitcast.10), calls=%async_computation.1 | async-start | bytes 1048576 | tf_op jit(solution)/shard_map/all_to_all | solution.py:415
  31.7 2.1 %shard_map.199 = (s32[8,128]{1,0:T(8,128)S(1)}, bf16[512,512]{1,0:T(8,128)(2,1)S(1)}, bf16[512,512]{1,0:T(8,128)(2,1)S(1)}, bf16[512,512]{1,0:T(8,128)(2,1)S(1)}) custom-call(s32[2]{0:T(128)} %pad_add_fusion.rank_ref, s32[2,8]{1,0:T(2,128)} %bitcast.22, s32[2,8]{1,0:T(2,128)} %bitcast.23, s32[2,256]{1,0:T(2,128)} %get-tuple-element.26.after_ref.slot_ref, ...), custom_call_target="tpu_custom_call" | custom-call | bytes 2558088 | tf_op jit(solution)/shard_map/pallas_call | solution.py:403
  33.8 0.0 copy-done.1
  33.8 0.0 copy-done.2
  33.9 0.0 copy-start
  33.9 3.1 %shard_map.202.class_ref = s32[2,256]{1,0:T(2,128)S(1)} custom-call(s32[2,1,256]{2,1,0:T(1,128)S(1)} %bitcast.17, s32[2,256]{1,0:T(2,128)S(1)} %copy-done.2, s32[4096,128]{1,0:T(8,128)} %bitcast.19), custom_call_target="tpu_custom_call" | custom-call | flops 1000000000 | bytes 2101248 | tf_op jit(solution)/shard_map/pallas_call | solution.py:403
  37.0 8.2 %all-to-all-done.1 = bf16[128,8,256]{2,1,0:T(8,128)(2,1)S(1)} async-done(((bf16[128,8,256]{2,1,0:T(8,128)(2,1)}), bf16[128,8,256]{2,1,0:T(8,128)(2,1)S(1)}, u32[]{:S(2)}, u32[]{:S(2)}) %all-to-all-start.1) | async-done | bytes 524320 | tf_op jit(solution)/shard_map/all_to_all | solution.py:415
  45.1 0.0 collective-permute-done.arrived_ref
  45.2 9.8 %shard_map.203 = (bf16[256,512]{1,0:T(8,128)(2,1)S(1)}, bf16[256,512]{1,0:T(8,128)(2,1)S(1)}, bf16[128,16,256]{2,1,0:T(8,128)(2,1)S(1)}) custom-call(s32[8,128]{1,0:T(8,128)S(1)} %get-tuple-element.27.facts_ref, s32[2,256]{1,0:T(2,128)S(1)} %copy-done, bf16[1024,256]{1,0:T(8,128)(2,1)S(1)} %bitcast.13, s32[2,256]{1,0:T(2,128)S(1)} %shard_map.202.class_ref, ...), custom_call_target="tpu_custom_call" | custom-call | flops 10000000000 | bytes 5775360 | tf_op jit(solution)/shard_map/pallas_call | solution.py:403
  55.0 23.1 %all_to_all.32.landed_ref = bf16[128,16,256]{2,1,0:T(8,128)(2,1)S(1)} all-to-all(bf16[128,16,256]{2,1,0:T(8,128)(2,1)S(1)} %get-tuple-element.36), channel_id=1, replica_groups=mesh['dp'=8,'table'=16] {'dp','table'}, dimensions={0} | all-to-all | bytes 2097152 | tf_op jit(solution)/shard_map/all_to_all | solution.py:415
  78.0 1.0 shard_map.204
  79.0 4.9 %all-to-all-start.3 = ((bf16[128,8,256]{2,1,0:T(8,128)(2,1)}), bf16[128,8,256]{2,1,0:T(8,128)(2,1)S(1)}, u32[]{:S(2)}, u32[]{:S(2)}) async-start(bf16[128,8,256]{2,1,0:T(8,128)(2,1)} %shard_map.204), calls=%async_computation.3 | async-start | bytes 1048576 | tf_op jit(solution)/shard_map/all_to_all | solution.py:415
  83.9 3.7 %collective-permute-start.1 = (bf16[256,512]{1,0:T(8,128)(2,1)S(1)}, bf16[256,512]{1,0:T(8,128)(2,1)S(1)}, u32[]{:S(2)}, u32[]{:S(2)}) collective-permute-start(bf16[256,512]{1,0:T(8,128)(2,1)S(1)} %get-tuple-element.37), channel_id=1, source_target_pairs={{0,64},{16,80},{32,96},{48,112},{64,0},{80,16},{96,32},{112,48},{1... | collective-permute-start | bytes 786440 | tf_op jit(solution)/shard_map/ppermute | solution.py:510
  87.7 5.5 %shard_map.206 = (f32[1024,128]{1,0:T(8,128)}, f32[2048,128]{1,0:T(8,128)}, f32[2048,256]{1,0:T(8,128)}) custom-call(bf16[128,16,256]{2,1,0:T(8,128)(2,1)S(1)} %all_to_all.32.landed_ref, s32[128,8]{1,0:T(8,128)S(1)} %bitcast.15, bf16[32,256]{1,0:T(8,128)(2,1)S(1)} %get-tuple-element.29.marks_ref), custom_call_target="tpu_custom_call" | custom-call | flops 3000000000 | bytes 1069056 | tf_op jit(solution)/shard_map/pallas_call | solution.py:403
  93.2 5.9 %collective-permute-done.1.arrived_ref = bf16[256,512]{1,0:T(8,128)(2,1)S(1)} collective-permute-done((bf16[256,512]{1,0:T(8,128)(2,1)S(1)}, bf16[256,512]{1,0:T(8,128)(2,1)S(1)}, u32[]{:S(2)}, u32[]{:S(2)}) %collective-permute-start.1) | collective-permute-done | bytes 262176 | tf_op jit(solution)/shard_map/ppermute | solution.py:510
  99.1 0.0 all-to-all-done.3.shares_ref
  99.1 1.1 %shard_map.205 = (bf16[2,256,512]{2,1,0:T(8,128)(2,1)}, f32[64,512]{1,0:T(8,128)}, f32[128,512]{1,0:T(8,128)}, f32[256,512]{1,0:T(8,128)}) custom-call(s32[8,128]{1,0:T(8,128)S(1)} %get-tuple-element.27.facts_ref, bf16[256,512]{1,0:T(8,128)(2,1)S(1)} %get-tuple-element.34.kept_ref, bf16[256,512]{1,0:T(8,128)(2,1)S(1)} %collective-permute-done.1.arrived_ref, ...), custom_call_target="tpu_custom_call" | custom-call | bytes 1052672 | tf_op jit(solution)/shard_map/pallas_call | solution.py:403
  (3 shorter events, 0.0 us)
Async XLA Ops:
  2.5 21.0 %all-to-all-start = ((s32[128,1,8]{2,1,0:T(1,128)}), s32[128,1,8]{2,1,0:T(1,128)S(1)}, u32[]{:S(2)}, u32[]{:S(2)}) async-start(s32[128,1,8]{2,1,0:T(1,128)} %bitcast.20), calls=%async_computation | async-start | bytes 131072 | tf_op jit(solution)/shard_map/all_to_all | solution.py:415
  14.0 31.2 %collective-permute-start = (bf16[2,256,512]{2,1,0:T(8,128)(2,1)}, bf16[2,256,512]{2,1,0:T(8,128)(2,1)S(1)}, u32[]{:S(2)}, u32[]{:S(2)}) collective-permute-start(bf16[2,256,512]{2,1,0:T(8,128)(2,1)} %cotangent_ref.1), channel_id=1, source_target_pairs={{0,64},{16,80},{32,96},{48,112},{64,0},{80,16},{96,32},{112,48},{1... | collective-permute-start | bytes 1572872 | tf_op jit(solution)/shard_map/ppermute | solution.py:457
  27.1 6.7 %copy-start.1 = (s32[2,256,1]{1,2,0:T(1,128)S(1)}, s32[2,256,1]{1,2,0:T(1,128)}, u32[]{:S(2)}) copy-start(s32[2,256,1]{1,2,0:T(1,128)} %param.17) | copy-start | bytes 6148
  27.1 6.7 %copy-start.2 = (s32[2,256]{1,0:T(2,128)S(1)}, s32[2,256]{1,0:T(2,128)}, u32[]{:S(2)}) copy-start(s32[2,256]{1,0:T(2,128)} %item_ref.3) | copy-start | bytes 6148
  27.1 18.0 %all-to-all-start.1 = ((bf16[128,8,256]{2,1,0:T(8,128)(2,1)}), bf16[128,8,256]{2,1,0:T(8,128)(2,1)S(1)}, u32[]{:S(2)}, u32[]{:S(2)}) async-start(bf16[128,8,256]{2,1,0:T(8,128)(2,1)} %bitcast.10), calls=%async_computation.1 | async-start | bytes 1048576 | tf_op jit(solution)/shard_map/all_to_all | solution.py:415
  33.9 11.3 %copy-start = (s32[2,256]{1,0:T(2,128)S(1)}, s32[2,256]{1,0:T(2,128)}, u32[]{:S(2)}) copy-start(s32[2,256]{1,0:T(2,128)} %get-tuple-element.26.after_ref.slot_ref) | copy-start | bytes 6148
  79.0 20.0 %all-to-all-start.3 = ((bf16[128,8,256]{2,1,0:T(8,128)(2,1)}), bf16[128,8,256]{2,1,0:T(8,128)(2,1)S(1)}, u32[]{:S(2)}, u32[]{:S(2)}) async-start(bf16[128,8,256]{2,1,0:T(8,128)(2,1)} %shard_map.204), calls=%async_computation.3 | async-start | bytes 1048576 | tf_op jit(solution)/shard_map/all_to_all | solution.py:415
  83.9 15.1 %collective-permute-start.1 = (bf16[256,512]{1,0:T(8,128)(2,1)S(1)}, bf16[256,512]{1,0:T(8,128)(2,1)S(1)}, u32[]{:S(2)}, u32[]{:S(2)}) collective-permute-start(bf16[256,512]{1,0:T(8,128)(2,1)S(1)} %get-tuple-element.37), channel_id=1, source_target_pairs={{0,64},{16,80},{32,96},{48,112},{64,0},{80,16},{96,32},{112,48},{1... | collective-permute-start | bytes 786440 | tf_op jit(solution)/shard_map/ppermute | solution.py:510
